TPU v7x, 32 devices: a whole 2x2x4 slice. The times are simulated.
32 devices in a mesh: dp: 16 (over z, y, x), head: 2 (over core).
Axes of the slice: x: 2, y: 2, z: 4, core: 2. Of those that a mesh axis runs over, the one named last changes fastest.
Arguments:
- frames: bfloat16 [512, 192, 240], P(('dp', 'head')), may hold values from -6 to 6
- cotangent: bfloat16 [512, 192, 240], P(('dp', 'head')), may hold values from -6 to 6
- lengths: int32 [512], P('dp'), may hold values from 1 to 192, as said below
- head_params: float32 [2, 577968], P('head', 'dp'), may hold values from -3 to 3
- shared_params: float32 [180960], P(('dp', 'head')), may hold values from -3 to 3
- head_first: float32 [2, 577968], P('head', 'dp'), may hold values from -21.947428 to 21.947428
- head_second: float32 [2, 577968], P('head', 'dp'), may hold values from 3.93216 to 15.72864
- shared_first: float32 [180960], P(('dp', 'head')), may hold values from -21.947428 to 21.947428
- shared_second: float32 [180960], P(('dp', 'head')), may hold values from 3.93216 to 15.72864
Outputs:
- layer_out: bfloat16 [512, 192, 240], P(('dp', 'head'))
- input_grad: float32 [512, 192, 240], P(('dp', 'head'))
- head_first_new: float32 [2, 577968], P('head', 'dp')
- head_second_new: float32 [2, 577968], P('head', 'dp')
- head_new: float32 [2, 577968], P('head', 'dp')
- head_copy: bfloat16 [2, 577968], P('head', 'dp')
- shared_first_new: float32 [180960], P(('dp', 'head'))
- shared_second_new: float32 [180960], P(('dp', 'head'))
- shared_new: float32 [180960], P(('dp', 'head'))
- shared_copy: bfloat16 [180960], P(('dp', 'head'))
Inputs may be any that keep to these rules, and one draw needn't show every extreme that they name: `lengths`: each utterance has 1 to 192 valid frames; the last utterance has exactly 192.
All inputs are finite; a program needn't handle non-finite values.
Results may differ from a plain program's by a relative error of at most 0.025.
Values may be sent and summed in bfloat16 or wider, within the bound.
A program may use at most 256 MiB of HBM per device.

v0:
```python
import functools
import math

import jax
import jax.numpy as jnp
from jax import lax
from jax.experimental import pallas as pl
from jax.experimental.pallas import tpu as pltpu
from jax.sharding import PartitionSpec as P

BF = jnp.bfloat16
F32 = jnp.float32
LANES = 128


def up_to(count, unit):
    return -(-count // unit) * unit


def grid_place(nz):
    me = lax.axis_index("dp")
    core = lax.axis_index("head")
    zc = me // 4
    rest = me - 4 * zc
    yc = rest // 2
    xc = rest - 2 * yc
    return me, core, zc, yc, xc


def remote(src, dst, send, recv, dp, head):
    return pltpu.make_async_remote_copy(
        src_ref=src,
        dst_ref=dst,
        send_sem=send,
        recv_sem=recv,
        device_id={"dp": dp, "head": head},
        device_id_type=pl.DeviceIdType.MESH,
    )


def greet(nz, me, core, zc, yc, xc):
    barrier = pltpu.get_barrier_semaphore()

    def hello(dp, head):
        pl.semaphore_signal(
            barrier, inc=1, device_id={"dp": dp, "head": head}, device_id_type=pl.DeviceIdType.MESH
        )

    for k in range(1, nz):
        hello(lax.rem(zc + k, nz) * 4 + 2 * yc + xc, core)
    hello(4 * zc + 2 * (1 - yc) + xc, core)
    hello(4 * zc + 2 * yc + 1 - xc, core)
    hello(me, 1 - core)
    pl.semaphore_wait(barrier, nz + 2)


def gather_kernel(nz, src, out, sz, rz, s1, r1, s2, r2, sc, rc):
    rows = src.shape[0]
    row_a = up_to(rows // 2, 16)
    parts = (pl.ds(0, row_a), pl.ds(row_a, rows - row_a))
    me, core, zc, yc, xc = grid_place(nz)
    greet(nz, me, core, zc, yc, xc)
    out[me, core] = src[...]
    y_peer = 4 * zc + 2 * (1 - yc) + xc
    x_peer = 4 * zc + 2 * yc + 1 - xc
    firsts = (y_peer, x_peer)
    seconds = (x_peer, y_peer)
    pending = []

    def send(slot, p, send_sem, recv_sem, dp, head):
        block = out.at[slot, core, parts[p]]
        copy = remote(block, block, send_sem, recv_sem, dp, head)
        copy.start()
        pending.append(copy)

    def arrived(slot, which, p, send_sem, recv_sem):
        block = out.at[slot, which, parts[p]]
        remote(block, block, send_sem, recv_sem, me, 1 - core).wait_recv()

    zs = [lax.rem(zc + k, nz) for k in range(nz)]
    here = 2 * yc + xc
    first_here = (2 * (1 - yc) + xc, 2 * yc + 1 - xc)
    second_here = ((2 * yc + 1 - xc, 2 * (1 - yc) + 1 - xc), (2 * (1 - yc) + xc, 2 * (1 - yc) + 1 - xc))
    for k in range(1, nz):
        for p in (0, 1):
            send(me, p, sz.at[p, k], rz.at[p, zc], zs[k] * 4 + here, core)
    for k in range(nz):
        z = zs[k]
        slot = 4 * z + here
        for p in (0, 1):
            if k:
                arrived(slot, core, p, sz.at[p, k], rz.at[p, z])
            send(slot, p, s1.at[p, k], r1.at[p, z], firsts[p], core)
            send(slot, p, s2.at[p, k, 0], r2.at[p, z, 0], seconds[p], core)
            send(slot, p, sc.at[p, k, 0], rc.at[p, z, 0], me, 1 - core)
    for k in range(nz):
        z = zs[k]
        for p in (0, 1):
            slot = 4 * z + first_here[p]
            arrived(slot, core, p, s1.at[p, k], r1.at[p, z])
            send(slot, p, s2.at[p, k, 1], r2.at[p, z, 1], seconds[p], core)
            send(slot, p, sc.at[p, k, 1], rc.at[p, z, 1], me, 1 - core)
    for k in range(nz):
        z = zs[k]
        for p in (0, 1):
            for b in (0, 1):
                slot = 4 * z + second_here[p][b]
                arrived(slot, core, p, s2.at[p, k, b], r2.at[p, z, b])
                send(slot, p, sc.at[p, k, 2 + b], rc.at[p, z, 2 + b], me, 1 - core)
    for k in range(nz):
        z = zs[k]
        for p in (0, 1):
            for b, at in enumerate((here, first_here[p]) + second_here[p]):
                arrived(4 * z + at, 1 - core, p, sc.at[p, k, b], rc.at[p, z, b])
    for copy in pending:
        copy.wait_send()


def gather_all(block, dp, collective_id):
    rows = block.shape[0]
    nz = dp // 4
    dma = pltpu.SemaphoreType.DMA
    return pl.pallas_call(
        functools.partial(gather_kernel, nz),
        out_shape=jax.ShapeDtypeStruct((dp, 2, rows, LANES), block.dtype),
        in_specs=[pl.BlockSpec(memory_space=pltpu.VMEM)],
        out_specs=pl.BlockSpec(memory_space=pltpu.VMEM),
        scratch_shapes=[dma((2, nz)), dma((2, nz)), dma((2, nz)), dma((2, nz)), dma((2, nz, 2)), dma((2, nz, 2)), dma((2, nz, 4)), dma((2, nz, 4))],
        compiler_params=pltpu.CompilerParams(
            collective_id=collective_id, has_side_effects=True, vmem_limit_bytes=40 << 20
        ),
        name="gather_weights",
    )(block)


def scatter_kernel(nz, g, out, c1, t1, rx1, t2, rx2, t3, rx3, sc, rc, s1, r1, s2, r2, s3, r3):
    rows = g.shape[2]
    row_a = up_to(rows // 2, 16)
    starts = (0, row_a)
    sizes = (row_a, rows - row_a)
    parts = tuple(pl.ds(a, n) for a, n in zip(starts, sizes))
    me, core, zc, yc, xc = grid_place(nz)
    greet(nz, me, core, zc, yc, xc)
    y_peer = 4 * zc + 2 * (1 - yc) + xc
    x_peer = 4 * zc + 2 * yc + 1 - xc
    firsts = (x_peer, y_peer)
    seconds = (y_peer, x_peer)
    pending = []

    def send(src, dst, send_sem, recv_sem, dp, head):
        copy = remote(src, dst, send_sem, recv_sem, dp, head)
        copy.start()
        pending.append(copy)

    def arrived(block, send_sem, recv_sem):
        remote(block, block, send_sem, recv_sem, me, 1 - core).wait_recv()

    order = list(range(1, nz)) + [0]
    zs = [lax.rem(zc + k, nz) for k in range(nz)]
    give = ((1 - xc, 2 + 1 - xc), (2 * (1 - yc), 2 * (1 - yc) + 1))
    second_give = (1 - yc, 1 - xc)
    second_keep = (yc, xc)

    def place(p, b):
        return 2 * b + xc if p == 0 else 2 * yc + b

    for k in order:
        z = zs[k]
        send(g.at[1 - core, pl.ds(4 * z, 4)], c1.at[pl.ds(4 * z, 4)], sc.at[k], rc.at[z], me, 1 - core)
    for k in order:
        z = zs[k]
        arrived(c1.at[pl.ds(4 * z, 4)], sc.at[k], rc.at[z])
        for p in (0, 1):
            n = pl.ds(0, sizes[p])
            for b in (0, 1):
                slot = 4 * z + give[p][b]
                t1[p, z, b, n] = (g[core, slot, parts[p]].astype(F32) + c1[slot, parts[p]].astype(F32)).astype(BF)
            send(t1.at[p, z, :, n], rx1.at[p, z, :, n], s1.at[p, k], r1.at[p, z], firsts[p], core)

    def partial(p, z, b):
        slot = 4 * z + place(p, b)
        n = pl.ds(0, sizes[p])
        return g[core, slot, parts[p]].astype(F32) + c1[slot, parts[p]].astype(F32) + rx1[p, z, b, n].astype(F32)

    for k in order:
        z = zs[k]
        for p in (0, 1):
            n = pl.ds(0, sizes[p])
            arrived(rx1.at[p, z, :, n], s1.at[p, k], r1.at[p, z])
            t2[p, z, n] = partial(p, z, second_give[p]).astype(BF)
            send(t2.at[p, z, n], rx2.at[p, z, n], s2.at[p, k], r2.at[p, z], seconds[p], core)
    for k in order:
        z = zs[k]
        for p in (0, 1):
            n = pl.ds(0, sizes[p])
            arrived(rx2.at[p, z, n], s2.at[p, k], r2.at[p, z])
            total = partial(p, z, second_keep[p]) + rx2[p, z, n].astype(F32)
            if k:
                t3[p, z, n] = total.astype(BF)
                send(t3.at[p, z, n], rx3.at[p, zc, n], s3.at[p, k], r3.at[p, zc], 4 * z + 2 * yc + xc, core)
            else:
                out[parts[p], :] = total
    for k in order[:-1]:
        z = zs[k]
        for p in (0, 1):
            n = pl.ds(0, sizes[p])
            arrived(rx3.at[p, z, n], s3.at[p, k], r3.at[p, z])
            out[parts[p], :] += rx3[p, z, n].astype(F32)
    for copy in pending:
        copy.wait_send()


def scatter_all(g, collective_id):
    dp, rows = g.shape[1], g.shape[2]
    nz = dp // 4
    half = up_to(rows // 2, 16)
    dma = pltpu.SemaphoreType.DMA
    vm = pltpu.VMEM
    return pl.pallas_call(
        functools.partial(scatter_kernel, nz),
        out_shape=jax.ShapeDtypeStruct((rows, LANES), F32),
        in_specs=[pl.BlockSpec(memory_space=pltpu.VMEM)],
        out_specs=pl.BlockSpec(memory_space=pltpu.VMEM),
        scratch_shapes=[
            vm((dp, rows, LANES), BF),
            vm((2, nz, 2, half, LANES), BF),
            vm((2, nz, 2, half, LANES), BF),
            vm((2, nz, half, LANES), BF),
            vm((2, nz, half, LANES), BF),
            vm((2, nz, half, LANES), BF),
            vm((2, nz, half, LANES), BF),
            dma((nz,)), dma((nz,)), dma((2, nz)), dma((2, nz)), dma((2, nz)), dma((2, nz)), dma((2, nz)), dma((2, nz)),
        ],
        compiler_params=pltpu.CompilerParams(
            collective_id=collective_id, has_side_effects=True, vmem_limit_bytes=40 << 20
        ),
        name="scatter_grads",
    )(g)


def share_kernel(dp_count, src, out, ss, rs):
    me = lax.axis_index("dp")
    core = lax.axis_index("head")
    own = 2 * me + core
    total = 2 * dp_count
    barrier = pltpu.get_barrier_semaphore()

    def peer(k):
        other = lax.rem(own + k, total)
        dp = other // 2
        return other, dp, other - 2 * dp

    @pl.loop(1, total)
    def _(k):
        _, dp, head = peer(k)
        pl.semaphore_signal(
            barrier, inc=1, device_id={"dp": dp, "head": head}, device_id_type=pl.DeviceIdType.MESH
        )

    pl.semaphore_wait(barrier, total - 1)
    out[own] = src[...]

    @pl.loop(1, total)
    def _(k):
        _, dp, head = peer(k)
        remote(src, out.at[own], ss.at[k], rs.at[own], dp, head).start()

    @pl.loop(1, total)
    def _(k):
        other, dp, head = peer(k)
        remote(src, out.at[other], ss.at[k], rs.at[other], dp, head).wait()


def share_all(block, dp, collective_id):
    dma = pltpu.SemaphoreType.DMA
    return pl.pallas_call(
        functools.partial(share_kernel, dp),
        out_shape=jax.ShapeDtypeStruct((2 * dp,) + block.shape, block.dtype),
        in_specs=[pl.BlockSpec(memory_space=pltpu.VMEM)],
        out_specs=pl.BlockSpec(memory_space=pltpu.VMEM),
        scratch_shapes=[dma((2 * dp,)), dma((2 * dp,))],
        compiler_params=pltpu.CompilerParams(collective_id=collective_id, has_side_effects=True),
        name="share_sums",
    )(block)

HEADS = 4
HD = 60
FF = 960
KW = 15
STEP = 10
KREL = 383


NORM_EPS = 1e-05
BETA_ONE = 0.9
BETA_TWO = 0.999
LEARN_RATE = 0.1
WEIGHT_DECAY = 0.01
ADAM_EPS = 1e-08
(
    UP_ONE,
    UPB_ONE,
    DOWN_ONE,
    UP_TWO,
    UPB_TWO,
    DOWN_TWO,
    W_QUERY,
    W_KEY,
    W_VALUE,
    B_QUERY,
    B_VALUE,
    REL_TABLE,
    W_OUT,
    FFA_GAIN,
    FFA_BIAS,
    ATT_GAIN,
    ATT_BIAS,
    CNV_GAIN,
    CNV_BIAS,
    FFB_GAIN,
    FFB_BIAS,
    OUT_GAIN,
    OUT_BIAS,
    DOWNB_ONE,
    DOWNB_TWO,
    B_OUT,
    POINT_ONE,
    POINTB_ONE,
    DEPTH_KERNEL,
    DEPTH_BIAS,
    BATCH_GAIN,
    BATCH_BIAS,
    POINT_TWO,
    POINTB_TWO,
) = range(34)
JOIN_AXIS = {
    UP_ONE: 1,
    UPB_ONE: 0,
    DOWN_ONE: 0,
    UP_TWO: 1,
    UPB_TWO: 0,
    DOWN_TWO: 0,
    W_QUERY: 1,
    W_KEY: 1,
    W_VALUE: 1,
    B_QUERY: 0,
    B_VALUE: 0,
    REL_TABLE: 0,
    W_OUT: 0,
}
VECTOR_NAMES = (
    FFA_GAIN,
    FFA_BIAS,
    ATT_GAIN,
    ATT_BIAS,
    CNV_GAIN,
    CNV_BIAS,
    FFB_GAIN,
    FFB_BIAS,
    OUT_GAIN,
    OUT_BIAS,
    DOWNB_ONE,
    DOWNB_TWO,
    B_OUT,
)
FFN_ONE = (FFA_GAIN, FFA_BIAS, UP_ONE, UPB_ONE, DOWN_ONE, DOWNB_ONE)
FFN_TWO = (FFB_GAIN, FFB_BIAS, UP_TWO, UPB_TWO, DOWN_TWO, DOWNB_TWO)


def for_sending(x):

    def short(part):
        return part.astype(jnp.bfloat16) if part.dtype == jnp.float32 else part

    return jax.tree.map(short, x)


def head_layout(model_dim, hidden, heads_here, head_size, rel_count):
    head_width = heads_here * head_size
    return [
        (UP_ONE, (model_dim, hidden)),
        (UPB_ONE, (hidden,)),
        (DOWN_ONE, (hidden, model_dim)),
        (UP_TWO, (model_dim, hidden)),
        (UPB_TWO, (hidden,)),
        (DOWN_TWO, (hidden, model_dim)),
        (W_QUERY, (model_dim, head_width)),
        (W_KEY, (model_dim, head_width)),
        (W_VALUE, (model_dim, head_width)),
        (B_QUERY, (head_width,)),
        (B_VALUE, (head_width,)),
        (REL_TABLE, (heads_here, rel_count)),
        (W_OUT, (head_width, model_dim)),
    ]


def shared_layout(model_dim, kernel):
    entries = [(entry_name, (model_dim,)) for entry_name in VECTOR_NAMES]
    entries += [
        (POINT_ONE, (model_dim, 2 * model_dim)),
        (POINTB_ONE, (2 * model_dim,)),
        (DEPTH_KERNEL, (kernel, model_dim)),
        (DEPTH_BIAS, (model_dim,)),
        (BATCH_GAIN, (model_dim,)),
        (BATCH_BIAS, (model_dim,)),
        (POINT_TWO, (model_dim, model_dim)),
        (POINTB_TWO, (model_dim,)),
    ]
    return entries


def unflatten(flat_vector, layout):
    result = {}
    offset = 0
    for entry_name, dims_of in layout:
        amount = math.prod(dims_of)
        result[entry_name] = flat_vector[offset : offset + amount].reshape(dims_of)
        offset += amount
    return result


def flatten_dict(grads, layout, full_length):
    flat_parts = [grads[entry_name].reshape(-1) for entry_name, dims_of in layout]
    used_count = sum((math.prod(dims_of) for entry_name, dims_of in layout))
    flat_parts.append(jnp.zeros((full_length - used_count,), jnp.float32))
    return jnp.concatenate(flat_parts)


def spread_frames(normed_lower_half):
    return normed_lower_half


def collect_frames(partial_value):
    return partial_value


def spread_grads(branch_gradient):
    return branch_gradient


def collect_grads(partial_value):
    return partial_value


def norm_forward(values, norm_gain, norm_bias):
    centre = values - jnp.mean(values, -1, keepdims=True)
    inv_spread = lax.rsqrt(jnp.mean(centre * centre, -1, keepdims=True) + NORM_EPS)
    scaled = centre * inv_spread
    return (scaled * norm_gain + norm_bias, scaled, inv_spread)


def norm_backward(grad_normed, scaled, inv_spread, norm_gain):
    gain_grad = jnp.sum(grad_normed * scaled, (0, 1))
    bias_grad = jnp.sum(grad_normed, (0, 1))
    grad_scaled = grad_normed * norm_gain
    values_grad = inv_spread * (
        grad_scaled
        - jnp.mean(grad_scaled, -1, keepdims=True)
        - scaled * jnp.mean(grad_scaled * scaled, -1, keepdims=True)
    )
    return (values_grad, gain_grad, bias_grad)


def depthwise(signal, kernel):
    tap_count = kernel.shape[0]
    half_width = tap_count // 2
    length = signal.shape[1]
    padded = jnp.pad(signal, ((0, 0), (half_width, half_width), (0, 0)))
    result = padded[:, 0:length] * kernel[0]
    for tap_index in range(1, tap_count):
        result = result + padded[:, tap_index : tap_index + length] * kernel[tap_index]
    return result


def rel_expand(rel_table, length):
    heads_here = rel_table.shape[0]
    padded = jnp.pad(rel_table, ((0, 0), (1, 1)))
    tiled = jnp.tile(padded, (1, length))[:, : 2 * length * length]
    return tiled.reshape(heads_here, length, 2 * length)[:, :, length:]


def rel_collect(grid):
    heads_here, length = (grid.shape[0], grid.shape[1])
    shifted = jnp.pad(grid, ((0, 0), (0, 0), (length, 0))).reshape(heads_here, 2 * length * length)
    shifted = jnp.pad(shifted, ((0, 0), (0, length))).reshape(heads_here, length, 2 * length + 1)
    return jnp.sum(shifted, 1)[:, 1 : 2 * length]


def ffn_forward(values, layer_weights, names):
    gain_key, bias_key, upper_random_key, upperb_key, lower_random_key, lowerb_key = names
    normed, scaled, inv_spread = norm_forward(
        values,
        layer_weights[gain_key].astype(jnp.float32),
        layer_weights[bias_key].astype(jnp.float32),
    )
    gathered_params = spread_frames(normed.astype(jnp.bfloat16))
    upper_pre = jnp.einsum(
        "eav,vi->eai",
        gathered_params,
        layer_weights[upper_random_key],
        preferred_element_type=jnp.float32,
    )
    upper_pre = upper_pre + layer_weights[upperb_key].astype(jnp.float32)
    active_values = (upper_pre * jax.nn.sigmoid(upper_pre)).astype(jnp.bfloat16)
    partial_value = jnp.einsum(
        "wmp,pz->wmz",
        active_values,
        layer_weights[lower_random_key],
        preferred_element_type=jnp.float32,
    )
    branch = collect_frames(partial_value) + layer_weights[lowerb_key].astype(jnp.float32)
    return (values + 0.5 * branch, (scaled, inv_spread, gathered_params, upper_pre))


def ffn_backward(grad_out, stored, layer_weights, names):
    gain_key, bias_key, upper_random_key, upperb_key, lower_random_key, lowerb_key = names
    scaled, inv_spread, gathered_params, upper_pre = stored
    branch_gradient = (0.5 * grad_out).astype(jnp.bfloat16)
    wide_gradient = spread_grads(branch_gradient)
    sigmoid_up = jax.nn.sigmoid(upper_pre)
    active_values = (upper_pre * sigmoid_up).astype(jnp.bfloat16)
    lower_gradient = jnp.einsum(
        "mbc,mbx->cx", active_values, wide_gradient, preferred_element_type=jnp.float32
    )
    active_grad = jnp.einsum(
        "amz,tz->amt",
        wide_gradient,
        layer_weights[lower_random_key],
        preferred_element_type=jnp.float32,
    )
    upper_gradient = (active_grad * sigmoid_up * (1.0 + upper_pre * (1.0 - sigmoid_up))).astype(
        jnp.bfloat16
    )
    upperw_grad = jnp.einsum(
        "rzx,rzm->xm", gathered_params, upper_gradient, preferred_element_type=jnp.float32
    )
    normed_part = jnp.einsum(
        "rvc,hc->rvh",
        upper_gradient,
        layer_weights[upper_random_key],
        preferred_element_type=jnp.float32,
    )
    normed_grad = collect_grads(normed_part)
    values_grad, gain_grad, bias_grad = norm_backward(
        normed_grad, scaled, inv_spread, layer_weights[gain_key].astype(jnp.float32)
    )
    grads = {
        upper_random_key: upperw_grad,
        upperb_key: jnp.sum(upper_gradient, (0, 1), dtype=jnp.float32),
        lower_random_key: lower_gradient,
        lowerb_key: jnp.sum(branch_gradient, (0, 1), dtype=jnp.float32),
        gain_key: gain_grad,
        bias_key: bias_grad,
    }
    return (grad_out + values_grad, grads)


def score_block(queries, key_rows, rel_bias, key_valid):
    scores = jnp.einsum(
        "sihe,sjhe->shij", queries, key_rows, preferred_element_type=jnp.float32
    ) * HD ** (-0.5)
    scores = scores + rel_bias[None]
    return jnp.where(key_valid[:, None, None, :], scores, -1e30)


def attention_forward(values, layer_weights, key_valid):
    normed, scaled, inv_spread = norm_forward(
        values,
        layer_weights[ATT_GAIN].astype(jnp.float32),
        layer_weights[ATT_BIAS].astype(jnp.float32),
    )
    gathered_params = spread_frames(normed.astype(jnp.bfloat16))
    count_seq, length = (gathered_params.shape[0], gathered_params.shape[1])
    heads_here = layer_weights[REL_TABLE].shape[0]
    head_shape = (count_seq, length, heads_here, HD)
    queries = (
        (
            jnp.einsum(
                "yoz,zv->yov",
                gathered_params,
                layer_weights[W_QUERY],
                preferred_element_type=jnp.float32,
            )
            + layer_weights[B_QUERY].astype(jnp.float32)
        )
        .astype(jnp.bfloat16)
        .reshape(head_shape)
    )
    key_rows = (
        jnp.einsum(
            "yoz,zv->yov",
            gathered_params,
            layer_weights[W_KEY],
            preferred_element_type=jnp.float32,
        )
        .astype(jnp.bfloat16)
        .reshape(head_shape)
    )
    value_rows = (
        (
            jnp.einsum(
                "yoz,zv->yov",
                gathered_params,
                layer_weights[W_VALUE],
                preferred_element_type=jnp.float32,
            )
            + layer_weights[B_VALUE].astype(jnp.float32)
        )
        .astype(jnp.bfloat16)
        .reshape(head_shape)
    )
    rel_bias = rel_expand(layer_weights[REL_TABLE].astype(jnp.float32), length)
    scores = score_block(queries, key_rows, rel_bias, key_valid)
    row_max = jnp.max(scores, -1, keepdims=True)
    exponent = jnp.exp(scores - row_max)
    row_total = jnp.sum(exponent, -1, keepdims=True)
    soft_weights = exponent / row_total
    log_total = row_max + jnp.log(row_total)
    mixed_head_output = jnp.einsum(
        "shij,sjhe->sihe",
        soft_weights.astype(jnp.bfloat16),
        value_rows,
        preferred_element_type=jnp.float32,
    )
    mixed_head_output = mixed_head_output.astype(jnp.bfloat16).reshape(
        count_seq, length, heads_here * HD
    )
    partial_value = jnp.einsum(
        "rpa,ah->rph", mixed_head_output, layer_weights[W_OUT], preferred_element_type=jnp.float32
    )
    branch = collect_frames(partial_value) + layer_weights[B_OUT].astype(jnp.float32)
    stored = (
        scaled,
        inv_spread,
        gathered_params,
        queries,
        key_rows,
        value_rows,
        log_total,
        mixed_head_output,
        rel_bias,
    )
    return (values + branch, stored)


def attention_backward(grad_out, stored, layer_weights, key_valid):
    (
        scaled,
        inv_spread,
        gathered_params,
        queries,
        key_rows,
        value_rows,
        log_total,
        mixed_head_output,
        rel_bias,
    ) = stored
    count_seq, length = (gathered_params.shape[0], gathered_params.shape[1])
    branch_gradient = grad_out.astype(jnp.bfloat16)
    wide_gradient = spread_grads(branch_gradient)
    output_gradient = jnp.einsum(
        "yig,yif->gf", mixed_head_output, wide_gradient, preferred_element_type=jnp.float32
    )
    mixed_grad = jnp.einsum(
        "eom,vm->eov", wide_gradient, layer_weights[W_OUT], preferred_element_type=jnp.float32
    )
    mixed_grad = mixed_grad.astype(jnp.bfloat16).reshape(queries.shape)
    scores = score_block(queries, key_rows, rel_bias, key_valid)
    soft_weights = jnp.exp(scores - log_total)
    weights_grad = jnp.einsum(
        "sihe,sjhe->shij", mixed_grad, value_rows, preferred_element_type=jnp.float32
    )
    value_gradient = jnp.einsum(
        "shij,sihe->sjhe",
        soft_weights.astype(jnp.bfloat16),
        mixed_grad,
        preferred_element_type=jnp.float32,
    )
    scores_grad = soft_weights * (
        weights_grad - jnp.sum(soft_weights * weights_grad, -1, keepdims=True)
    )
    scores_grad = scores_grad.astype(jnp.bfloat16)
    query_gradient = jnp.einsum(
        "shij,sjhe->sihe", scores_grad, key_rows, preferred_element_type=jnp.float32
    )
    key_gradient = jnp.einsum(
        "shij,sihe->sjhe", scores_grad, queries, preferred_element_type=jnp.float32
    )
    flat_shape = (count_seq, length, queries.shape[2] * HD)
    query_gradient = (query_gradient * HD ** (-0.5)).astype(jnp.bfloat16).reshape(flat_shape)
    key_gradient = (key_gradient * HD ** (-0.5)).astype(jnp.bfloat16).reshape(flat_shape)
    value_gradient = value_gradient.astype(jnp.bfloat16).reshape(flat_shape)
    table_grad = rel_collect(jnp.sum(scores_grad, 0, dtype=jnp.float32))
    normed_part = jnp.einsum(
        "baz,nz->ban", query_gradient, layer_weights[W_QUERY], preferred_element_type=jnp.float32
    )
    normed_part = normed_part + jnp.einsum(
        "baz,nz->ban", key_gradient, layer_weights[W_KEY], preferred_element_type=jnp.float32
    )
    normed_part = normed_part + jnp.einsum(
        "baz,nz->ban", value_gradient, layer_weights[W_VALUE], preferred_element_type=jnp.float32
    )
    normed_grad = collect_grads(normed_part)
    values_grad, gain_grad, bias_grad = norm_backward(
        normed_grad, scaled, inv_spread, layer_weights[ATT_GAIN].astype(jnp.float32)
    )
    grads = {
        W_OUT: output_gradient,
        B_OUT: jnp.sum(branch_gradient, (0, 1), dtype=jnp.float32),
        W_QUERY: jnp.einsum(
            "exa,exn->an", gathered_params, query_gradient, preferred_element_type=jnp.float32
        ),
        W_KEY: jnp.einsum(
            "exa,exn->an", gathered_params, key_gradient, preferred_element_type=jnp.float32
        ),
        W_VALUE: jnp.einsum(
            "exa,exn->an", gathered_params, value_gradient, preferred_element_type=jnp.float32
        ),
        B_QUERY: jnp.sum(query_gradient, (0, 1), dtype=jnp.float32),
        B_VALUE: jnp.sum(value_gradient, (0, 1), dtype=jnp.float32),
        REL_TABLE: table_grad,
        ATT_GAIN: gain_grad,
        ATT_BIAS: bias_grad,
    }
    return (grad_out + values_grad, grads)


def conv_forward(values, layer_weights, own_valid):
    model_dim = values.shape[-1]
    normed, scaled, inv_spread = norm_forward(
        values,
        layer_weights[CNV_GAIN].astype(jnp.float32),
        layer_weights[CNV_BIAS].astype(jnp.float32),
    )
    normed_lower_half = normed.astype(jnp.bfloat16)
    lifted = jnp.einsum(
        "zkh,hp->zkp",
        normed_lower_half,
        layer_weights[POINT_ONE],
        preferred_element_type=jnp.float32,
    )
    lifted = lifted + layer_weights[POINTB_ONE].astype(jnp.float32)
    valid_mask = own_valid[..., None]
    linear_half = lifted[..., :model_dim]
    sigmoid_gate = jax.nn.sigmoid(lifted[..., model_dim:])
    glu_out = linear_half * sigmoid_gate * valid_mask
    kernel = layer_weights[DEPTH_KERNEL].astype(jnp.float32)
    conv_out = depthwise(glu_out, kernel) + layer_weights[DEPTH_BIAS].astype(jnp.float32)
    here = jnp.sum(own_valid)
    mean_here = jnp.sum(conv_out * valid_mask, (0, 1)) / here
    masked_centre = (conv_out - mean_here) * valid_mask
    sums = jnp.zeros((8, 256), jnp.float32)
    sums = sums.at[0, :model_dim].set(mean_here)
    sums = sums.at[1, :model_dim].set(jnp.sum(masked_centre * masked_centre, (0, 1)))
    sums = sums.at[2].set(here)
    everyone = share_all(sums, lax.axis_size("dp"), 2)
    counts = everyone[:, 2, :1]
    means = everyone[:, 0, :model_dim]
    valid_count = jnp.sum(counts)
    mean_all = jnp.sum(means * counts, 0) / valid_count
    spread = jnp.sum(everyone[:, 1, :model_dim] + counts * (means - mean_all) ** 2, 0) / valid_count
    centre = conv_out - mean_all
    inv_batch = lax.rsqrt(spread + NORM_EPS)
    normal = centre * inv_batch
    shifted = normal * layer_weights[BATCH_GAIN].astype(jnp.float32) + layer_weights[
        BATCH_BIAS
    ].astype(jnp.float32)
    active_values = (shifted * jax.nn.sigmoid(shifted)).astype(jnp.bfloat16)
    branch = jnp.einsum(
        "zkh,hp->zkp", active_values, layer_weights[POINT_TWO], preferred_element_type=jnp.float32
    )
    branch = branch + layer_weights[POINTB_TWO].astype(jnp.float32)
    stored = (
        scaled,
        inv_spread,
        normed_lower_half,
        linear_half,
        sigmoid_gate,
        glu_out,
        normal,
        shifted,
        active_values,
        inv_batch,
        valid_count,
        valid_mask,
    )
    return (values + branch, stored)


def conv_backward(grad_out, stored, layer_weights):
    (
        scaled,
        inv_spread,
        normed_lower_half,
        linear_half,
        sigmoid_gate,
        glu_out,
        normal,
        shifted,
        active_values,
        inv_batch,
        valid_count,
        valid_mask,
    ) = stored
    length = glu_out.shape[1]
    kernel = layer_weights[DEPTH_KERNEL].astype(jnp.float32)
    tap_count = kernel.shape[0]
    half_width = tap_count // 2
    branch_gradient = grad_out.astype(jnp.bfloat16)
    second_ffn_gradient = jnp.einsum(
        "qkj,qkc->jc", active_values, branch_gradient, preferred_element_type=jnp.float32
    )
    active_grad = jnp.einsum(
        "bmk,gk->bmg",
        branch_gradient,
        layer_weights[POINT_TWO],
        preferred_element_type=jnp.float32,
    )
    sigmoid_bn = jax.nn.sigmoid(shifted)
    shifted_grad = active_grad * sigmoid_bn * (1.0 + shifted * (1.0 - sigmoid_bn))
    scaled_grad = shifted_grad * layer_weights[BATCH_GAIN].astype(jnp.float32)
    model_dim = scaled_grad.shape[-1]
    sums = jnp.zeros((8, 256), jnp.float32)
    sums = sums.at[0, :model_dim].set(jnp.sum(scaled_grad, (0, 1)))
    sums = sums.at[1, :model_dim].set(jnp.sum(scaled_grad * normal, (0, 1)))
    everyone = jnp.sum(share_all(sums, lax.axis_size("dp"), 3), 0)
    sum_plain, sum_cross = everyone[0, :model_dim], everyone[1, :model_dim]
    conv_grad = inv_batch * (
        scaled_grad - valid_mask * (sum_plain + normal * sum_cross) / valid_count
    )
    padded_glu = jnp.pad(glu_out, ((0, 0), (half_width, half_width), (0, 0)))
    padded_grad = jnp.pad(conv_grad, ((0, 0), (half_width, half_width), (0, 0)))
    kernel_rows = []
    glu_grad = jnp.zeros_like(glu_out)
    for tap_index in range(tap_count):
        kernel_rows.append(
            jnp.sum(conv_grad * padded_glu[:, tap_index : tap_index + length], (0, 1))
        )
        start_at = tap_count - 1 - tap_index
        glu_grad = glu_grad + padded_grad[:, start_at : start_at + length] * kernel[tap_index]
    glu_grad = glu_grad * valid_mask
    linear_grad = glu_grad * sigmoid_gate
    gate_grad = glu_grad * linear_half * sigmoid_gate * (1.0 - sigmoid_gate)
    lifted_gradient = jnp.concatenate([linear_grad, gate_grad], -1).astype(jnp.bfloat16)
    one_grad = jnp.einsum(
        "qkj,qkc->jc", normed_lower_half, lifted_gradient, preferred_element_type=jnp.float32
    )
    normed_grad = jnp.einsum(
        "bmk,gk->bmg",
        lifted_gradient,
        layer_weights[POINT_ONE],
        preferred_element_type=jnp.float32,
    )
    values_grad, gain_grad, bias_grad = norm_backward(
        normed_grad, scaled, inv_spread, layer_weights[CNV_GAIN].astype(jnp.float32)
    )
    grads = {
        POINT_TWO: second_ffn_gradient,
        POINTB_TWO: jnp.sum(branch_gradient, (0, 1), dtype=jnp.float32),
        BATCH_GAIN: jnp.sum(shifted_grad * normal, (0, 1)),
        BATCH_BIAS: jnp.sum(shifted_grad, (0, 1)),
        DEPTH_KERNEL: jnp.stack(kernel_rows),
        DEPTH_BIAS: jnp.sum(conv_grad, (0, 1)),
        POINT_ONE: one_grad,
        POINTB_ONE: jnp.sum(lifted_gradient, (0, 1), dtype=jnp.float32),
        CNV_GAIN: gain_grad,
        CNV_BIAS: bias_grad,
    }
    return (grad_out + values_grad, grads)


def adam_update(master, gradient, moment_one, moment_two):
    first_new = BETA_ONE * moment_one + (1.0 - BETA_ONE) * gradient
    second_new = BETA_TWO * moment_two + (1.0 - BETA_TWO) * gradient * gradient
    first_hat = first_new / (1.0 - BETA_ONE**STEP)
    second_hat = second_new / (1.0 - BETA_TWO**STEP)
    updated = master - LEARN_RATE * (
        first_hat / (jnp.sqrt(second_hat) + ADAM_EPS) + WEIGHT_DECAY * master
    )
    return (first_new, second_new, updated)


def per_device(
    frames,
    cotangent,
    lengths,
    head_params,
    shared_params,
    head_first,
    head_second,
    shared_first,
    shared_second,
):
    model_dim = frames.shape[-1]
    seq_here = frames.shape[0]
    length = frames.shape[1]
    head_count = lax.axis_size("head")
    dp_count = lax.axis_size("dp")
    head_index = lax.axis_index("head")
    head_size = head_params.shape[1]
    shared_size = shared_params.shape[0]
    head_rows = up_to(up_to(head_size, LANES) // LANES, 16)
    shared_rows = up_to(up_to(shared_size, LANES) // LANES, 16)
    mine = jnp.concatenate(
        [
            jnp.pad(head_params[0], (0, head_rows * LANES - head_size)).reshape(head_rows, LANES),
            jnp.pad(shared_params, (0, shared_rows * LANES - shared_size)).reshape(shared_rows, LANES),
        ]
    ).astype(jnp.bfloat16)
    gathered = gather_all(mine, dp_count, 1)
    head_row = gathered[:, :, :head_rows].reshape(dp_count, 2, -1)[:, :, :head_size]
    head_row = head_row.transpose(1, 0, 2).reshape(2, -1)
    shared_all = gathered[:, :, head_rows:].reshape(dp_count * 2, -1)[:, :shared_size].reshape(-1)
    layout = head_layout(model_dim, FF // head_count, HEADS // head_count, HD, KREL)
    own_lengths = lax.dynamic_slice_in_dim(lengths, head_index * seq_here, seq_here)
    pieces = [unflatten(head_row[row_index], layout) for row_index in range(head_row.shape[0])]
    layer_weights = {
        entry_name: jnp.concatenate(
            [piece_dict[entry_name] for piece_dict in pieces], JOIN_AXIS[entry_name]
        )
        for entry_name, dims_of in layout
    }
    layer_weights.update(unflatten(shared_all, shared_layout(model_dim, KW)))
    positions = jnp.arange(length, dtype=jnp.int32)
    own_valid = (positions[None, :] < own_lengths[:, None]).astype(jnp.float32)
    key_valid = positions[None, :] < own_lengths[:, None]
    values = frames.astype(jnp.float32)
    values, stored_one = ffn_forward(values, layer_weights, FFN_ONE)
    values, stored_att = attention_forward(values, layer_weights, key_valid)
    values, stored_cnv = conv_forward(values, layer_weights, own_valid)
    values, stored_two = ffn_forward(values, layer_weights, FFN_TWO)
    final, out_scaled, out_inv = norm_forward(
        values,
        layer_weights[OUT_GAIN].astype(jnp.float32),
        layer_weights[OUT_BIAS].astype(jnp.float32),
    )
    gradient, gain_grad, bias_grad = norm_backward(
        cotangent.astype(jnp.float32),
        out_scaled,
        out_inv,
        layer_weights[OUT_GAIN].astype(jnp.float32),
    )
    grads = {OUT_GAIN: gain_grad, OUT_BIAS: bias_grad}
    gradient, more_grads = ffn_backward(gradient, stored_two, layer_weights, FFN_TWO)
    grads.update(more_grads)
    gradient, more_grads = conv_backward(gradient, stored_cnv, layer_weights)
    grads.update(more_grads)
    gradient, more_grads = attention_backward(gradient, stored_att, layer_weights, key_valid)
    grads.update(more_grads)
    gradient, more_grads = ffn_backward(gradient, stored_one, layer_weights, FFN_ONE)
    grads.update(more_grads)
    row_width = head_size * dp_count
    halves = [
        {name: jnp.split(grads[name], 2, JOIN_AXIS[name])[row] for name, _ in layout} for row in (0, 1)
    ]
    head_flat = jnp.stack([flatten_dict(half, layout, row_width) for half in halves])
    head_flat = jnp.pad(
        head_flat.reshape(2, dp_count, head_size), ((0, 0), (0, 0), (0, head_rows * LANES - head_size))
    ).reshape(2, dp_count, head_rows, LANES)
    shared_flat = flatten_dict(
        grads, shared_layout(model_dim, KW), shared_size * dp_count * head_count
    ).reshape(dp_count, 2, shared_size).transpose(1, 0, 2)
    shared_flat = jnp.pad(
        shared_flat, ((0, 0), (0, 0), (0, shared_rows * LANES - shared_size))
    ).reshape(2, dp_count, shared_rows, LANES)
    summed = scatter_all(jnp.concatenate([head_flat, shared_flat], 2).astype(jnp.bfloat16), 4)
    head_grad = summed[:head_rows].reshape(1, -1)[:, :head_size]
    shared_grad = summed[head_rows:].reshape(-1)[:shared_size]
    head_one, head_two, head_next = adam_update(head_params, head_grad, head_first, head_second)
    shared_one, shared_two, shared_next = adam_update(
        shared_params, shared_grad, shared_first, shared_second
    )
    return (
        final.astype(jnp.bfloat16),
        gradient,
        head_one,
        head_two,
        head_next,
        head_next.astype(jnp.bfloat16),
        shared_one,
        shared_two,
        shared_next,
        shared_next.astype(jnp.bfloat16),
    )


def solution(mesh):
    return jax.shard_map(
        per_device,
        mesh=mesh,
        in_specs=(
            P(("dp", "head"), None, None),
            P(("dp", "head"), None, None),
            P("dp"),
            P("head", "dp"),
            P(("dp", "head")),
            P("head", "dp"),
            P("head", "dp"),
            P(("dp", "head")),
            P(("dp", "head")),
        ),
        out_specs=(
            P(("dp", "head"), None, None),
            P(("dp", "head"), None, None),
            P("head", "dp"),
            P("head", "dp"),
            P("head", "dp"),
            P("head", "dp"),
            P(("dp", "head")),
            P(("dp", "head")),
            P(("dp", "head")),
            P(("dp", "head")),
        ),
        check_vma=False,
    )
```

profile of v0, /device:TPU:0, one launch (start us, length us, event | category | flops | bytes accessed | tf_op | source)
XLA Modules:
  0.0 608.2 jit_solution(5697641190949504569)
XLA Ops:
  6.2 2.5 fusion.24
  10.4 24.0 %gather_weights.1 = bf16[16,2,336,128]{3,2,1,0:T(8,128)(2,1)S(1)} custom-call(bf16[336,128]{1,0:T(8,128)(2,1)S(1)} %pad_maximum_fusion.4.src), custom_call_target="tpu_custom_call" | custom-call | tf_op jit(solution)/shard_map/gather_weights/pallas_call | solution.py:123
  36.2 4.2 reshape.659
  79.3 7.0 %multiply_convert_fusion.4 = (bf16[16,192,960]{2,1,0:T(8,128)(2,1)S(1)}, f32[16,192,960]{2,1,0:T(8,128)}) fusion(f32[960]{0:T(1024)S(1)} %copy-done.137, bf16[240,480]{1,0:T(8,128)(2,1)S(1)} %copy-done.57, bf16[240,480]{1,0:T(8,128)(2,1)S(1)} %copy-done.53, bf16[16,192,240]{2,1,0:T(8,128)(2,1)S(1)} %copy-done.18, f32[240]{0:T(256)S(1)} %copy-done.148, ...), kind=kOutput, calls=%fused_computation.11 | convolution fusion | flops 1438617600 | bytes 19660416 | tf_op jit(solution)/shard_map/eav,vi->eai/dot_general | solution.py:497
  86.3 2.4 fusion.144
  94.7 4.4 copy.106
  99.1 3.2 add_convert_fusion.4
  102.3 4.4 copy.105
  106.8 3.2 convolution_convert_fusion.1
  110.0 4.5 copy.107
  114.5 6.8 %fusion.145 = (f32[16,4,192]{2,1,0:T(4,128)S(1)}, f32[16,4,192,192]{2,3,1,0:T(8,128)S(1)}) fusion(f32[4,192,192]{1,2,0:T(8,128)} %copy.110, bf16[16,192,4,60]{1,0,3,2:T(8,128)(2,1)} %bitcast.214, bf16[16,192,4,60]{1,0,3,2:T(8,128)(2,1)} %bitcast.221, pred[16,192]{1,0:T(8,128)(4,1)S(1)} %copy-done.142), kind=kOutput, calls=%fused_computation.335 | convolution fusion | flops 292540416 | bytes 13028352 | tf_op jit(solution)/shard_map/sihe,sjhe->shij/dot_general | solution.py:559
  121.3 3.0 fusion
  125.8 6.2 %convert_bitcast_fusion.1 = bf16[16,192,4,60]{1,3,2,0:T(8,128)(2,1)S(1)} fusion(f32[16,4,192,192]{2,3,1,0:T(8,128)S(1)} %get-tuple-element.231, f32[16,4,192]{2,1,0:T(4,128)S(1)} %fusion, f32[16,4,192]{2,1,0:T(4,128)S(1)} %get-tuple-element.230, bf16[16,192,4,60]{1,0,3,2:T(8,128)(2,1)} %bitcast.219), kind=kOutput, calls=%fused_computation.153 | convolution fusion | flops 290930688 | bytes 12484608 | tf_op jit(solution)/shard_map/shij,sjhe->sihe/dot_general | solution.py:619
  132.1 2.4 copy.113
  134.5 4.5 copy.114
  139.0 2.2 fusion.146
  143.5 2.7 copy-done.4
  149.6 7.3 %multiply_reduce_fusion.27 = (f32[240]{0:T(256)S(1)}, f32[16,192,240]{2,1,0:T(8,128)}) fusion(f32[16,192]{1,0:T(8,128)S(1)} %get-tuple-element.224, f32[240]{0:T(256)S(1)} %copy-done.143, f32[240]{0:T(256)S(1)} %bitcast.241, f32[240]{0:T(256)S(1)} %bitcast.243, f32[240]{0:T(256)S(1)} %bitcast.246, f32[240]{0:T(256)S(1)} %bitcast.248, f32[240]{0:T(256)S(1)} %bitcast.250, ...), kind=kLoop, calls=%fused_computation.116 | loop fusion | flops 23592720 | bytes 5926848 | tf_op jit(solution)/shard_map/reduce_sum | solution.py:750
  157.7 2.6 multiply_reduce_fusion.26
  161.8 13.0 %share_sums.2 = f32[32,8,256]{2,1,0:T(8,128)} custom-call(f32[8,256]{1,0:T(8,128)} %copy-done.90), custom_call_target="tpu_custom_call" | custom-call | tf_op jit(solution)/shard_map/share_sums/pallas_call | solution.py:276
  179.3 3.5 fusion.147
  184.4 3.8 multiply_convert_fusion.3
  188.3 2.2 fusion.148
  193.1 3.7 fusion.28
  196.9 2.7 fusion.118
  199.6 8.5 %fusion.150 = (bf16[960]{0:T(1024)(128)(2,1)S(1)}, bf16[16,192,960]{2,1,0:T(8,128)(2,1)}) fusion(f32[16,192,960]{2,1,0:T(8,128)S(1)} %get-tuple-element.237, f32[960]{0:T(1024)S(1)} %copy-done.139, bf16[16,192,240]{2,1,0:T(8,128)(2,1)S(1)} %get-tuple-element.127, bf16[480,240]{1,0:T(8,128)(2,1)S(1)} %copy-done.66, bf16[480,240]{1,0:T(8,128)(2,1)S(1)} %copy-done.63), kind=kOutput, calls=%fused_computation.340 | convolution fusion | flops 1448938496 | bytes 19635840 | tf_op jit(solution)/shard_map/amz,tz->amt/dot_general | solution.py:525
  213.7 2.2 reshape.705
  216.0 6.5 %fusion.67 = bf16[240,960]{1,0:T(8,128)(2,1)S(1)} fusion(bf16[16,192,960]{2,1,0:T(8,128)(2,1)} %get-tuple-element.250, f32[16,192,240]{2,1,0:T(8,128)} %copy-done.23, f32[240]{0:T(256)} %get-tuple-element.173, f32[240]{0:T(256)} %get-tuple-element.174, f32[16,192]{1,0:T(8,128)} %copy-done.86, f32[16,192]{1,0:T(8,128)} %copy-done.77), kind=kOutput, calls=%fused_computation.173 | convolution fusion | flops 1419494400 | bytes 9334656 | tf_op jit(solution)/shard_map/rzx,rzm->xm/dot_general | solution.py:534
  222.6 6.9 %multiply_reduce_fusion.17 = (bf16[240]{0:T(256)(128)(2,1)}, f32[16,192]{1,0:T(8,128)}, f32[16,192]{1,0:T(8,128)}, bf16[240]{0:T(256)(128)(2,1)}, f32[16,192,240]{2,1,0:T(8,128)}) fusion(f32[16,192,240]{2,1,0:T(8,128)S(1)} %copy-done.24, f32[16,192]{1,0:T(8,128)S(1)} %copy-done.87, f32[16,192]{1,0:T(8,128)S(1)} %copy-done.78, f32[240]{0:T(256)S(1)} %copy-done.127, ...), kind=kOutput, calls=%fused_computation.70 | convolution fusion | flops 1423128064 | bytes 12308352 | tf_op jit(solution)/shard_map/rvc,hc->rvh/dot_general | solution.py:537
  233.8 9.6 %convert_reduce_fusion.5 = (bf16[240]{0:T(256)(128)(2,1)}, f32[16,192,240]{2,1,0:T(8,128)S(1)}, bf16[240]{0:T(256)(128)(2,1)}) fusion(f32[16,192]{1,0:T(8,128)S(1)} %broadcast_multiply_fusion.6, f32[16,192,240]{2,1,0:T(8,128)} %copy-done.23, f32[16,192]{1,0:T(8,128)} %copy-done.77, f32[16,192]{1,0:T(8,128)S(1)} %broadcast_multiply_fusion.7, ...), kind=kLoop, calls=%fused_computation.301 | loop fusion | flops 14007840 | bytes 13372224 | tf_op jit(solution)/shard_map/reduce_sum | solution.py:859
  251.1 7.6 %multiply_reduce_fusion.1 = (bf16[240]{0:T(256)(128)(2,1)}, f32[240]{0:T(256)S(1)}, f32[240]{0:T(256)S(1)}, bf16[240]{0:T(256)(128)(2,1)}, f32[16,192,240]{2,1,0:T(8,128)}) fusion(f32[16,192,240]{2,1,0:T(8,128)} %get-tuple-element.133, f32[240]{0:T(256)S(1)} %copy-done.133, f32[240]{0:T(256)S(1)} %broadcast_divide_fusion, f32[240]{0:T(256)S(1)} %copy-done.125, ...), kind=kOutput, calls=%fused_computation.54 | convolution fusion | flops 368638976 | bytes 9370176 | tf_op jit(solution)/shard_map/bmk,gk->bmg/dot_general | solution.py:813
  259.4 13.0 %share_sums.3 = f32[32,8,256]{2,1,0:T(8,128)} custom-call(f32[8,256]{1,0:T(8,128)} %copy-done.89), custom_call_target="tpu_custom_call" | custom-call | tf_op jit(solution)/shard_map/share_sums/pallas_call | solution.py:276
  273.4 31.4 %multiply_reduce_fusion.2 = (bf16[240]{0:T(256)(128)(2,1)S(1)}, bf16[240]{0:T(256)(128)(2,1)S(1)}, bf16[240]{0:T(256)(128)(2,1)S(1)}, bf16[240]{0:T(256)(128)(2,...) fusion(f32[16,192,240]{2,1,0:T(8,128)} %copy-done.10, ...), kind=kLoop, calls=%fused_computation.55 | loop fusion | flops 29487360 | bytes 11821252 | tf_op jit(solution)/shard_map/reduce_sum | solution.py:837
  315.0 28.1 %multiply_convert_fusion.9 = (bf16[16,192,240]{2,1,0:T(8,128)(2,1)S(1)}, f32[16,192,240]{2,1,0:T(8,128)S(1)}) fusion(f32[16,192,480]{2,1,0:T(8,128)} %copy-done.4, f32[16,192]{1,0:T(8,128)S(1)} %get-tuple-element.224, f32[240]{0:T(256)S(1)} %bitcast.242, f32[240]{0:T(256)S(1)} %bitcast.244, f32[240]{0:T(256)} %bitcast.245, f32[240]{0:T(256)} %bitcast.247, ...), kind=kLoop, calls=%fused_computation.80 | loop fusion | flops 25804800 | bytes 10348608 | tf_op jit(solution)/shard_map/convert.146
  343.1 4.4 multiply_convert_fusion.8
  349.5 3.1 fusion.69
  352.6 4.9 multiply_reduce_fusion.18
  361.0 5.1 convert_reduce_fusion.4
  369.9 2.5 convolution_convert_fusion
  372.4 2.7 copy.116
  375.2 8.8 %fusion.152 = (bf16[4,60]{1,0:T(4,128)(2,1)S(1)}, bf16[16,192,4,60]{1,3,2,0:T(8,128)(2,1)}) fusion(f32[16,4,192,192]{2,3,1,0:T(8,128)} %copy-done.1, f32[16,4,192]{2,1,0:T(4,128)} %bitcast.232, bf16[16,192,4,60]{1,0,3,2:T(8,128)(2,1)S(1)} %bitcast.212), kind=kOutput, calls=%fused_computation.342 | convolution fusion | flops 289308416 | bytes 12435936 | tf_op jit(solution)/shard_map/shij,sihe->sjhe/dot_general | solution.py:673
  385.1 4.1 copy.129
  389.2 4.4 copy.130
  397.4 10.3 %multiply_reduce_fusion = (f32[16,4,192]{2,1,0:T(4,128)S(1)}, f32[16,4,192,192]{2,3,1,0:T(8,128)S(1)}) fusion(f32[16,4,192,192]{2,3,1,0:T(8,128)} %copy-done.1, f32[16,4,192]{2,1,0:T(4,128)} %bitcast.233, bf16[16,192,4,60]{1,0,3,2:T(8,128)(2,1)} %bitcast.220, bf16[16,192,4,60]{1,0,3,2:T(8,128)(2,1)S(1)} %bitcast.213), kind=kOutput, calls=%fused_computation.3 | convolution fusion | flops 290181120 | bytes 21921792 | tf_op jit(solution)/shard_map/sihe,sjhe->shij/dot_general | solution.py:670
  407.7 10.7 %convert_reduce_fusion = (f32[4,192,192]{1,2,0:T(8,128)S(1)}, bf16[16,4,192,192]{2,3,1,0:T(8,128)(2,1)}) fusion(f32[16,4,192,192]{2,3,1,0:T(8,128)S(1)} %get-tuple-element.244, f32[16,4,192]{2,1,0:T(4,128)S(1)} %get-tuple-element.243, f32[16,4,192,192]{2,3,1,0:T(8,128)} %copy-done.1, f32[16,4,192]{2,1,0:T(4,128)S(1)} %bitcast.234), kind=kLoop, calls=%fused_computation | loop fusion | flops 14008320 | bytes 24281088 | tf_op jit(solution)/shard_map/reduce_sum | solution.py:693
  419.6 5.4 fusion.62
  425.0 3.2 fusion.151
  429.4 3.4 copy.126
  440.1 4.0 reshape.699
  446.5 2.3 fusion.84
  450.0 3.8 copy.122
  457.6 2.2 fusion.85
  459.9 5.3 multiply_reduce_fusion.19
  465.2 2.8 fusion.113
  468.1 11.8 %fusion.149 = (bf16[960]{0:T(1024)(128)(2,1)S(1)}, bf16[16,192,960]{2,1,0:T(8,128)(2,1)}) fusion(f32[16,192,960]{2,1,0:T(8,128)} %get-tuple-element.227, f32[960]{0:T(1024)S(1)} %copy-done.138, bf16[480,240]{1,0:T(8,128)(2,1)S(1)} %copy-done.60, bf16[480,240]{1,0:T(8,128)(2,1)S(1)} %copy-done.56, f32[16,192,240]{2,1,0:T(8,128)S(1)} %get-tuple-element.129), kind=kOutput, calls=%fused_computation.339 | convolution fusion | flops 1450413056 | bytes 21110400 | tf_op jit(solution)/shard_map/amz,tz->amt/dot_general | solution.py:525
  484.4 5.4 fusion.65
  490.0 6.9 %fusion.23 = (bf16[240]{0:T(256)(128)(2,1)}, f32[16,192]{1,0:T(8,128)}, f32[16,192]{1,0:T(8,128)}, bf16[240]{0:T(256)(128)(2,1)}, f32[16,192,240]{2,1,0:T(8,128)}) fusion(bf16[16,192,240]{2,1,0:T(8,128)(2,1)S(1)} %copy-done.20, f32[16,192]{1,0:T(8,128)S(1)} %copy-done.85, f32[16,192]{1,0:T(8,128)S(1)} %copy-done.74, f32[240]{0:T(256)S(1)} %copy-done.120, ...), kind=kOutput, calls=%fused_computation.43 | convolution fusion | flops 1423865344 | bytes 10833792 | tf_op jit(solution)/shard_map/rvc,hc->rvh/dot_general | solution.py:537
  496.9 16.0 %concatenate.108 = bf16[180960]{0:T(1024)(128)(2,1)S(1)} concatenate(bf16[240]{0:T(256)(128)(2,1)} %get-tuple-element.95, bf16[240]{0:T(256)(128)(2,1)} %get-tuple-element.107, bf16[240]{0:T(256)(128)(2,1)} %get-tuple-element.74, bf16[240]{0:T(256)(128)(2,1)} %get-tuple-element.106, bf16[240]{0:T(256)(128)(2,1)} %get-tuple-element.72, bf16[240]{0:T(256)(128)(2,1)} %get-tuple-element.105, ...), dimensions={0} | concatenate | bytes 723840 | tf_op jit(solution)/shard_map/concatenate | solution.py:426
  514.3 22.6 %concatenate.106 = bf16[577968]{0:T(1024)(128)(2,1)} concatenate(bf16[115200]{0:T(1024)(128)(2,1)S(1)} %reshape.691, bf16[480]{0:T(512)(128)(2,1)S(1)} %get-tuple-element.218, bf16[115200]{0:T(1024)(128)(2,1)S(1)} %reshape.692, bf16[115200]{0:T(1024)(128)(2,1)S(1)} %copy-done.34, bf16[480]{0:T(512)(128)(2,1)S(1)} %copy-done.134, bf16[115200]{0:T(1024)(128)(2,1)S(1)} %copy-done.33, ...), dimensions={0} | concatenate | bytes 2311872 | tf_op jit(solution)/shard_map/concatenate | solution.py:426
  536.9 2.8 stack.73
  541.6 5.8 fusion.22
  548.5 28.3 %concatenate.107 = bf16[577968]{0:T(1024)(128)(2,1)} concatenate(bf16[115200]{0:T(1024)(128)(2,1)S(1)} %reshape.702, bf16[480]{0:T(512)(128)(2,1)} %get-tuple-element.219, bf16[115200]{0:T(1024)(128)(2,1)} %reshape.703, bf16[115200]{0:T(1024)(128)(2,1)} %reshape.704, bf16[480]{0:T(512)(128)(2,1)} %get-tuple-element.217, bf16[115200]{0:T(1024)(128)(2,1)} %reshape.705, ...), dimensions={0} | concatenate | bytes 2311872 | tf_op jit(solution)/shard_map/concatenate | solution.py:426
  576.8 2.8 stack.74
  580.5 24.9 %scatter_grads.1 = f32[336,128]{1,0:T(8,128)S(1)} custom-call(bf16[2,16,336,128]{3,2,1,0:T(8,128)(2,1)S(1)} %pad_maximum_fusion.1.g), custom_call_target="tpu_custom_call" | custom-call | tf_op jit(solution)/shard_map/scatter_grads/pallas_call | solution.py:219
  (509 shorter events, 144.1 us)
Async XLA Ops:
  0.6 9.3 %copy-start.35 = (f32[1,36123]{1,0:T(1,128)S(1)}, f32[1,36123]{1,0:T(1,128)}, u32[]{:S(2)}) copy-start(f32[1,36123]{1,0:T(1,128)} %param.22) | copy-start | bytes 433480
  46.0 14.3 %copy-start.28 = (bf16[32,5655]{1,0:T(8,128)(2,1)S(1)}, bf16[32,5655]{1,0:T(8,128)(2,1)}, u32[]{:S(2)}) copy-start(bf16[32,5655]{1,0:T(8,128)(2,1)} %slice.569) | copy-start | bytes 1085764
  57.0 9.2 %copy-start.145 = (bf16[120]{0:T(256)(128)(2,1)S(1)}, bf16[120]{0:T(256)(128)(2,1)}, u32[]{:S(2)}) copy-start(bf16[120]{0:T(256)(128)(2,1)} %get-tuple-element.158) | copy-start | bytes 724
  57.0 9.2 %copy-start.146 = (bf16[120]{0:T(256)(128)(2,1)S(1)}, bf16[120]{0:T(256)(128)(2,1)}, u32[]{:S(2)}) copy-start(bf16[120]{0:T(256)(128)(2,1)} %get-tuple-element.159) | copy-start | bytes 724
  57.0 10.1 %copy-start.140 = (bf16[480]{0:T(512)(128)(2,1)S(1)}, bf16[480]{0:T(512)(128)(2,1)}, u32[]{:S(2)}) copy-start(bf16[480]{0:T(512)(128)(2,1)} %get-tuple-element.146) | copy-start | bytes 2884
  57.0 10.1 %copy-start.141 = (bf16[480]{0:T(512)(128)(2,1)S(1)}, bf16[480]{0:T(512)(128)(2,1)}, u32[]{:S(2)}) copy-start(bf16[480]{0:T(512)(128)(2,1)} %get-tuple-element.147) | copy-start | bytes 2884
  57.0 10.8 %copy-start.117 = (bf16[2,383]{1,0:T(2,128)(2,1)S(1)}, bf16[2,383]{1,0:T(2,128)(2,1)}, u32[]{:S(2)}) copy-start(bf16[2,383]{1,0:T(2,128)(2,1)} %reshape.673) | copy-start | bytes 4600
  62.1 28.0 %copy-start.93 = (f32[240]{0:T(256)}, f32[240]{0:T(256)S(1)}, u32[]{:S(2)}) copy-start(f32[240]{0:T(256)S(1)} %get-tuple-element.183) | copy-start | bytes 2884
  63.6 10.8 %copy-start.47 = (bf16[754,240]{1,0:T(8,128)(2,1)}, bf16[754,240]{1,0:T(8,128)(2,1)S(1)}, u32[]{:S(2)}) copy-start(bf16[754,240]{1,0:T(8,128)(2,1)S(1)} %slice.500) | copy-start | bytes 1085764
  79.2 7.1 %copy-start.19 = (bf16[16,192,240]{2,1,0:T(8,128)(2,1)S(1)}, bf16[16,192,240]{2,1,0:T(8,128)(2,1)}, u32[]{:S(2)}) copy-start(bf16[16,192,240]{2,1,0:T(8,128)(2,1)} %param.19) | copy-start | bytes 4423684
  79.2 7.1 %copy-start.55 = (bf16[480,240]{1,0:T(8,128)(2,1)S(1)}, bf16[480,240]{1,0:T(8,128)(2,1)}, u32[]{:S(2)}) copy-start(bf16[480,240]{1,0:T(8,128)(2,1)} %reshape.662) | copy-start | bytes 691204
  79.2 7.1 %copy-start.59 = (bf16[480,240]{1,0:T(8,128)(2,1)S(1)}, bf16[480,240]{1,0:T(8,128)(2,1)}, u32[]{:S(2)}) copy-start(bf16[480,240]{1,0:T(8,128)(2,1)} %reshape.663) | copy-start | bytes 691204
  79.2 7.0 %copy-start.154 = (f32[240]{0:T(256)S(1)}, f32[240]{0:T(256)}, u32[]{:S(2)}) copy-start(f32[240]{0:T(256)} %get-tuple-element.184) | copy-start | bytes 2884
  89.0 50.0 %copy-start.2 = (f32[16,192,240]{2,1,0:T(8,128)}, f32[16,192,240]{2,1,0:T(8,128)S(1)}, u32[]{:S(2)}) copy-start(f32[16,192,240]{2,1,0:T(8,128)S(1)} %get-tuple-element.229) | copy-start | bytes 8847364
  92.9 6.2 %copy-start.135 = (f32[240]{0:T(256)S(1)}, f32[240]{0:T(256)}, u32[]{:S(2)}) copy-start(f32[240]{0:T(256)} %get-tuple-element.257) | copy-start | bytes 2884
  106.8 7.7 %copy-start.142 = (pred[16,192]{1,0:T(8,128)(4,1)S(1)}, pred[16,192]{1,0:T(8,128)(4,1)}, u32[]{:S(2)}) copy-start(pred[16,192]{1,0:T(8,128)(4,1)} %get-tuple-element.225) | copy-start | bytes 9220
  132.1 6.9 %copy-start.129 = (f32[240]{0:T(256)S(1)}, f32[240]{0:T(256)}, u32[]{:S(2)}) copy-start(f32[240]{0:T(256)} %get-tuple-element.181) | copy-start | bytes 2884
  156.9 22.4 %copy-start.6 = (f32[16,192,240]{2,1,0:T(8,128)S(1)}, f32[16,192,240]{2,1,0:T(8,128)}, u32[]{:S(2)}) copy-start(f32[16,192,240]{2,1,0:T(8,128)} %copy-done.5) | copy-start | bytes 8847364
  156.9 22.4 %copy-start.123 = (f32[240]{0:T(256)S(1)}, f32[240]{0:T(256)}, u32[]{:S(2)}) copy-start(f32[240]{0:T(256)} %get-tuple-element.177) | copy-start | bytes 2884
  190.6 6.3 %copy-start.9 = (f32[16,192,240]{2,1,0:T(8,128)}, f32[16,192,240]{2,1,0:T(8,128)S(1)}, u32[]{:S(2)}) copy-start(f32[16,192,240]{2,1,0:T(8,128)S(1)} %get-tuple-element.239) | copy-start | bytes 8847364
  216.0 6.5 %copy-start.24 = (f32[16,192,240]{2,1,0:T(8,128)S(1)}, f32[16,192,240]{2,1,0:T(8,128)}, u32[]{:S(2)}) copy-start(f32[16,192,240]{2,1,0:T(8,128)} %copy-done.23) | copy-start | bytes 8847364
  216.0 6.6 %copy-start.62 = (bf16[240,480]{1,0:T(8,128)(2,1)S(1)}, bf16[240,480]{1,0:T(8,128)(2,1)}, u32[]{:S(2)}) copy-start(bf16[240,480]{1,0:T(8,128)(2,1)} %reshape.681) | copy-start | bytes 691204
  216.0 6.6 %copy-start.65 = (bf16[240,480]{1,0:T(8,128)(2,1)S(1)}, bf16[240,480]{1,0:T(8,128)(2,1)}, u32[]{:S(2)}) copy-start(bf16[240,480]{1,0:T(8,128)(2,1)} %reshape.682) | copy-start | bytes 691204
  216.0 6.6 %copy-start.78 = (f32[16,192]{1,0:T(8,128)S(1)}, f32[16,192]{1,0:T(8,128)}, u32[]{:S(2)}) copy-start(f32[16,192]{1,0:T(8,128)} %copy-done.77) | copy-start | bytes 36868
  216.0 6.6 %copy-start.87 = (f32[16,192]{1,0:T(8,128)S(1)}, f32[16,192]{1,0:T(8,128)}, u32[]{:S(2)}) copy-start(f32[16,192]{1,0:T(8,128)} %copy-done.86) | copy-start | bytes 36868
  216.0 6.6 %copy-start.127 = (f32[240]{0:T(256)S(1)}, f32[240]{0:T(256)}, u32[]{:S(2)}) copy-start(f32[240]{0:T(256)} %get-tuple-element.174) | copy-start | bytes 2884
  233.8 11.2 %copy-start.11 = (f32[16,192,240]{2,1,0:T(8,128)S(1)}, f32[16,192,240]{2,1,0:T(8,128)}, u32[]{:S(2)}) copy-start(f32[16,192,240]{2,1,0:T(8,128)} %get-tuple-element.133) | copy-start | bytes 8847364
  233.8 11.2 %copy-start.124 = (f32[240]{0:T(256)S(1)}, f32[240]{0:T(256)}, u32[]{:S(2)}) copy-start(f32[240]{0:T(256)} %get-tuple-element.177) | copy-start | bytes 2884
  233.8 11.2 %copy-start.132 = (f32[240]{0:T(256)S(1)}, f32[240]{0:T(256)}, u32[]{:S(2)}) copy-start(f32[240]{0:T(256)} %copy-done.131) | copy-start | bytes 2884
  233.8 11.2 %copy-start.150 = (f32[240]{0:T(256)S(1)}, f32[240]{0:T(256)}, u32[]{:S(2)}) copy-start(f32[240]{0:T(256)} %get-tuple-element.176) | copy-start | bytes 2884
  273.4 41.6 %copy-start.98 = (f32[1,240]{1,0:T(1,128)S(1)}, f32[1,240]{1,0:T(1,128)}, u32[]{:S(2)}) copy-start(f32[1,240]{1,0:T(1,128)} %get-tuple-element.197) | copy-start | bytes 2884
  273.4 41.6 %copy-start.100 = (f32[1,240]{1,0:T(1,128)S(1)}, f32[1,240]{1,0:T(1,128)}, u32[]{:S(2)}) copy-start(f32[1,240]{1,0:T(1,128)} %get-tuple-element.198) | copy-start | bytes 2884
  273.4 41.6 %copy-start.102 = (f32[1,240]{1,0:T(1,128)S(1)}, f32[1,240]{1,0:T(1,128)}, u32[]{:S(2)}) copy-start(f32[1,240]{1,0:T(1,128)} %get-tuple-element.199) | copy-start | bytes 2884
  361.0 6.7 %copy-start.17 = (bf16[16,192,240]{2,1,0:T(8,128)(2,1)S(1)}, bf16[16,192,240]{2,1,0:T(8,128)(2,1)}, u32[]{:S(2)}) copy-start(bf16[16,192,240]{2,1,0:T(8,128)(2,1)} %copy.114) | copy-start | bytes 4423684
  385.1 8.6 %copy-start.13 = (bf16[16,192,240]{2,1,0:T(8,128)(2,1)S(1)}, bf16[16,192,240]{2,1,0:T(8,128)(2,1)}, u32[]{:S(2)}) copy-start(bf16[16,192,240]{2,1,0:T(8,128)(2,1)} %copy-done.12) | copy-start | bytes 4423684
  397.4 10.3 %copy-start.30 = (f32[8,8,192]{2,1,0:T(8,128)S(1)}, f32[8,8,192]{2,1,0:T(8,128)}, u32[]{:S(2)}) copy-start(f32[8,8,192]{2,1,0:T(8,128)} %log_add_fusion) | copy-start | bytes 147460
  418.4 6.6 %slice-start.1 = ((s8[6291456]{0:T(1024)(128)(4,1)}), s8[2097152]{0:T(1024)(128)(4,1)S(1)}, s32[]{:S(2)}) async-start(s8[6291456]{0:T(1024)(128)(4,1)} %bitcast.210), calls=%async_computation.1 | async-start | bytes 4194304
  438.8 7.7 %copy-start.26 = (bf16[16,192,240]{2,1,0:T(8,128)(2,1)S(1)}, bf16[16,192,240]{2,1,0:T(8,128)(2,1)}, u32[]{:S(2)}) copy-start(bf16[16,192,240]{2,1,0:T(8,128)(2,1)} %copy.126) | copy-start | bytes 4423684
  438.8 7.7 %copy-start.40 = (bf16[240,120]{1,0:T(8,128)(2,1)S(1)}, bf16[240,120]{1,0:T(8,128)(2,1)}, u32[]{:S(2)}) copy-start(bf16[240,120]{1,0:T(8,128)(2,1)} %reshape.670) | copy-start | bytes 172804
  438.8 7.7 %copy-start.44 = (bf16[240,120]{1,0:T(8,128)(2,1)S(1)}, bf16[240,120]{1,0:T(8,128)(2,1)}, u32[]{:S(2)}) copy-start(bf16[240,120]{1,0:T(8,128)(2,1)} %reshape.671) | copy-start | bytes 172804
  465.2 14.6 %slice-start.4 = ((s8[6291456]{0:T(1024)(128)(4,1)}), s8[4194304]{0:T(1024)(128)(4,1)S(1)}, s32[]{:S(2)}) async-start(s8[6291456]{0:T(1024)(128)(4,1)} %bitcast.274), calls=%async_computation.4 | async-start | bytes 8388608
  468.0 11.8 %copy-start.22 = (f32[16,192,240]{2,1,0:T(8,128)}, f32[16,192,240]{2,1,0:T(8,128)S(1)}, u32[]{:S(2)}) copy-start(f32[16,192,240]{2,1,0:T(8,128)S(1)} %get-tuple-element.129) | copy-start | bytes 8847364
  468.1 11.8 %slice-start.5 = ((s8[6291456]{0:T(1024)(128)(4,1)}), s8[2097152]{0:T(1024)(128)(4,1)S(1)}, s32[]{:S(2)}) async-start(s8[6291456]{0:T(1024)(128)(4,1)} %bitcast.274), calls=%async_computation.5 | async-start | bytes 4194304
  489.9 7.0 %copy-start.32 = (bf16[115200]{0:T(1024)(128)(2,1)S(1)}, bf16[115200]{0:T(1024)(128)(2,1)}, u32[]{:S(2)}) copy-start(bf16[115200]{0:T(1024)(128)(2,1)} %reshape.712) | copy-start | bytes 691204
  489.9 7.0 %copy-start.88 = (bf16[3600]{0:T(1024)(128)(2,1)S(1)}, bf16[3600]{0:T(1024)(128)(2,1)}, u32[]{:S(2)}) copy-start(bf16[3600]{0:T(1024)(128)(2,1)} %reshape.713) | copy-start | bytes 21604
  489.9 7.0 %copy-start.118 = (bf16[480]{0:T(512)(128)(2,1)S(1)}, bf16[480]{0:T(512)(128)(2,1)}, u32[]{:S(2)}) copy-start(bf16[480]{0:T(512)(128)(2,1)} %fusion.75) | copy-start | bytes 2884
  489.9 7.0 %copy-start.144 = (bf16[240]{0:T(256)(128)(2,1)S(1)}, bf16[240]{0:T(256)(128)(2,1)}, u32[]{:S(2)}) copy-start(bf16[240]{0:T(256)(128)(2,1)} %get-tuple-element.93) | copy-start | bytes 1444
  489.9 24.3 %copy-start.33 = (bf16[115200]{0:T(1024)(128)(2,1)S(1)}, bf16[115200]{0:T(1024)(128)(2,1)}, u32[]{:S(2)}) copy-start(bf16[115200]{0:T(1024)(128)(2,1)} %reshape.694) | copy-start | bytes 691204
  489.9 24.3 %copy-start.34 = (bf16[115200]{0:T(1024)(128)(2,1)S(1)}, bf16[115200]{0:T(1024)(128)(2,1)}, u32[]{:S(2)}) copy-start(bf16[115200]{0:T(1024)(128)(2,1)} %reshape.693) | copy-start | bytes 691204
  489.9 24.3 %copy-start.69 = (bf16[28800]{0:T(1024)(128)(2,1)S(1)}, bf16[28800]{0:T(1024)(128)(2,1)}, u32[]{:S(2)}) copy-start(bf16[28800]{0:T(1024)(128)(2,1)} %reshape.701) | copy-start | bytes 172804
  490.0 24.3 %copy-start.70 = (bf16[28800]{0:T(1024)(128)(2,1)S(1)}, bf16[28800]{0:T(1024)(128)(2,1)}, u32[]{:S(2)}) copy-start(bf16[28800]{0:T(1024)(128)(2,1)} %reshape.697) | copy-start | bytes 172804
  490.0 24.3 %copy-start.116 = (bf16[766]{0:T(1024)(128)(2,1)S(1)}, bf16[766]{0:T(1024)(128)(2,1)}, u32[]{:S(2)}) copy-start(bf16[766]{0:T(1024)(128)(2,1)} %reshape.700) | copy-start | bytes 4600
  490.0 24.3 %copy-start.134 = (bf16[480]{0:T(512)(128)(2,1)S(1)}, bf16[480]{0:T(512)(128)(2,1)}, u32[]{:S(2)}) copy-start(bf16[480]{0:T(512)(128)(2,1)} %get-tuple-element.216) | copy-start | bytes 2884
  514.3 22.6 %copy-start.147 = (bf16[2]{0:T(256)(128)(2,1)}, bf16[2]{0:T(256)(128)(2,1)S(1)}, u32[]{:S(2)}) copy-start(bf16[2]{0:T(256)(128)(2,1)S(1)} %broadcast.369) | copy-start | bytes 16
  541.6 6.4 %copy-start.31 = (bf16[240,480]{1,0:T(8,128)(2,1)S(1)}, bf16[240,480]{1,0:T(8,128)(2,1)}, u32[]{:S(2)}) copy-start(bf16[240,480]{1,0:T(8,128)(2,1)} %get-tuple-element.169) | copy-start | bytes 691204
  541.6 6.9 %copy-start.67 = (bf16[28800]{0:T(1024)(128)(2,1)S(1)}, bf16[28800]{0:T(1024)(128)(2,1)}, u32[]{:S(2)}) copy-start(bf16[28800]{0:T(1024)(128)(2,1)} %reshape.710) | copy-start | bytes 172804
  541.6 6.9 %copy-start.68 = (bf16[28800]{0:T(1024)(128)(2,1)S(1)}, bf16[28800]{0:T(1024)(128)(2,1)}, u32[]{:S(2)}) copy-start(bf16[28800]{0:T(1024)(128)(2,1)} %reshape.708) | copy-start | bytes 172804
  541.6 6.9 %copy-start.71 = (bf16[28800]{0:T(1024)(128)(2,1)S(1)}, bf16[28800]{0:T(1024)(128)(2,1)}, u32[]{:S(2)}) copy-start(bf16[28800]{0:T(1024)(128)(2,1)} %reshape.707) | copy-start | bytes 172804
  580.2 25.2 %copy-start.83 = (f32[5655]{0:T(1024)S(1)}, f32[5655]{0:T(1024)}, u32[]{:S(2)}) copy-start(f32[5655]{0:T(1024)} %param.23) | copy-start | bytes 67864
  580.3 25.2 %copy-start.91 = (f32[5655]{0:T(1024)S(1)}, f32[5655]{0:T(1024)}, u32[]{:S(2)}) copy-start(f32[5655]{0:T(1024)} %param.27) | copy-start | bytes 67864
  580.3 25.2 %copy-start.92 = (f32[5655]{0:T(1024)S(1)}, f32[5655]{0:T(1024)}, u32[]{:S(2)}) copy-start(f32[5655]{0:T(1024)} %param.26) | copy-start | bytes 67864
  580.3 25.9 %copy-start.36 = (f32[1,36123]{1,0:T(1,128)S(1)}, f32[1,36123]{1,0:T(1,128)}, u32[]{:S(2)}) copy-start(f32[1,36123]{1,0:T(1,128)} %param.22) | copy-start | bytes 433480
  580.3 25.8 %copy-start.81 = (f32[1,36123]{1,0:T(1,128)S(1)}, f32[1,36123]{1,0:T(1,128)}, u32[]{:S(2)}) copy-start(f32[1,36123]{1,0:T(1,128)} %param.25) | copy-start | bytes 433480
  580.3 25.8 %copy-start.82 = (f32[1,36123]{1,0:T(1,128)S(1)}, f32[1,36123]{1,0:T(1,128)}, u32[]{:S(2)}) copy-start(f32[1,36123]{1,0:T(1,128)} %param.24) | copy-start | bytes 433480
  (98 other events, 300.6 us)
where the time goes:
time: 615 us; the launch traced here: 608 us
  local copies, waits for them, and re-layouts  221 us (36%)
  matrix products  158 us (26%)
  other arithmetic  151 us (25%)
  Pallas kernels  74.8 us (12%)
    concatenate x3, local copies, waits for them, and re-layouts, flatten_dict(): return jnp.concatenate(flat_parts)  66.9 us
    another operation x4, other arithmetic  33.6 us
    reduce_sum x1, other arithmetic, conv_backward(): jnp.sum(conv_grad * padded_glu[:, tap_index:tap_index + length], (0, 1))  31.4 us
    pallas_call x2, Pallas kernels, share_all(): pl.pallas_call(functools.partial(share_kernel, dp), out_shape=jax.ShapeDt...  26 us
    pallas_call x1, Pallas kernels, scatter_all(): pl.pallas_call(functools.partial(scatter_kernel, nz), out_shape=jax.Shape...  24.9 us
    pallas_call x1, Pallas kernels, gather_all(): pl.pallas_call(functools.partial(gather_kernel, nz), out_shape=jax.ShapeD...  24 us
    reshape x21, local copies, waits for them, and re-layouts, flatten_dict(): grads[entry_name].reshape(-1)  23 us
    dot_general x2, matrix products, ffn_backward(): jnp.einsum('amz,tz->amt', wide_gradient, layer_weights[lower_random_key],...  20.3 us

commit v1 on v0

v1 whole, which is shorter than its diff:
```python
import functools
import math

import jax
import jax.numpy as jnp
from jax import lax
from jax.experimental import pallas as pl
from jax.experimental.pallas import tpu as pltpu
from jax.sharding import PartitionSpec as P

BF = jnp.bfloat16
F32 = jnp.float32
LANES = 128


def up_to(count, unit):
    return -(-count // unit) * unit


def grid_place(nz):
    me = lax.axis_index("dp")
    core = lax.axis_index("head")
    zc = me // 4
    rest = me - 4 * zc
    yc = rest // 2
    xc = rest - 2 * yc
    return me, core, zc, yc, xc


def remote(src, dst, send, recv, dp, head):
    return pltpu.make_async_remote_copy(
        src_ref=src,
        dst_ref=dst,
        send_sem=send,
        recv_sem=recv,
        device_id={"dp": dp, "head": head},
        device_id_type=pl.DeviceIdType.MESH,
    )


def greet(nz, me, core, zc, yc, xc):
    barrier = pltpu.get_barrier_semaphore()

    def hello(dp, head):
        pl.semaphore_signal(
            barrier, inc=1, device_id={"dp": dp, "head": head}, device_id_type=pl.DeviceIdType.MESH
        )

    for k in range(1, nz):
        hello(lax.rem(zc + k, nz) * 4 + 2 * yc + xc, core)
    hello(4 * zc + 2 * (1 - yc) + xc, core)
    hello(4 * zc + 2 * yc + 1 - xc, core)
    hello(me, 1 - core)
    pl.semaphore_wait(barrier, nz + 2)


def gather_kernel(nz, src, out, sz, rz, s1, r1, s2, r2, sc, rc):
    rows = src.shape[0]
    row_a = up_to(rows // 2, 16)
    parts = (pl.ds(0, row_a), pl.ds(row_a, rows - row_a))
    me, core, zc, yc, xc = grid_place(nz)
    greet(nz, me, core, zc, yc, xc)
    out[me, core] = src[...]
    y_peer = 4 * zc + 2 * (1 - yc) + xc
    x_peer = 4 * zc + 2 * yc + 1 - xc
    firsts = (y_peer, x_peer)
    seconds = (x_peer, y_peer)
    pending = []

    def send(slot, p, send_sem, recv_sem, dp, head):
        block = out.at[slot, core, parts[p]]
        copy = remote(block, block, send_sem, recv_sem, dp, head)
        copy.start()
        pending.append(copy)

    def arrived(slot, which, p, send_sem, recv_sem):
        block = out.at[slot, which, parts[p]]
        remote(block, block, send_sem, recv_sem, me, 1 - core).wait_recv()

    zs = [lax.rem(zc + k, nz) for k in range(nz)]
    here = 2 * yc + xc
    first_here = (2 * (1 - yc) + xc, 2 * yc + 1 - xc)
    second_here = ((2 * yc + 1 - xc, 2 * (1 - yc) + 1 - xc), (2 * (1 - yc) + xc, 2 * (1 - yc) + 1 - xc))
    for k in range(1, nz):
        for p in (0, 1):
            send(me, p, sz.at[p, k], rz.at[p, zc], zs[k] * 4 + here, core)
    for k in range(nz):
        z = zs[k]
        slot = 4 * z + here
        for p in (0, 1):
            if k:
                arrived(slot, core, p, sz.at[p, k], rz.at[p, z])
            send(slot, p, s1.at[p, k], r1.at[p, z], firsts[p], core)
            send(slot, p, s2.at[p, k, 0], r2.at[p, z, 0], seconds[p], core)
            send(slot, p, sc.at[p, k, 0], rc.at[p, z, 0], me, 1 - core)
    for k in range(nz):
        z = zs[k]
        for p in (0, 1):
            slot = 4 * z + first_here[p]
            arrived(slot, core, p, s1.at[p, k], r1.at[p, z])
            send(slot, p, s2.at[p, k, 1], r2.at[p, z, 1], seconds[p], core)
            send(slot, p, sc.at[p, k, 1], rc.at[p, z, 1], me, 1 - core)
    for k in range(nz):
        z = zs[k]
        for p in (0, 1):
            for b in (0, 1):
                slot = 4 * z + second_here[p][b]
                arrived(slot, core, p, s2.at[p, k, b], r2.at[p, z, b])
                send(slot, p, sc.at[p, k, 2 + b], rc.at[p, z, 2 + b], me, 1 - core)
    for k in range(nz):
        z = zs[k]
        for p in (0, 1):
            for b, at in enumerate((here, first_here[p]) + second_here[p]):
                arrived(4 * z + at, 1 - core, p, sc.at[p, k, b], rc.at[p, z, b])
    for copy in pending:
        copy.wait_send()


def gather_all(block, dp, collective_id):
    rows = block.shape[0]
    nz = dp // 4
    dma = pltpu.SemaphoreType.DMA
    return pl.pallas_call(
        functools.partial(gather_kernel, nz),
        out_shape=jax.ShapeDtypeStruct((dp, 2, rows, LANES), block.dtype),
        in_specs=[pl.BlockSpec(memory_space=pltpu.VMEM)],
        out_specs=pl.BlockSpec(memory_space=pltpu.VMEM),
        scratch_shapes=[dma((2, nz)), dma((2, nz)), dma((2, nz)), dma((2, nz)), dma((2, nz, 2)), dma((2, nz, 2)), dma((2, nz, 4)), dma((2, nz, 4))],
        compiler_params=pltpu.CompilerParams(
            collective_id=collective_id, has_side_effects=True, vmem_limit_bytes=40 << 20
        ),
        name="gather_weights",
    )(block)


def scatter_kernel(nz, g, out, c1, t1, rx1, t2, rx2, t3, rx3, sc, rc, s1, r1, s2, r2, s3, r3):
    rows = g.shape[2]
    row_a = up_to(rows // 2, 16)
    starts = (0, row_a)
    sizes = (row_a, rows - row_a)
    parts = tuple(pl.ds(a, n) for a, n in zip(starts, sizes))
    me, core, zc, yc, xc = grid_place(nz)
    greet(nz, me, core, zc, yc, xc)
    y_peer = 4 * zc + 2 * (1 - yc) + xc
    x_peer = 4 * zc + 2 * yc + 1 - xc
    firsts = (x_peer, y_peer)
    seconds = (y_peer, x_peer)
    pending = []

    def send(src, dst, send_sem, recv_sem, dp, head):
        copy = remote(src, dst, send_sem, recv_sem, dp, head)
        copy.start()
        pending.append(copy)

    def arrived(block, send_sem, recv_sem):
        remote(block, block, send_sem, recv_sem, me, 1 - core).wait_recv()

    order = list(range(1, nz)) + [0]
    zs = [lax.rem(zc + k, nz) for k in range(nz)]
    give = ((1 - xc, 2 + 1 - xc), (2 * (1 - yc), 2 * (1 - yc) + 1))
    second_give = (1 - yc, 1 - xc)
    second_keep = (yc, xc)

    def place(p, b):
        return 2 * b + xc if p == 0 else 2 * yc + b

    for k in order:
        z = zs[k]
        send(g.at[1 - core, pl.ds(4 * z, 4)], c1.at[pl.ds(4 * z, 4)], sc.at[k], rc.at[z], me, 1 - core)
    for k in order:
        z = zs[k]
        arrived(c1.at[pl.ds(4 * z, 4)], sc.at[k], rc.at[z])
        for p in (0, 1):
            n = pl.ds(0, sizes[p])
            for b in (0, 1):
                slot = 4 * z + give[p][b]
                t1[p, z, b, n] = (g[core, slot, parts[p]].astype(F32) + c1[slot, parts[p]].astype(F32)).astype(BF)
            send(t1.at[p, z, :, n], rx1.at[p, z, :, n], s1.at[p, k], r1.at[p, z], firsts[p], core)

    def partial(p, z, b):
        slot = 4 * z + place(p, b)
        n = pl.ds(0, sizes[p])
        return g[core, slot, parts[p]].astype(F32) + c1[slot, parts[p]].astype(F32) + rx1[p, z, b, n].astype(F32)

    for k in order:
        z = zs[k]
        for p in (0, 1):
            n = pl.ds(0, sizes[p])
            arrived(rx1.at[p, z, :, n], s1.at[p, k], r1.at[p, z])
            t2[p, z, n] = partial(p, z, second_give[p]).astype(BF)
            send(t2.at[p, z, n], rx2.at[p, z, n], s2.at[p, k], r2.at[p, z], seconds[p], core)
    for k in order:
        z = zs[k]
        for p in (0, 1):
            n = pl.ds(0, sizes[p])
            arrived(rx2.at[p, z, n], s2.at[p, k], r2.at[p, z])
            total = partial(p, z, second_keep[p]) + rx2[p, z, n].astype(F32)
            if k:
                t3[p, z, n] = total.astype(BF)
                send(t3.at[p, z, n], rx3.at[p, zc, n], s3.at[p, k], r3.at[p, zc], 4 * z + 2 * yc + xc, core)
            else:
                out[parts[p], :] = total
    for k in order[:-1]:
        z = zs[k]
        for p in (0, 1):
            n = pl.ds(0, sizes[p])
            arrived(rx3.at[p, z, n], s3.at[p, k], r3.at[p, z])
            out[parts[p], :] += rx3[p, z, n].astype(F32)
    for copy in pending:
        copy.wait_send()


def scatter_all(g, collective_id):
    dp, rows = g.shape[1], g.shape[2]
    nz = dp // 4
    half = up_to(rows // 2, 16)
    dma = pltpu.SemaphoreType.DMA
    vm = pltpu.VMEM
    return pl.pallas_call(
        functools.partial(scatter_kernel, nz),
        out_shape=jax.ShapeDtypeStruct((rows, LANES), F32),
        in_specs=[pl.BlockSpec(memory_space=pltpu.VMEM)],
        out_specs=pl.BlockSpec(memory_space=pltpu.VMEM),
        scratch_shapes=[
            vm((dp, rows, LANES), BF),
            vm((2, nz, 2, half, LANES), BF),
            vm((2, nz, 2, half, LANES), BF),
            vm((2, nz, half, LANES), BF),
            vm((2, nz, half, LANES), BF),
            vm((2, nz, half, LANES), BF),
            vm((2, nz, half, LANES), BF),
            dma((nz,)), dma((nz,)), dma((2, nz)), dma((2, nz)), dma((2, nz)), dma((2, nz)), dma((2, nz)), dma((2, nz)),
        ],
        compiler_params=pltpu.CompilerParams(
            collective_id=collective_id, has_side_effects=True, vmem_limit_bytes=40 << 20
        ),
        name="scatter_grads",
    )(g)


def share_kernel(dp_count, src, out, ss, rs):
    me = lax.axis_index("dp")
    core = lax.axis_index("head")
    own = 2 * me + core
    total = 2 * dp_count
    barrier = pltpu.get_barrier_semaphore()

    def peer(k):
        other = lax.rem(own + k, total)
        dp = other // 2
        return other, dp, other - 2 * dp

    @pl.loop(1, total)
    def _(k):
        _, dp, head = peer(k)
        pl.semaphore_signal(
            barrier, inc=1, device_id={"dp": dp, "head": head}, device_id_type=pl.DeviceIdType.MESH
        )

    pl.semaphore_wait(barrier, total - 1)
    out[own] = src[...]

    @pl.loop(1, total)
    def _(k):
        _, dp, head = peer(k)
        remote(src, out.at[own], ss.at[k], rs.at[own], dp, head).start()

    @pl.loop(1, total)
    def _(k):
        other, dp, head = peer(k)
        remote(src, out.at[other], ss.at[k], rs.at[other], dp, head).wait()


def share_all(block, dp, collective_id):
    dma = pltpu.SemaphoreType.DMA
    return pl.pallas_call(
        functools.partial(share_kernel, dp),
        out_shape=jax.ShapeDtypeStruct((2 * dp,) + block.shape, block.dtype),
        in_specs=[pl.BlockSpec(memory_space=pltpu.VMEM)],
        out_specs=pl.BlockSpec(memory_space=pltpu.VMEM),
        scratch_shapes=[dma((2 * dp,)), dma((2 * dp,))],
        compiler_params=pltpu.CompilerParams(collective_id=collective_id, has_side_effects=True),
        name="share_sums",
    )(block)


HEADS = 4
HD = 60
FF = 960
KW = 15
STEP = 10
KREL = 383
NORM_EPS = 1e-05
BETA_ONE = 0.9
BETA_TWO = 0.999
LEARN_RATE = 0.1
WEIGHT_DECAY = 0.01
ADAM_EPS = 1e-08
LOG2E = 1.4426950408889634
LN2 = 0.6931471805599453
SCALE = HD ** (-0.5)
UNIT = 1.28125
D = 240
DP = 256
HF = 480
HFP = 512
FFP = 1024
HC = 120
MASK_LANE = 120
NEG = -1e30
FFA, ATT, CNV, FFB, OUT = 0, 2, 4, 6, 8
DOWNB_ONE, DOWNB_TWO, B_OUT, BATCH_GAIN, BATCH_BIAS, TAPS, DEPTH_BIAS = 10, 11, 12, 13, 14, 16, 31
VEC_ROWS = 32
BIG = 60 << 20


def head_places():
    out, at = {}, 0
    for name, size in (
        ("up1", D * HF), ("upb1", HF), ("dn1", HF * D), ("up2", D * HF), ("upb2", HF), ("dn2", HF * D),
        ("wq", D * HC), ("wk", D * HC), ("wv", D * HC), ("bq", HC), ("bv", HC),
        ("rel", 2 * KREL), ("wo", HC * D),
    ):
        out[name] = at
        at += size
    return out, at


def shared_places():
    out, at = {}, 0
    for name, size in (
        ("vec", 13 * D), ("p1", 2 * D * D), ("pb1", 2 * D), ("taps", KW * D), ("db", D),
        ("bg", D), ("bb", D), ("p2", D * D), ("pb2", D),
    ):
        out[name] = at
        at += size
    return out, at


def lane_iota(shape):
    return lax.broadcasted_iota(jnp.int32, shape, len(shape) - 1)


def slot_rows(size):
    return up_to(-(-(size + LANES - 1) // LANES), 16)


def dot(a, b):
    return jnp.dot(a, b, preferred_element_type=F32)


def dot_t(a, b):
    return lax.dot_general(a, b, (((1,), (1,)), ((), ())), preferred_element_type=F32)


def t_dot(a, b):
    return lax.dot_general(a, b, (((0,), (0,)), ((), ())), preferred_element_type=F32)


def vmem_call(body, outs, ins, scratch=(), name=None, limit=BIG):
    return pl.pallas_call(
        body,
        out_shape=outs,
        in_specs=[pl.BlockSpec(memory_space=pltpu.VMEM) for _ in ins],
        out_specs=jax.tree.map(lambda _: pl.BlockSpec(memory_space=pltpu.VMEM), outs),
        scratch_shapes=list(scratch),
        compiler_params=pltpu.CompilerParams(vmem_limit_bytes=limit),
        name=name,
    )(*ins)


def own_offsets(head_size, shared_size):
    me = lax.axis_index("dp")
    core = lax.axis_index("head")
    return lax.rem(me * head_size, LANES), lax.rem((2 * me + core) * shared_size, LANES)


def push_lanes(x, shift):
    rolled = pltpu.roll(x, shift, 1)
    before = jnp.concatenate([jnp.zeros((1, LANES), F32), rolled[:-1]], 0)
    return jnp.where(lane_iota(x.shape) >= shift, rolled, before)


def pull_lanes(x, shift):
    rolled = pltpu.roll(x, lax.rem(LANES - shift, LANES), 1)
    after = jnp.concatenate([rolled[1:], jnp.zeros((1, LANES), F32)], 0)
    return jnp.where(lane_iota(x.shape) < LANES - shift, rolled, after)


def align_kernel(head_ref, shared_ref, out):
    head_size, shared_size = head_ref.shape[1], shared_ref.shape[0]
    hr, sr = slot_rows(head_size), slot_rows(shared_size)
    ho, so = own_offsets(head_size, shared_size)
    x = jnp.concatenate([head_ref[...], jnp.zeros((1, hr * LANES - head_size), F32)], 1)
    out[pl.ds(0, hr), :] = push_lanes(x.reshape(hr, LANES), ho).astype(BF)
    x = shared_ref[...].reshape(1, shared_size)
    x = jnp.concatenate([x, jnp.zeros((1, sr * LANES - shared_size), F32)], 1)
    out[pl.ds(hr, sr), :] = push_lanes(x.reshape(sr, LANES), so).astype(BF)


def adam_kernel(g_ref, hp, hf, hs, sp, sf, ss, hf_o, hs_o, hp_o, hc_o, sf_o, ss_o, sp_o, sc_o):
    head_size, shared_size = hp.shape[1], sp.shape[0]
    hr, sr = slot_rows(head_size), slot_rows(shared_size)
    ho, so = own_offsets(head_size, shared_size)

    def update(master, g, first, second):
        first_new = BETA_ONE * first + (1.0 - BETA_ONE) * g
        second_new = BETA_TWO * second + (1.0 - BETA_TWO) * g * g
        first_hat = first_new * (1.0 / (1.0 - BETA_ONE**STEP))
        second_hat = second_new * (1.0 / (1.0 - BETA_TWO**STEP))
        new = master - LEARN_RATE * (first_hat / (jnp.sqrt(second_hat) + ADAM_EPS) + WEIGHT_DECAY * master)
        return first_new, second_new, new

    g = pull_lanes(g_ref[pl.ds(0, hr), :], ho).reshape(1, hr * LANES)[:, :head_size]
    one, two, new = update(hp[...], g, hf[...], hs[...])
    hf_o[...] = one
    hs_o[...] = two
    hp_o[...] = new
    hc_o[...] = new.astype(BF)
    g = pull_lanes(g_ref[pl.ds(hr, sr), :], so).reshape(sr * LANES)[:shared_size]
    one, two, new = update(sp[...], g, sf[...], ss[...])
    sf_o[...] = one
    ss_o[...] = two
    sp_o[...] = new
    sc_o[...] = new.astype(BF)


def row_phases(rows, pitch):
    if rows == 1:
        return 1, 1, 0
    period = LANES // math.gcd(pitch, LANES)
    return period, rows // period, period * pitch // LANES


def take(flat, at, rows, pitch, col, width, dst, row0, lane0):
    period, count, stride = row_phases(rows, pitch)
    lane = lane_iota((count, LANES))
    for j in range(period):
        start = at + j * pitch + col
        q, l = divmod(start, LANES)

        def load(t):
            if count == 1:
                return flat[pl.ds(q + t, 1), :]
            return flat[pl.ds(q + t, count, stride), :]

        pieces = [load(t) for t in range(-(-(l + width) // LANES))]
        if l:
            pieces = [pltpu.roll(x, LANES - l, 1) for x in pieces]
        for t in range(-(-width // LANES)):
            value = pieces[t]
            if l and t + 1 < len(pieces):
                value = jnp.where(lane < LANES - l, value, pieces[t + 1])
            left = width - t * LANES
            if left < LANES:
                value = jnp.where(lane < left, value, 0.0)
            rows_at = pl.ds(row0 + j, 1) if count == 1 else pl.ds(row0 + j, count, period)
            dst[lane0 // LANES + t, rows_at, :] = value


def give(flat, at, rows, pitch, col, width, src, row0, lane0):
    period, count, stride = row_phases(rows, pitch)
    lane = lane_iota((count, LANES))
    for j in range(period):
        start = at + j * pitch + col
        q, l = divmod(start, LANES)
        rows_at = pl.ds(row0 + j, 1) if count == 1 else pl.ds(row0 + j, count, period)
        pieces = [src[lane0 // LANES + t, rows_at, :] for t in range(-(-width // LANES))]
        if l:
            pieces = [pltpu.roll(x, l, 1) for x in pieces]
        total = -(-(l + width) // LANES)
        for t in range(total):
            here = pl.ds(q + t, 1) if count == 1 else pl.ds(q + t, count, stride)
            if not l:
                value = pieces[t]
            elif t == 0:
                value = pieces[0]
            elif t == len(pieces):
                value = pieces[t - 1]
            else:
                value = jnp.where(lane >= l, pieces[t], pieces[t - 1])
            lo = l if t == 0 else 0
            hi = min(LANES, l + width - t * LANES)
            if lo or hi < LANES:
                keep = (lane >= lo) & (lane < hi)
                value = jnp.where(keep, value, flat[here, :])
            flat[here, :] = value


def spill(tiles, rows, dst, factor=None):
    for t in range(dst.shape[1] // LANES):
        value = tiles[t, pl.ds(0, rows), :]
        if factor:
            value = factor * value
        dst[:, pl.ds(t * LANES, LANES)] = value.astype(dst.dtype)


def load_tiles(src, tiles):
    for t in range(src.shape[1] // LANES):
        tiles[t, pl.ds(0, src.shape[0]), :] = src[:, pl.ds(t * LANES, LANES)]


def flat_rows(total, size):
    return up_to(total // LANES + slot_rows(size) + 16, 16)


def weights_kernel(sizes, got, up1, dn1, up2, dn2, qkv, wo, p1, p2, vec, rel, fh, fs, wide, tall, tmp):
    dp, head_size, shared_size = sizes
    hr, sr = slot_rows(head_size), slot_rows(shared_size)
    hp, _ = head_places()
    sp, _ = shared_places()
    row8 = lax.broadcasted_iota(jnp.int32, (8, LANES), 0)

    def merge(flat, first_row, block):
        head = flat[pl.ds(first_row, 8), :]
        flat[pl.ds(first_row, 8), :] = block[:8] + jnp.where(row8 == 0, head, 0.0)
        flat[pl.ds(first_row + 8, block.shape[0] - 8), :] = block[8:]

    for g in range(2):
        fh[g, pl.ds(0, 8), :] = jnp.zeros((8, LANES), F32)
    fs[pl.ds(0, 8), :] = jnp.zeros((8, LANES), F32)

    @pl.loop(0, dp)
    def _(i):
        for g in range(2):
            merge(fh.at[g], (i * head_size) // LANES, got[i, g, pl.ds(0, hr), :].astype(F32))
        for g in range(2):
            merge(fs, ((2 * i + g) * shared_size) // LANES, got[i, g, pl.ds(hr, sr), :].astype(F32))

    lane = lane_iota((1, LANES))

    def clear(tiles, count, row, size):
        for t in range(count):
            tiles[t, pl.ds(row, size), :] = jnp.zeros((size, LANES), F32)

    def patch(tiles, tile, row, where, value):
        part = tiles[tile, pl.ds(row, 1), :]
        tiles[tile, pl.ds(row, 1), :] = jnp.where(where, value, part)

    for dst_ref, place, bplace in ((up1, "up1", "upb1"), (up2, "up2", "upb2")):
        clear(wide, 8, 240, 16)
        for g in range(2):
            take(fh.at[g], hp[place], D, HF, 0, HF, wide, 0, g * HFP)
            take(fh.at[g], hp[bplace], 1, HF, 0, HF, wide, 240, g * HFP)
        patch(wide, 3, 240, lane == HF - 3 * LANES, UNIT)
        spill(wide, DP, dst_ref)
    for dst_ref, place, brow in ((dn1, "dn1", DOWNB_ONE), (dn2, "dn2", DOWNB_TWO)):
        for g in range(2):
            clear(tall, 2, g * HFP + HF, 32)
            take(fh.at[g], hp[place], HF, D, 0, D, tall, g * HFP, 0)
        take(fs, sp["vec"] + brow * D, 1, D, 0, D, tall, HF, 0)
        spill(tall, FFP, dst_ref, 0.5)
    clear(wide, 6, 240, 16)
    for g in range(2):
        for which, (place, bplace) in enumerate((("wq", "bq"), ("wk", None), ("wv", "bv"))):
            lane0 = which * DP + g * LANES
            take(fh.at[g], hp[place], D, HC, 0, HC, wide, 0, lane0)
            if bplace:
                take(fh.at[g], hp[bplace], 1, HC, 0, HC, wide, 240, lane0)
    patch(wide, 0, 240, lane == MASK_LANE, 1.0)
    patch(wide, 4, 240, (lane >= MASK_LANE) & (lane < MASK_LANE + 3), 1.0)
    spill(wide, DP, qkv)
    clear(tall, 2, 0, DP)
    for g in range(2):
        take(fh.at[g], hp["wo"], HC, D, 0, D, tall, g * LANES, 0)
    take(fs, sp["vec"] + B_OUT * D, 1, D, 0, D, tall, MASK_LANE, 0)
    spill(tall, DP, wo)
    clear(wide, 4, 240, 16)
    for half in range(2):
        take(fs, sp["p1"], D, 2 * D, half * D, D, wide, 0, half * DP)
        take(fs, sp["pb1"] + half * D, 1, D, 0, D, wide, 240, half * DP)
    spill(wide, DP, p1)
    clear(tall, 2, 240, 16)
    take(fs, sp["p2"], D, D, 0, D, tall, 0, 0)
    take(fs, sp["pb2"], 1, D, 0, D, tall, 240, 0)
    spill(tall, DP, p2)
    take(fs, sp["vec"], 16, D, 0, D, tall, 0, 0)
    take(fs, sp["taps"], 16, D, 0, D, tall, TAPS, 0)
    take(fs, sp["bg"], 1, D, 0, D, tall, BATCH_GAIN, 0)
    take(fs, sp["bb"], 1, D, 0, D, tall, BATCH_BIAS, 0)
    for row, value in ((FFA + 1, 1.0), (ATT + 1, 1.0), (CNV + 1, 1.0), (FFB + 1, 1.0), (BATCH_BIAS, UNIT)):
        patch(tall, 1, row, lane == D - LANES, value)
    spill(tall, VEC_ROWS, vec)
    length = rel.shape[1]
    for n in range(HEADS):
        take(fh.at[n // 2], hp["rel"] + (n % 2) * KREL, 1, KREL, 0, KREL, tmp, 0, 0)
        row = jnp.concatenate([tmp[t, pl.ds(0, 1), :] for t in range(3)] + [jnp.zeros((1, LANES), F32)], 1)
        rows = jnp.broadcast_to(row, (length, 4 * LANES))
        rows = pltpu.roll(rows, 4 * LANES - (length - 1), 1, stride=1, stride_axis=0)
        rel[n] = rows[:, :length] * LOG2E


def make_weights(got, head_size, shared_size, length):
    dp = got.shape[0]

    def s(*shape, dtype=BF):
        return jax.ShapeDtypeStruct(shape, dtype)

    outs = (
        s(DP, FFP), s(FFP, DP), s(DP, FFP), s(FFP, DP), s(DP, 3 * DP), s(DP, DP), s(DP, 2 * DP), s(DP, DP),
        s(VEC_ROWS, DP, dtype=F32), s(HEADS, length, length, dtype=F32),
    )
    vm = pltpu.VMEM
    scratch = (
        vm((2, flat_rows(head_size * dp, head_size), LANES), F32),
        vm((flat_rows(shared_size * 2 * dp, shared_size), LANES), F32),
        vm((8, DP, LANES), F32),
        vm((2, FFP, LANES), F32),
        vm((4, 8, LANES), F32),
    )
    return vmem_call(
        functools.partial(weights_kernel, (dp, head_size, shared_size)), outs, (got,), scratch, "make_weights"
    )


def flatten_kernel(sizes, up1, dn1, up2, dn2, qkv, wo, p1, p2, vec, rel, out, fh, fs, wide, tall, tmp):
    dp, head_size, shared_size = sizes
    hr, sr = slot_rows(head_size), slot_rows(shared_size)
    hp, used_h = head_places()
    sp, used_s = shared_places()
    for g in range(2):
        first = used_h // LANES // 8 * 8
        fh[g, pl.ds(first, fh.shape[1] - first), :] = jnp.zeros((fh.shape[1] - first, LANES), F32)
    first = used_s // LANES // 8 * 8
    fs[pl.ds(first, fs.shape[0] - first), :] = jnp.zeros((fs.shape[0] - first, LANES), F32)
    for src, place, bplace in ((up1, "up1", "upb1"), (up2, "up2", "upb2")):
        load_tiles(src, wide)
        for g in range(2):
            give(fh.at[g], hp[place], D, HF, 0, HF, wide, 0, g * HFP)
            give(fh.at[g], hp[bplace], 1, HF, 0, HF, wide, 240, g * HFP)
    for src, place, brow in ((dn1, "dn1", DOWNB_ONE), (dn2, "dn2", DOWNB_TWO)):
        for t in range(2):
            tall[t] = 0.5 * src[pl.ds(t * LANES, LANES), :].T
        for g in range(2):
            give(fh.at[g], hp[place], HF, D, 0, D, tall, g * HFP, 0)
        give(fs, sp["vec"] + brow * D, 1, D, 0, D, tall, HF, 0)
    load_tiles(qkv, wide)
    load_tiles(wo, tall)
    for g in range(2):
        for which, (place, bplace) in enumerate((("wq", "bq"), ("wk", None), ("wv", "bv"))):
            lane0 = which * DP + g * LANES
            give(fh.at[g], hp[place], D, HC, 0, HC, wide, 0, lane0)
            if bplace:
                give(fh.at[g], hp[bplace], 1, HC, 0, HC, wide, 240, lane0)
        give(fh.at[g], hp["wo"], HC, D, 0, D, tall, g * LANES, 0)
    give(fs, sp["vec"] + B_OUT * D, 1, D, 0, D, tall, MASK_LANE, 0)
    load_tiles(p1, wide)
    load_tiles(p2, tall)
    for half in range(2):
        give(fs, sp["p1"], D, 2 * D, half * D, D, wide, 0, half * DP)
        give(fs, sp["pb1"] + half * D, 1, D, 0, D, wide, 240, half * DP)
    give(fs, sp["p2"], D, D, 0, D, tall, 0, 0)
    give(fs, sp["pb2"], 1, D, 0, D, tall, 240, 0)
    load_tiles(vec, tall)
    for row in range(10):
        give(fs, sp["vec"] + row * D, 1, D, 0, D, tall, row, 0)
    give(fs, sp["taps"], 16, D, 0, D, tall, TAPS, 0)
    give(fs, sp["bg"], 1, D, 0, D, tall, BATCH_GAIN, 0)
    give(fs, sp["bb"], 1, D, 0, D, tall, BATCH_BIAS, 0)
    length = rel.shape[0] // HEADS
    for n in range(HEADS):
        total = jnp.zeros((8, 4 * LANES), F32)
        for block in range(length // 8):
            rows = rel[pl.ds(n * length + 8 * block, 8), :]
            rows = jnp.concatenate([rows, jnp.zeros((8, 4 * LANES - length), F32)], 1)
            total = total + pltpu.roll(rows, length - 8 - 8 * block, 1)
        row = total[7:8]
        for i in range(7):
            row = row + pltpu.roll(total[i : i + 1], 7 - i, 1)
        for t in range(4):
            tmp[t, pl.ds(0, 1), :] = row[:, t * LANES : (t + 1) * LANES]
        give(fh.at[n // 2], hp["rel"] + (n % 2) * KREL, 1, KREL, 0, KREL, tmp, 0, 0)

    @pl.loop(0, dp)
    def _(i):
        for g in range(2):
            out[g, i, pl.ds(0, hr), :] = fh[g, pl.ds((i * head_size) // LANES, hr), :].astype(BF)
            out[g, i, pl.ds(hr, sr), :] = fs[pl.ds(((2 * i + g) * shared_size) // LANES, sr), :].astype(BF)


def flatten_grads(grads, dp, head_size, shared_size):
    rows = slot_rows(head_size) + slot_rows(shared_size)
    vm = pltpu.VMEM
    scratch = (
        vm((2, flat_rows(head_size * dp, head_size), LANES), F32),
        vm((flat_rows(shared_size * 2 * dp, shared_size), LANES), F32),
        vm((8, DP, LANES), F32),
        vm((2, FFP, LANES), F32),
        vm((4, 8, LANES), F32),
    )
    return vmem_call(
        functools.partial(flatten_kernel, (dp, head_size, shared_size)),
        jax.ShapeDtypeStruct((2, dp, rows, LANES), BF),
        grads,
        scratch,
        "flatten_grads",
    )


def lane_mask():
    return jnp.where(lane_iota((1, DP)) < D, 1.0, 0.0)


def sigmoid(x):
    return 0.5 * jnp.tanh(0.5 * x) + 0.5


def row_sum(x):
    return jnp.sum(x, -1, keepdims=True)


def norm(x, gain, bias):
    centre = (x - row_sum(x) * (1.0 / D)) * lane_mask()
    inv = lax.rsqrt(row_sum(centre * centre) * (1.0 / D) + NORM_EPS)
    scaled = centre * inv
    return scaled * gain + bias, scaled, inv


def keep_norm(scaled, inv):
    return jnp.where(lane_iota(scaled.shape) == DP - 1, inv, scaled)


def norm_grad(grad, kept, gain):
    dg = grad * gain
    inv = kept[:, DP - 1 :]
    first = row_sum(dg) * (1.0 / D)
    second = row_sum(dg * kept) * (1.0 / D)
    return inv * (dg - first - kept * second) * lane_mask()


def add_rows(ref, row, value):
    ref[pl.ds(row, 1), :] += jnp.sum(value, 0, keepdims=True)


def norm_param_grads(ref, row, grad, kept):
    add_rows(ref, row, grad * kept)
    add_rows(ref, row + 1, grad)


def silu_pair(u):
    s = sigmoid(u)
    h = u * s
    return h, s + h * (1.0 - s)


def widen(x):
    rows = x.shape[0]
    return jnp.concatenate([x.astype(F32), jnp.zeros((rows, DP - D), F32)], 1)


def head_masks():
    lane = lane_iota((1, DP))
    out = []
    for n in range(HEADS):
        first = (n // 2) * LANES + (n % 2) * HD
        out.append((lane >= first) & (lane < first + HD))
    return out


def valid_rows(lengths, at, length):
    return lax.broadcasted_iota(jnp.int32, (length, 1), 0) < lengths[at]


def phase_a_kernel(
    seqs, lengths, frames, up, dn, wqkv, wo, p1, vec, rel,
    kept1_o, a1_o, h_o, sp_o, kept2_o, a2_o, qkv_o, e_o, rl_o, m_o,
    x2_o, kept3_o, a3_o, f1_o, f2_o, gl_o, w_o, stats_o,
    pad,
):
    step = pl.program_id(0)
    length = frames.shape[1]
    tokens = seqs * length
    first_seq = lax.axis_index("head") * (seqs * pl.num_programs(0)) + step * seqs

    def v(row):
        return vec[pl.ds(row, 1), :]

    x0 = widen(frames[...].reshape(tokens, D))
    a, scaled, inv = norm(x0, v(FFA), v(FFA + 1))
    a = a.astype(BF)
    a1_o[...] = a
    kept1_o[...] = keep_norm(scaled, inv)
    h, slope = silu_pair(dot(a, up[...]))
    h = h.astype(BF)
    h_o[...] = h
    sp_o[...] = slope.astype(BF)
    x1 = x0 + dot(h, dn[...])
    a, scaled, inv = norm(x1, v(ATT), v(ATT + 1))
    a = a.astype(BF)
    a2_o[...] = a
    kept2_o[...] = keep_norm(scaled, inv)
    qkv = dot(a, wqkv[...])
    lane = lane_iota((1, DP))
    masks = head_masks()
    for b in range(seqs):
        rows = pl.ds(b * length, length)
        valid = valid_rows(lengths, first_seq + b, length)
        part = qkv[b * length : (b + 1) * length]
        q = (part[:, :DP] * (SCALE * LOG2E)).astype(BF)
        k = part[:, DP : 2 * DP]
        k = jnp.where(lane == MASK_LANE, jnp.where(valid, 0.0, NEG), k).astype(BF)
        vv = part[:, 2 * DP :].astype(BF)
        qkv_o[rows, pl.ds(0, DP)] = q
        qkv_o[rows, pl.ds(DP, DP)] = k
        qkv_o[rows, pl.ds(2 * DP, DP)] = vv
        zero = jnp.zeros_like(q)
        mixed = jnp.zeros((length, DP), F32)
        shares = jnp.zeros((length, DP), F32)
        for n in range(HEADS):
            qm = jnp.where(masks[n] | (lane == MASK_LANE), q, zero)
            s = dot_t(qm, k) + rel[n]
            e = jnp.exp2(s - jnp.max(s, -1, keepdims=True)).astype(BF)
            e_o[b, pl.ds(n * length, length), :] = e
            o = dot(e, vv)
            r = 1.0 / o[:, MASK_LANE : MASK_LANE + 1]
            here = masks[n] | (lane == MASK_LANE) if n == 0 else masks[n]
            shares = jnp.where(here, r, shares)
            mixed = jnp.where(here, o, mixed)
        rl_o[rows, :] = shares
        m_o[rows, :] = (mixed * shares).astype(BF)
    x2 = x1 + dot(m_o[...], wo[...])
    x2_o[...] = x2
    a, scaled, inv = norm(x2, v(CNV), v(CNV + 1))
    a = a.astype(BF)
    a3_o[...] = a
    kept3_o[...] = keep_norm(scaled, inv)
    e = dot(a, p1[...])
    half = KW // 2

    @pl.when(step == 0)
    def _():
        pad[...] = jnp.zeros(pad.shape, F32)
        stats_o[...] = jnp.zeros(stats_o.shape, F32)

    count = jnp.float32(0.0)
    total = jnp.zeros((1, DP), F32)
    for b in range(seqs):
        rows = pl.ds(b * length, length)
        valid = jnp.where(valid_rows(lengths, first_seq + b, length), 1.0, 0.0)
        linear = e[b * length : (b + 1) * length, :DP]
        gate = sigmoid(e[b * length : (b + 1) * length, DP:])
        f1 = gate * valid
        gl = linear * f1
        f1_o[rows, :] = f1.astype(BF)
        f2_o[rows, :] = (gl * (1.0 - gate)).astype(BF)
        gl_o[rows, :] = gl.astype(BF)
        for t in range(2):
            cols = pl.ds(t * LANES, LANES)
            pad[b, t, pl.ds(8, length), :] = gl[:, t * LANES : (t + 1) * LANES]
            acc = jnp.broadcast_to(vec[pl.ds(DEPTH_BIAS, 1), cols], (length, LANES))
            for r in range(KW):
                acc = acc + pad[b, t, pl.ds(8 - half + r, length), :] * vec[pl.ds(TAPS + r, 1), cols]
            w_o[rows, cols] = acc
        total = total + jnp.sum(w_o[rows, :] * valid, 0, keepdims=True)
        count = count + lengths[first_seq + b].astype(F32)
    mean = total / count
    square = jnp.zeros((1, DP), F32)
    for b in range(seqs):
        valid = jnp.where(valid_rows(lengths, first_seq + b, length), 1.0, 0.0)
        centre = (w_o[pl.ds(b * length, length), :] - mean) * valid
        square = square + jnp.sum(centre * centre, 0, keepdims=True)
    old = stats_o[pl.ds(4, 1), :]
    new = old + count
    for t in range(2):
        cols = slice(t * LANES, (t + 1) * LANES)
        before = stats_o[pl.ds(t, 1), :]
        delta = mean[:, cols] - before
        stats_o[pl.ds(t, 1), :] = before + delta * (count / new)
        stats_o[pl.ds(2 + t, 1), :] += square[:, cols] + delta * delta * (old * count / new)
    stats_o[pl.ds(4, 1), :] = new


def batch_stats(shared, keep):
    counts = shared[:, 4:5, :]
    total = jnp.sum(counts, 0)
    means, spreads = [], []
    for t in range(2):
        each = shared[:, t : t + 1, :]
        mean = jnp.sum(each * counts, 0) / total
        spread = (jnp.sum(shared[:, 2 + t : 3 + t, :], 0) + jnp.sum(counts * (each - mean) ** 2, 0)) / total
        means.append(mean)
        spreads.append(spread)
    keep[pl.ds(0, 1), :] = jnp.concatenate(means, 1)
    keep[pl.ds(1, 1), :] = lax.rsqrt(jnp.concatenate(spreads, 1) + NORM_EPS)
    keep[pl.ds(2, 1), :] = jnp.concatenate([total, total], 1)


def phase_b_kernel(
    seqs, shared, w, x2, cotangent, p2, up, dn, vec,
    out_o, dy_o, dx3_o, dup_o, ddn_o, dp2_o, vec_o, sums_o,
    keep,
):
    step = pl.program_id(0)
    length = cotangent.shape[1]
    tokens = seqs * length

    @pl.when(step == 0)
    def _():
        batch_stats(shared[...], keep)
        for ref in (dup_o, ddn_o, dp2_o, vec_o, sums_o):
            ref[...] = jnp.zeros(ref.shape, F32)

    def v(row):
        return vec[pl.ds(row, 1), :]

    z = (w[...] - keep[pl.ds(0, 1), :]) * keep[pl.ds(1, 1), :]
    hc, slope_c = silu_pair(z * v(BATCH_GAIN) + v(BATCH_BIAS))
    hc = hc.astype(BF)
    x3 = x2[...] + dot(hc, p2[...])
    a, scaled, inv = norm(x3, v(FFB), v(FFB + 1))
    a = a.astype(BF)
    kept = keep_norm(scaled, inv)
    h, slope = silu_pair(dot(a, up[...]))
    h = h.astype(BF)
    slope = slope.astype(BF)
    x4 = x3 + dot(h, dn[...])
    final, scaled, inv = norm(x4, v(OUT), v(OUT + 1))
    out_o[...] = final[:, :D].astype(BF).reshape(seqs, length, D)
    g = widen(cotangent[...].reshape(tokens, D))
    kept4 = keep_norm(scaled, inv)
    norm_param_grads(vec_o, OUT, g, kept4)
    dx4 = norm_grad(g, kept4, v(OUT))
    do = dx4.astype(BF)
    ddn_o[...] += t_dot(do, h)
    du = (dot_t(do, dn[...]) * slope.astype(F32)).astype(BF)
    dup_o[...] += t_dot(a, du)
    da = dot_t(du, up[...])
    norm_param_grads(vec_o, FFB, da, kept)
    dx3 = dx4 + norm_grad(da, kept, v(FFB))
    dx3_o[...] = dx3
    dc = dx3.astype(BF)
    dp2_o[...] += t_dot(hc, dc)
    dy = dot_t(dc, p2[...]) * slope_c
    dy_o[...] = dy
    first = jnp.sum(dy, 0, keepdims=True)
    second = jnp.sum(dy * z, 0, keepdims=True)
    vec_o[pl.ds(BATCH_BIAS, 1), :] += first
    vec_o[pl.ds(BATCH_GAIN, 1), :] += second
    for t in range(2):
        cols = slice(t * LANES, (t + 1) * LANES)
        sums_o[pl.ds(t, 1), :] += first[:, cols]
        sums_o[pl.ds(2 + t, 1), :] += second[:, cols]


def phase_c_kernel(
    seqs, lengths, shared, shared_b, w, dy, dx3, gl, f1, f2, a3, kept3, qkv, e_all, rl, m, a2, kept2, h, slope, a1, kept1,
    p1, wo, wqkv, dn, up, vec,
    dx0_o, dp1_o, dwo_o, dqkv_o, dup_o, ddn_o, vec_o, rel_o,
    keep, padw, padg, grads,
):
    step = pl.program_id(0)
    length = dx0_o.shape[1]
    tokens = seqs * length
    first_seq = lax.axis_index("head") * (seqs * pl.num_programs(0)) + step * seqs
    half = KW // 2

    def v(row):
        return vec[pl.ds(row, 1), :]

    @pl.when(step == 0)
    def _():
        batch_stats(shared[...], keep)
        sums = jnp.sum(shared_b[...], 0)
        keep[pl.ds(3, 1), :] = jnp.concatenate([sums[0:1], sums[1:2]], 1)
        keep[pl.ds(4, 1), :] = jnp.concatenate([sums[2:3], sums[3:4]], 1)
        for ref in (dp1_o, dwo_o, dqkv_o, dup_o, ddn_o, vec_o, rel_o, padw, padg):
            ref[...] = jnp.zeros(ref.shape, F32)

    gain = v(BATCH_GAIN)
    inv_batch = keep[pl.ds(1, 1), :]
    mean = keep[pl.ds(0, 1), :]
    plain = gain * keep[pl.ds(3, 1), :] / keep[pl.ds(2, 1), :]
    cross = gain * keep[pl.ds(4, 1), :] / keep[pl.ds(2, 1), :]
    for b in range(seqs):
        rows = pl.ds(b * length, length)
        valid = jnp.where(valid_rows(lengths, first_seq + b, length), 1.0, 0.0)
        z = (w[rows, :] - mean) * inv_batch
        dw = inv_batch * (dy[rows, :] * gain - valid * (plain + z * cross))
        add_rows(vec_o, DEPTH_BIAS, dw)
        for t in range(2):
            cols = pl.ds(t * LANES, LANES)
            here = dw[:, t * LANES : (t + 1) * LANES]
            padw[b, t, pl.ds(8, length), :] = here
            padg[b, t, pl.ds(8, length), :] = gl[rows, cols].astype(F32)
            acc = jnp.zeros((length, LANES), F32)
            for r in range(KW):
                acc = acc + padw[b, t, pl.ds(8 + half - r, length), :] * vec[pl.ds(TAPS + r, 1), cols]
                tap = here * padg[b, t, pl.ds(8 - half + r, length), :]
                vec_o[pl.ds(TAPS + r, 1), cols] += jnp.sum(tap, 0, keepdims=True)
            grads[rows, cols] = (acc * f1[rows, cols].astype(F32)).astype(BF)
            grads[rows, pl.ds(DP + t * LANES, LANES)] = (acc * f2[rows, cols].astype(F32)).astype(BF)
    de = grads[:, pl.ds(0, 2 * DP)]
    dp1_o[...] += t_dot(a3[...], de)
    da = dot_t(de, p1[...])
    norm_param_grads(vec_o, CNV, da, kept3[...])
    dx2 = dx3[...] + norm_grad(da, kept3[...], v(CNV))
    db = dx2.astype(BF)
    dwo_o[...] += t_dot(m[...], db)
    dm = dot_t(db, wo[...])
    lane = lane_iota((1, DP))
    masks = head_masks()
    wide_rows = lax.broadcasted_iota(jnp.int32, (DP, LANES), 0)
    wide_lane = lane_iota((DP, LANES))
    for b in range(seqs):
        rows = pl.ds(b * length, length)
        q = qkv[rows, pl.ds(0, DP)]
        k = qkv[rows, pl.ds(DP, DP)]
        vv = qkv[rows, pl.ds(2 * DP, DP)]
        dmb = (dm[b * length : (b + 1) * length] * rl[rows, :]).astype(BF)
        product = (dmb.astype(F32) * m[rows, :].astype(F32)).astype(BF)
        zero = jnp.zeros_like(q)
        dq = jnp.zeros((length, DP), F32)
        dk = jnp.zeros((length, DP), F32)
        dv = jnp.zeros((length, DP), F32)
        for n in range(HEADS):
            first = (n // 2) * LANES + (n % 2) * HD
            pick = (wide_rows >= first) & (wide_rows < first + HD) & (wide_lane > MASK_LANE) & (wide_lane < MASK_LANE + 3)
            level = dot(product, jnp.where(pick, -1.0, 0.0).astype(BF))
            high = level.astype(BF)
            low = (level - high.astype(F32)).astype(BF)
            side = jnp.where(lane_iota((1, LANES)) == MASK_LANE + 1, high, low)
            dmm = jnp.where(masks[n], dmb, zero)
            dmm = jnp.concatenate(
                [jnp.where(lane_iota((1, LANES)) > MASK_LANE, side, dmm[:, :LANES]), dmm[:, LANES:]], 1
            )
            e = e_all[b, pl.ds(n * length, length), :]
            ds = (e.astype(F32) * dot_t(dmm, vv)).astype(BF)
            rel_o[pl.ds(n * length, length), :] += ds.astype(F32)
            dq = jnp.where(masks[n], dot(ds, k), dq)
            dk = dk + t_dot(ds, jnp.where(masks[n], q, zero))
            dv = dv + t_dot(e, dmm)
        grads[rows, pl.ds(0, DP)] = (dq * SCALE).astype(BF)
        grads[rows, pl.ds(DP, DP)] = (dk * LN2).astype(BF)
        grads[rows, pl.ds(2 * DP, DP)] = dv.astype(BF)
    dqkv = grads[...]
    dqkv_o[...] += t_dot(a2[...], dqkv)
    da = dot_t(dqkv, wqkv[...])
    norm_param_grads(vec_o, ATT, da, kept2[...])
    dx1 = dx2 + norm_grad(da, kept2[...], v(ATT))
    do = dx1.astype(BF)
    ddn_o[...] += t_dot(do, h[...])
    du = (dot_t(do, dn[...]) * slope[...].astype(F32)).astype(BF)
    dup_o[...] += t_dot(a1[...], du)
    da = dot_t(du, up[...])
    norm_param_grads(vec_o, FFA, da, kept1[...])
    dx0 = dx1 + norm_grad(da, kept1[...], v(FFA))
    dx0_o[...] = dx0[:, :D].reshape(seqs, length, D)


def layer_call(body, steps, ins, outs, scratch, name):
    def spec(item):
        kind, shape = item
        if kind == "smem":
            return pl.BlockSpec(memory_space=pltpu.SMEM)
        if kind == "tile":
            return pl.BlockSpec(shape, lambda i: (i,) + (0,) * (len(shape) - 1))
        return pl.BlockSpec(shape, lambda i: (0,) * len(shape))

    arrays = [a for _, _, a in ins]
    return pl.pallas_call(
        body,
        grid=(steps,),
        out_shape=tuple(jax.ShapeDtypeStruct(full, dtype) for _, _, full, dtype in outs),
        in_specs=[spec((kind, block)) for kind, block, _ in ins],
        out_specs=tuple(spec((kind, block)) for kind, block, _, _ in outs),
        scratch_shapes=list(scratch),
        compiler_params=pltpu.CompilerParams(vmem_limit_bytes=BIG, dimension_semantics=("arbitrary",)),
        name=name,
    )(*arrays)


def tile_in(array, steps):
    return ("tile", (array.shape[0] // steps,) + array.shape[1:], array)


def whole_in(array):
    return ("whole", array.shape, array)


def tile_out(steps, shape, dtype):
    return ("tile", (shape[0] // steps,) + shape[1:], shape, dtype)


def whole_out(shape):
    return ("whole", shape, shape, F32)


SEQS_A = 2
SEQS_B = 4
SEQS_C = 2


def per_device(
    frames, cotangent, lengths, head_params, shared_params, head_first, head_second, shared_first, shared_second
):
    seq_here, length, _ = frames.shape
    tokens = seq_here * length
    dp = lax.axis_size("dp")
    head_size, shared_size = head_params.shape[1], shared_params.shape[0]
    rows = slot_rows(head_size) + slot_rows(shared_size)
    vm = pltpu.VMEM
    mine = vmem_call(
        align_kernel, jax.ShapeDtypeStruct((rows, LANES), BF), (head_params, shared_params), name="align"
    )
    got = gather_all(mine, dp, 1)
    up1, dn1, up2, dn2, wqkv, wo, p1, p2, vec, rel = make_weights(got, head_size, shared_size, length)

    steps = seq_here // SEQS_A
    t = functools.partial(tile_out, steps)
    (
        kept1, a1, h1, slope1, kept2, a2, qkv, e_all, rl, m, x2, kept3, a3, f1, f2, gl, w, stats
    ) = layer_call(
        functools.partial(phase_a_kernel, SEQS_A),
        steps,
        [("smem", None, lengths), tile_in(frames, steps)] + [whole_in(x) for x in (up1, dn1, wqkv, wo, p1, vec, rel)],
        [
            t((tokens, DP), F32), t((tokens, DP), BF), t((tokens, FFP), BF), t((tokens, FFP), BF),
            t((tokens, DP), F32), t((tokens, DP), BF), t((tokens, 3 * DP), BF),
            t((seq_here, HEADS * length, length), BF), t((tokens, DP), F32), t((tokens, DP), BF),
            t((tokens, DP), F32), t((tokens, DP), F32), t((tokens, DP), BF), t((tokens, DP), BF),
            t((tokens, DP), BF), t((tokens, DP), BF), t((tokens, DP), F32), whole_out((8, LANES)),
        ],
        [vm((SEQS_A, 2, length + 16, LANES), F32)],
        "phase_a",
    )
    shared_a = share_all(stats, dp, 2)
    steps = seq_here // SEQS_B
    t = functools.partial(tile_out, steps)
    layer_out, dy, dx3, dup2, ddn2, dp2, vec_b, sums = layer_call(
        functools.partial(phase_b_kernel, SEQS_B),
        steps,
        [whole_in(shared_a), tile_in(w, steps), tile_in(x2, steps), tile_in(cotangent, steps)]
        + [whole_in(x) for x in (p2, up2, dn2, vec)],
        [
            t((seq_here, length, D), BF), t((tokens, DP), F32), t((tokens, DP), F32),
            whole_out((DP, FFP)), whole_out((DP, FFP)), whole_out((DP, DP)), whole_out((VEC_ROWS, DP)),
            whole_out((8, LANES)),
        ],
        [vm((8, DP), F32)],
        "phase_b",
    )
    shared_b = share_all(sums, dp, 3)
    steps = seq_here // SEQS_C
    t = functools.partial(tile_out, steps)
    input_grad, dp1, dwo, dqkv, dup1, ddn1, vec_c, rel_sum = layer_call(
        functools.partial(phase_c_kernel, SEQS_C),
        steps,
        [("smem", None, lengths), whole_in(shared_a), whole_in(shared_b)]
        + [
            tile_in(x, steps)
            for x in (w, dy, dx3, gl, f1, f2, a3, kept3, qkv, e_all, rl, m, a2, kept2, h1, slope1, a1, kept1)
        ]
        + [whole_in(x) for x in (p1, wo, wqkv, dn1, up1, vec)],
        [
            t((seq_here, length, D), F32), whole_out((DP, 2 * DP)), whole_out((DP, DP)), whole_out((DP, 3 * DP)),
            whole_out((DP, FFP)), whole_out((DP, FFP)), whole_out((VEC_ROWS, DP)), whole_out((HEADS * length, length)),
        ],
        [
            vm((8, DP), F32),
            vm((SEQS_C, 2, length + 16, LANES), F32),
            vm((SEQS_C, 2, length + 16, LANES), F32),
            vm((SEQS_C * length, 3 * DP), BF),
        ],
        "phase_c",
    )
    grads = flatten_grads((dup1, ddn1, dup2, ddn2, dqkv, dwo, dp1, dp2, vec_b + vec_c, rel_sum), dp, head_size, shared_size)
    summed = scatter_all(grads, 4)
    h_shape, s_shape = head_params.shape, shared_params.shape

    def s(shape, dtype=F32):
        return jax.ShapeDtypeStruct(shape, dtype)

    updated = vmem_call(
        adam_kernel,
        (s(h_shape), s(h_shape), s(h_shape), s(h_shape, BF), s(s_shape), s(s_shape), s(s_shape), s(s_shape, BF)),
        (summed, head_params, head_first, head_second, shared_params, shared_first, shared_second),
        name="adam",
    )
    return (layer_out, input_grad) + tuple(updated)


def solution(mesh):
    frames = P(("dp", "head"), None, None)
    heads = P("head", "dp")
    shared = P(("dp", "head"))
    return jax.shard_map(
        per_device,
        mesh=mesh,
        in_specs=(frames, frames, P("dp"), heads, shared, heads, heads, shared, shared),
        out_specs=(frames, frames) + (heads,) * 4 + (shared,) * 4,
        check_vma=False,
    )
```

time: 615 us -> 219 us (0.36); the launches traced: 608 us -> 219 us
  local copies, waits for them, and re-layouts: 221 us -> 4.85 us
  matrix products: 158 us -> 0 us
  other arithmetic: 151 us -> 1.38 us
  Pallas kernels: 74.8 us -> 212 us
    dot_general x36 -> x0, matrix products: 158 us -> none  [the longest x2 20.3 us: ffn_backward(): jnp.einsum('amz,tz->amt', wide_gradient, layer_weights[lower_random_key],...]
    pallas_call x0 -> x7, Pallas kernels: none -> 142 us  [the longest x3 123 us: layer_call(): pl.pallas_call(body, grid=(steps,), out_shape=tuple((jax.ShapeDtypeStruct...]
    reduce_sum x23 -> x0, other arithmetic: 94.8 us -> none  [the longest x1 31.4 us: conv_backward(): jnp.sum(conv_grad * padded_glu[:, tap_index:tap_index + length], (0, 1))]
    reshape x52 -> x0, local copies, waits for them, and re-layouts: 66.9 us -> none  [the longest x21 23 us: flatten_dict(): grads[entry_name].reshape(-1)]
    concatenate x3 -> x0, local copies, waits for them, and re-layouts: 66.9 us -> none  [flatten_dict(): return jnp.concatenate(flat_parts)]
    another operation x5 -> x0, other arithmetic: 33.7 us -> none
    convert_element_type x8 -> x0, local copies, waits for them, and re-layouts: 24.8 us -> none  [the longest x1 4.45 us: attention_forward(): key_rows = jnp.einsum('yoz,zv->yov', gathered_params, layer_weights[W_KEY...]
    another operation x22 -> x0, local copies, waits for them, and re-layouts: 18.5 us -> none  [the longest x16 9.51 us: conv_backward(): jnp.stack(kernel_rows)]
where the time goes in v1:
time: 219 us
  Pallas kernels  212 us (97%)
  local copies, waits for them, and re-layouts  4.85 us (2%)
    pallas_call x3, Pallas kernels, layer_call(): pl.pallas_call(body, grid=(steps,), out_shape=tuple((jax.ShapeDtypeStruct...  123 us
    pallas_call x1, Pallas kernels, gather_all(): pl.pallas_call(functools.partial(gather_kernel, nz), out_shape=jax.ShapeD...  23.9 us
    pallas_call x1, Pallas kernels, scatter_all(): pl.pallas_call(functools.partial(scatter_kernel, nz), out_shape=jax.Shape...  23.9 us
    pallas_call x2, Pallas kernels, share_all(): pl.pallas_call(functools.partial(share_kernel, dp), out_shape=jax.ShapeDt...  21.4 us
    pallas_call x4, Pallas kernels, vmem_call(): pl.pallas_call(body, out_shape=outs, in_specs=[pl.BlockSpec(memory_space=...  19.5 us
    unnamed x10, local copies, waits for them, and re-layouts  4.85 us

profile of v1, /device:TPU:0, one launch (start us, length us, event | category | flops | bytes accessed | tf_op | source)
XLA Modules:
  0.0 218.6 jit_solution(14193950986390568363)
XLA Ops:
  0.6 1.7 align.1.src
  2.3 0.0 copy-start.3
  2.3 0.9 copy-done.3
  3.2 23.9 %gather_weights.1.got = bf16[16,2,336,128]{3,2,1,0:T(8,128)(2,1)S(1)} custom-call(bf16[336,128]{1,0:T(8,128)(2,1)S(1)} %copy-done.3), custom_call_target="tpu_custom_call" | custom-call | tf_op jit(solution)/shard_map/gather_weights/pallas_call | solution.py:123
  27.2 0.0 copy-start
  27.2 1.5 copy-done
  28.7 7.1 %make_weights.1 = (bf16[256,1024]{1,0:T(8,128)(2,1)}, bf16[1024,256]{1,0:T(8,128)(2,1)}, bf16[256,1024]{1,0:T(8,128)(2,1)}, bf16[1024,256]{1,0:T(8,128)(2,1)}, b...) custom-call(bf16[16,2,336,128]{3,2,1,0:T(8,128)(2,1)} %copy-done), custom_call_target="tpu_custom_call" | custom-call | tf_op jit(solution)/shard_map/make_weights/pallas_call | solution.py:361
  35.8 36.2 %phase_a.1 = (f32[3072,256]{1,0:T(8,128)}, bf16[3072,256]{1,0:T(8,128)(2,1)}, bf16[3072,1024]{1,0:T(8,128)(2,1)}, bf16[3072,1024]{1,0:T(8,128)(2,1)}, f32[3072,2...) custom-call(s32[32]{0:T(128)} %lengths.3, ...), custom_call_target="tpu_custom_call" | custom-call | tf_op jit(solution)/shard_map/phase_a/pallas_call | solution.py:1060
  72.0 11.5 %share_sums.2.shared = f32[32,8,128]{2,1,0:T(8,128)} custom-call(f32[8,128]{1,0:T(8,128)} %get-tuple-element.69.src), custom_call_target="tpu_custom_call" | custom-call | tf_op jit(solution)/shard_map/share_sums/pallas_call | solution.py:276
  83.6 27.4 %phase_b.1 = (bf16[16,192,240]{2,1,0:T(8,128)(2,1)}, f32[3072,256]{1,0:T(8,128)}, f32[3072,256]{1,0:T(8,128)}, f32[256,1024]{1,0:T(8,128)}, f32[256,1024]{1,0:T(...) custom-call(f32[32,8,128]{2,1,0:T(8,128)} %share_sums.2.shared, ...), custom_call_target="tpu_custom_call" | custom-call | tf_op jit(solution)/shard_map/phase_b/pallas_call | solution.py:1060
  111.0 9.9 %share_sums.3.shared_b = f32[32,8,128]{2,1,0:T(8,128)} custom-call(f32[8,128]{1,0:T(8,128)} %get-tuple-element.76.src), custom_call_target="tpu_custom_call" | custom-call | tf_op jit(solution)/shard_map/share_sums/pallas_call | solution.py:276
  120.9 0.0 copy-start.4
  120.9 59.3 %phase_c.1 = (f32[16,192,240]{2,1,0:T(8,128)}, f32[256,512]{1,0:T(8,128)}, f32[256,256]{1,0:T(8,128)}, f32[256,768]{1,0:T(8,128)}, f32[256,1024]{1,0:T(8,128)}, ...) custom-call(s32[32]{0:T(128)} %lengths.3, f32[32,8,128]{2,1,0:T(8,128)} %share_sums.2.shared, ...), custom_call_target="tpu_custom_call" | custom-call | tf_op jit(solution)/shard_map/phase_c/pallas_call | solution.py:1060
  180.2 0.0 copy-done.4
  180.2 1.4 add.3.vec
  181.6 8.4 %flatten_grads.1.g = bf16[2,16,336,128]{3,2,1,0:T(8,128)(2,1)} custom-call(f32[256,1024]{1,0:T(8,128)} %get-tuple-element.95.up1, f32[256,1024]{1,0:T(8,128)} %get-tuple-element.96.dn1, f32[256,1024]{1,0:T(8,128)} %get-tuple-element.97.up2, f32[256,1024]{1,0:T(8,128)} %get-tuple-element.98.dn2, f32[256,768]{1,0:T(8,128)} %get-tuple-element.99.qkv, ...), custom_call_target="tpu_custom_call" | custom-call | tf_op jit(solution)/shard_map/flatten_grads/pallas_call | solution.py:361
  190.0 0.0 copy-start.1
  190.0 1.8 copy-done.1
  191.8 23.9 %scatter_grads.1.g_ref = f32[336,128]{1,0:T(8,128)S(1)} custom-call(bf16[2,16,336,128]{3,2,1,0:T(8,128)(2,1)S(1)} %copy-done.1), custom_call_target="tpu_custom_call" | custom-call | tf_op jit(solution)/shard_map/scatter_grads/pallas_call | solution.py:219
  215.6 0.0 copy-start.2
  215.6 0.6 copy-done.2
  216.3 2.3 %adam.1 = (f32[1,36123]{1,0:T(1,128)}, f32[1,36123]{1,0:T(1,128)}, f32[1,36123]{1,0:T(1,128)}, bf16[1,36123]{1,0:T(2,128)(2,1)}, f32[5655]{0:T(1024)}, /*index=5...) custom-call(f32[336,128]{1,0:T(8,128)} %copy-done.2, f32[1,36123]{1,0:T(1,128)} %hp.1, f32[1,36123]{1,0:T(1,128)} %hf.1, ...), custom_call_target="tpu_custom_call" | custom-call | tf_op jit(solution)/shard_map/adam/pallas_call | solution.py:361
Async XLA Ops:
  2.3 0.9 copy-start.3
  27.2 1.5 copy-start
  120.9 59.3 %copy-start.4 = (f32[32,256]{1,0:T(8,128)S(1)}, f32[32,256]{1,0:T(8,128)}, u32[]{:S(2)}) copy-start(f32[32,256]{1,0:T(8,128)} %get-tuple-element.103) | copy-start | bytes 98308
  190.0 1.8 copy-start.1
  215.6 0.7 copy-start.2

commit v2 on v1

--- a/solution.py
+++ b/solution.py
@@ -238,50 +238,46 @@
     )(g)
 
 
-def share_kernel(dp_count, src, out, ss, rs):
-    me = lax.axis_index("dp")
-    core = lax.axis_index("head")
-    own = 2 * me + core
-    total = 2 * dp_count
+def peer_of(own, total, k):
+    other = lax.rem(own + k, total)
+    dp = other // 2
+    return other, dp, other - 2 * dp
+
+
+def own_number():
+    return 2 * lax.axis_index("dp") + lax.axis_index("head")
+
+
+def greet_all(total):
     barrier = pltpu.get_barrier_semaphore()
-
-    def peer(k):
-        other = lax.rem(own + k, total)
-        dp = other // 2
-        return other, dp, other - 2 * dp
+    own = own_number()
 
     @pl.loop(1, total)
     def _(k):
-        _, dp, head = peer(k)
+        _, dp, head = peer_of(own, total, k)
         pl.semaphore_signal(
             barrier, inc=1, device_id={"dp": dp, "head": head}, device_id_type=pl.DeviceIdType.MESH
         )
 
-    pl.semaphore_wait(barrier, total - 1)
-    out[own] = src[...]
+
+def share_start(total, src, inbox, ss, rs):
+    pl.semaphore_wait(pltpu.get_barrier_semaphore(), total - 1)
+    own = own_number()
+    inbox[own] = src[...]
 
     @pl.loop(1, total)
     def _(k):
-        _, dp, head = peer(k)
-        remote(src, out.at[own], ss.at[k], rs.at[own], dp, head).start()
+        _, dp, head = peer_of(own, total, k)
+        remote(src, inbox.at[own], ss.at[k], rs.at[own], dp, head).start()
+
+
+def share_finish(total, src, inbox, ss, rs):
+    own = own_number()
 
     @pl.loop(1, total)
     def _(k):
-        other, dp, head = peer(k)
-        remote(src, out.at[other], ss.at[k], rs.at[other], dp, head).wait()
-
-
-def share_all(block, dp, collective_id):
-    dma = pltpu.SemaphoreType.DMA
-    return pl.pallas_call(
-        functools.partial(share_kernel, dp),
-        out_shape=jax.ShapeDtypeStruct((2 * dp,) + block.shape, block.dtype),
-        in_specs=[pl.BlockSpec(memory_space=pltpu.VMEM)],
-        out_specs=pl.BlockSpec(memory_space=pltpu.VMEM),
-        scratch_shapes=[dma((2 * dp,)), dma((2 * dp,))],
-        compiler_params=pltpu.CompilerParams(collective_id=collective_id, has_side_effects=True),
-        name="share_sums",
-    )(block)
+        other, dp, head = peer_of(own, total, k)
+        remote(src, inbox.at[other], ss.at[k], rs.at[other], dp, head).wait()
 
 
 HEADS = 4
@@ -764,10 +760,16 @@
 def phase_a_kernel(
     seqs, lengths, frames, up, dn, wqkv, wo, p1, vec, rel,
     kept1_o, a1_o, h_o, sp_o, kept2_o, a2_o, qkv_o, e_o, rl_o, m_o,
-    x2_o, kept3_o, a3_o, f1_o, f2_o, gl_o, w_o, stats_o,
-    pad,
+    x2_o, kept3_o, a3_o, f1_o, f2_o, gl_o, w_o, keep_o,
+    pad, stats_o, inbox, ss, rs,
 ):
     step = pl.program_id(0)
+    total = inbox.shape[0]
+
+    @pl.when(step == 0)
+    def _():
+        greet_all(total)
+
     length = frames.shape[1]
     tokens = seqs * length
     first_seq = lax.axis_index("head") * (seqs * pl.num_programs(0)) + step * seqs
@@ -833,7 +835,7 @@
         stats_o[...] = jnp.zeros(stats_o.shape, F32)
 
     count = jnp.float32(0.0)
-    total = jnp.zeros((1, DP), F32)
+    summed = jnp.zeros((1, DP), F32)
     for b in range(seqs):
         rows = pl.ds(b * length, length)
         valid = jnp.where(valid_rows(lengths, first_seq + b, length), 1.0, 0.0)
@@ -851,9 +853,9 @@
             for r in range(KW):
                 acc = acc + pad[b, t, pl.ds(8 - half + r, length), :] * vec[pl.ds(TAPS + r, 1), cols]
             w_o[rows, cols] = acc
-        total = total + jnp.sum(w_o[rows, :] * valid, 0, keepdims=True)
+        summed = summed + jnp.sum(w_o[rows, :] * valid, 0, keepdims=True)
         count = count + lengths[first_seq + b].astype(F32)
-    mean = total / count
+    mean = summed / count
     square = jnp.zeros((1, DP), F32)
     for b in range(seqs):
         valid = jnp.where(valid_rows(lengths, first_seq + b, length), 1.0, 0.0)
@@ -869,6 +871,12 @@
         stats_o[pl.ds(2 + t, 1), :] += square[:, cols] + delta * delta * (old * count / new)
     stats_o[pl.ds(4, 1), :] = new
 
+    @pl.when(step == pl.num_programs(0) - 1)
+    def _():
+        share_start(total, stats_o, inbox, ss, rs)
+        share_finish(total, stats_o, inbox, ss, rs)
+        batch_stats(inbox[...], keep_o)
+
 
 def batch_stats(shared, keep):
     counts = shared[:, 4:5, :]
@@ -883,20 +891,22 @@
     keep[pl.ds(0, 1), :] = jnp.concatenate(means, 1)
     keep[pl.ds(1, 1), :] = lax.rsqrt(jnp.concatenate(spreads, 1) + NORM_EPS)
     keep[pl.ds(2, 1), :] = jnp.concatenate([total, total], 1)
+    keep[pl.ds(3, 5), :] = jnp.zeros((5, DP), F32)
 
 
 def phase_b_kernel(
-    seqs, shared, w, x2, cotangent, p2, up, dn, vec,
-    out_o, dy_o, dx3_o, dup_o, ddn_o, dp2_o, vec_o, sums_o,
-    keep,
+    seqs, keep, w, x2, cotangent, p2, up, dn, vec,
+    out_o, dy_o, dx3_o, dup_o, ddn_o, dp2_o, vec_o, keep_o,
+    sums_o, inbox, ss, rs,
 ):
     step = pl.program_id(0)
+    total = inbox.shape[0]
     length = cotangent.shape[1]
     tokens = seqs * length
 
     @pl.when(step == 0)
     def _():
-        batch_stats(shared[...], keep)
+        greet_all(total)
         for ref in (dup_o, ddn_o, dp2_o, vec_o, sums_o):
             ref[...] = jnp.zeros(ref.shape, F32)
 
@@ -941,12 +951,21 @@
         sums_o[pl.ds(t, 1), :] += first[:, cols]
         sums_o[pl.ds(2 + t, 1), :] += second[:, cols]
 
+    @pl.when(step == pl.num_programs(0) - 1)
+    def _():
+        share_start(total, sums_o, inbox, ss, rs)
+        share_finish(total, sums_o, inbox, ss, rs)
+        sums = jnp.sum(inbox[...], 0)
+        keep_o[...] = keep[...]
+        keep_o[pl.ds(3, 1), :] = jnp.concatenate([sums[0:1], sums[1:2]], 1)
+        keep_o[pl.ds(4, 1), :] = jnp.concatenate([sums[2:3], sums[3:4]], 1)
+
 
 def phase_c_kernel(
-    seqs, lengths, shared, shared_b, w, dy, dx3, gl, f1, f2, a3, kept3, qkv, e_all, rl, m, a2, kept2, h, slope, a1, kept1,
+    seqs, lengths, keep, w, dy, dx3, gl, f1, f2, a3, kept3, qkv, e_all, rl, m, a2, kept2, h, slope, a1, kept1,
     p1, wo, wqkv, dn, up, vec,
     dx0_o, dp1_o, dwo_o, dqkv_o, dup_o, ddn_o, vec_o, rel_o,
-    keep, padw, padg, grads,
+    padw, padg, grads,
 ):
     step = pl.program_id(0)
     length = dx0_o.shape[1]
@@ -959,10 +978,6 @@
 
     @pl.when(step == 0)
     def _():
-        batch_stats(shared[...], keep)
-        sums = jnp.sum(shared_b[...], 0)
-        keep[pl.ds(3, 1), :] = jnp.concatenate([sums[0:1], sums[1:2]], 1)
-        keep[pl.ds(4, 1), :] = jnp.concatenate([sums[2:3], sums[3:4]], 1)
         for ref in (dp1_o, dwo_o, dqkv_o, dup_o, ddn_o, vec_o, rel_o, padw, padg):
             ref[...] = jnp.zeros(ref.shape, F32)
 
@@ -1047,7 +1062,7 @@
     dx0_o[...] = dx0[:, :D].reshape(seqs, length, D)
 
 
-def layer_call(body, steps, ins, outs, scratch, name):
+def layer_call(body, steps, ins, outs, scratch, name, collective_id=None):
     def spec(item):
         kind, shape = item
         if kind == "smem":
@@ -1064,7 +1079,12 @@
         in_specs=[spec((kind, block)) for kind, block, _ in ins],
         out_specs=tuple(spec((kind, block)) for kind, block, _, _ in outs),
         scratch_shapes=list(scratch),
-        compiler_params=pltpu.CompilerParams(vmem_limit_bytes=BIG, dimension_semantics=("arbitrary",)),
+        compiler_params=pltpu.CompilerParams(
+            vmem_limit_bytes=BIG,
+            dimension_semantics=("arbitrary",),
+            collective_id=collective_id,
+            has_side_effects=collective_id is not None,
+        ),
         name=name,
     )(*arrays)
 
@@ -1105,10 +1125,12 @@
     got = gather_all(mine, dp, 1)
     up1, dn1, up2, dn2, wqkv, wo, p1, p2, vec, rel = make_weights(got, head_size, shared_size, length)
 
+    dma = pltpu.SemaphoreType.DMA
+    sharing = [vm((8, LANES), F32), vm((2 * dp, 8, LANES), F32), dma((2 * dp,)), dma((2 * dp,))]
     steps = seq_here // SEQS_A
     t = functools.partial(tile_out, steps)
     (
-        kept1, a1, h1, slope1, kept2, a2, qkv, e_all, rl, m, x2, kept3, a3, f1, f2, gl, w, stats
+        kept1, a1, h1, slope1, kept2, a2, qkv, e_all, rl, m, x2, kept3, a3, f1, f2, gl, w, keep
     ) = layer_call(
         functools.partial(phase_a_kernel, SEQS_A),
         steps,
@@ -1118,34 +1140,34 @@
             t((tokens, DP), F32), t((tokens, DP), BF), t((tokens, 3 * DP), BF),
             t((seq_here, HEADS * length, length), BF), t((tokens, DP), F32), t((tokens, DP), BF),
             t((tokens, DP), F32), t((tokens, DP), F32), t((tokens, DP), BF), t((tokens, DP), BF),
-            t((tokens, DP), BF), t((tokens, DP), BF), t((tokens, DP), F32), whole_out((8, LANES)),
+            t((tokens, DP), BF), t((tokens, DP), BF), t((tokens, DP), F32), whole_out((8, DP)),
         ],
-        [vm((SEQS_A, 2, length + 16, LANES), F32)],
+        [vm((SEQS_A, 2, length + 16, LANES), F32)] + sharing,
         "phase_a",
+        2,
     )
-    shared_a = share_all(stats, dp, 2)
     steps = seq_here // SEQS_B
     t = functools.partial(tile_out, steps)
-    layer_out, dy, dx3, dup2, ddn2, dp2, vec_b, sums = layer_call(
+    layer_out, dy, dx3, dup2, ddn2, dp2, vec_b, keep = layer_call(
         functools.partial(phase_b_kernel, SEQS_B),
         steps,
-        [whole_in(shared_a), tile_in(w, steps), tile_in(x2, steps), tile_in(cotangent, steps)]
+        [whole_in(keep), tile_in(w, steps), tile_in(x2, steps), tile_in(cotangent, steps)]
         + [whole_in(x) for x in (p2, up2, dn2, vec)],
         [
             t((seq_here, length, D), BF), t((tokens, DP), F32), t((tokens, DP), F32),
             whole_out((DP, FFP)), whole_out((DP, FFP)), whole_out((DP, DP)), whole_out((VEC_ROWS, DP)),
-            whole_out((8, LANES)),
+            whole_out((8, DP)),
         ],
-        [vm((8, DP), F32)],
+        sharing,
         "phase_b",
+        3,
     )
-    shared_b = share_all(sums, dp, 3)
     steps = seq_here // SEQS_C
     t = functools.partial(tile_out, steps)
     input_grad, dp1, dwo, dqkv, dup1, ddn1, vec_c, rel_sum = layer_call(
         functools.partial(phase_c_kernel, SEQS_C),
         steps,
-        [("smem", None, lengths), whole_in(shared_a), whole_in(shared_b)]
+        [("smem", None, lengths), whole_in(keep)]
         + [
             tile_in(x, steps)
             for x in (w, dy, dx3, gl, f1, f2, a3, kept3, qkv, e_all, rl, m, a2, kept2, h1, slope1, a1, kept1)
@@ -1156,7 +1178,6 @@
             whole_out((DP, FFP)), whole_out((DP, FFP)), whole_out((VEC_ROWS, DP)), whole_out((HEADS * length, length)),
         ],
         [
-            vm((8, DP), F32),
             vm((SEQS_C, 2, length + 16, LANES), F32),
             vm((SEQS_C, 2, length + 16, LANES), F32),
             vm((SEQS_C * length, 3 * DP), BF),

time: 219 us -> 214 us (0.977)
  Pallas kernels: 212 us -> 206 us
    pallas_call x2 -> x0, Pallas kernels: 21.4 us -> none  [share_all(): pl.pallas_call(functools.partial(share_kernel, dp), out_shape=jax.ShapeDt...]
    pallas_call x3, Pallas kernels: 123 us -> 139 us  [layer_call(): pl.pallas_call(body, grid=(steps,), out_shape=tuple((jax.ShapeDtypeStruct...]
    unnamed x10 -> x13, local copies, waits for them, and re-layouts: 4.85 us -> 6.01 us
where the time goes in v2:
time: 214 us
  Pallas kernels  206 us (96%)
  local copies, waits for them, and re-layouts  6.01 us (3%)
    pallas_call x3, Pallas kernels, layer_call(): pl.pallas_call(body, grid=(steps,), out_shape=tuple((jax.ShapeDtypeStruct...  139 us
    pallas_call x1, Pallas kernels, gather_all(): pl.pallas_call(functools.partial(gather_kernel, nz), out_shape=jax.ShapeD...  23.9 us
    pallas_call x1, Pallas kernels, scatter_all(): pl.pallas_call(functools.partial(scatter_kernel, nz), out_shape=jax.Shape...  22.9 us
    pallas_call x4, Pallas kernels, vmem_call(): pl.pallas_call(body, out_shape=outs, in_specs=[pl.BlockSpec(memory_space=...  19.5 us
    unnamed x13, local copies, waits for them, and re-layouts  6.01 us

profile of v2, /device:TPU:0, one launch (start us, length us, event | category | flops | bytes accessed | tf_op | source)
XLA Modules:
  0.0 213.7 jit_solution(12834833707647268588)
XLA Ops:
  0.6 1.7 align.1.src
  2.3 0.0 copy-start.3
  2.3 0.9 copy-done.3
  3.2 23.9 %gather_weights.1.got = bf16[16,2,336,128]{3,2,1,0:T(8,128)(2,1)S(1)} custom-call(bf16[336,128]{1,0:T(8,128)(2,1)S(1)} %copy-done.3), custom_call_target="tpu_custom_call" | custom-call | tf_op jit(solution)/shard_map/gather_weights/pallas_call | solution.py:123
  27.2 0.0 copy-start
  27.2 1.5 copy-done
  28.7 7.1 %make_weights.1 = (bf16[256,1024]{1,0:T(8,128)(2,1)}, bf16[1024,256]{1,0:T(8,128)(2,1)}, bf16[256,1024]{1,0:T(8,128)(2,1)}, bf16[1024,256]{1,0:T(8,128)(2,1)}, b...) custom-call(bf16[16,2,336,128]{3,2,1,0:T(8,128)(2,1)} %copy-done), custom_call_target="tpu_custom_call" | custom-call | tf_op jit(solution)/shard_map/make_weights/pallas_call | solution.py:357
  35.8 45.0 %phase_a.1 = (f32[3072,256]{1,0:T(8,128)}, bf16[3072,256]{1,0:T(8,128)(2,1)}, bf16[3072,1024]{1,0:T(8,128)(2,1)}, bf16[3072,1024]{1,0:T(8,128)(2,1)}, f32[3072,2...) custom-call(s32[32]{0:T(128)} %lengths.3, ...), custom_call_target="tpu_custom_call" | custom-call | tf_op jit(solution)/shard_map/phase_a/pallas_call | solution.py:1075
  80.8 35.3 %phase_b.1 = (bf16[16,192,240]{2,1,0:T(8,128)(2,1)}, f32[3072,256]{1,0:T(8,128)}, f32[3072,256]{1,0:T(8,128)}, f32[256,1024]{1,0:T(8,128)}, f32[256,1024]{1,0:T(...) custom-call(f32[8,256]{1,0:T(8,128)} %get-tuple-element.69.keep, ...), custom_call_target="tpu_custom_call" | custom-call | tf_op jit(solution)/shard_map/phase_b/pallas_call | solution.py:1075
  116.2 0.0 copy-start.5
  116.2 59.0 %phase_c.1 = (f32[16,192,240]{2,1,0:T(8,128)}, f32[256,512]{1,0:T(8,128)}, f32[256,256]{1,0:T(8,128)}, f32[256,768]{1,0:T(8,128)}, f32[256,1024]{1,0:T(8,128)}, ...) custom-call(s32[32]{0:T(128)} %lengths.3, f32[8,256]{1,0:T(8,128)} %get-tuple-element.76.keep, ...), custom_call_target="tpu_custom_call" | custom-call | tf_op jit(solution)/shard_map/phase_c/pallas_call | solution.py:1075
  175.1 0.0 copy-done.5
  175.2 1.4 add.3.vec
  176.5 8.4 %flatten_grads.1.g = bf16[2,16,336,128]{3,2,1,0:T(8,128)(2,1)} custom-call(f32[256,1024]{1,0:T(8,128)} %get-tuple-element.95.up1, f32[256,1024]{1,0:T(8,128)} %get-tuple-element.96.dn1, f32[256,1024]{1,0:T(8,128)} %get-tuple-element.97.up2, f32[256,1024]{1,0:T(8,128)} %get-tuple-element.98.dn2, f32[256,768]{1,0:T(8,128)} %get-tuple-element.99.qkv, ...), custom_call_target="tpu_custom_call" | custom-call | tf_op jit(solution)/shard_map/flatten_grads/pallas_call | solution.py:357
  184.9 0.0 copy-start.1
  184.9 1.8 copy-done.1
  186.7 0.0 copy-start.4
  186.7 22.9 %scatter_grads.1.g_ref = f32[336,128]{1,0:T(8,128)S(1)} custom-call(bf16[2,16,336,128]{3,2,1,0:T(8,128)(2,1)S(1)} %copy-done.1), custom_call_target="tpu_custom_call" | custom-call | tf_op jit(solution)/shard_map/scatter_grads/pallas_call | solution.py:219
  209.6 0.0 copy-start.2
  209.6 0.7 copy-done.2
  210.2 2.3 %adam.1 = (f32[1,36123]{1,0:T(1,128)}, f32[1,36123]{1,0:T(1,128)}, f32[1,36123]{1,0:T(1,128)}, bf16[1,36123]{1,0:T(2,128)(2,1)}, f32[5655]{0:T(1024)}, /*index=5...) custom-call(f32[336,128]{1,0:T(8,128)} %copy-done.2, f32[1,36123]{1,0:T(1,128)} %hp.1, f32[1,36123]{1,0:T(1,128)} %hf.1, ...), custom_call_target="tpu_custom_call" | custom-call | tf_op jit(solution)/shard_map/adam/pallas_call | solution.py:357
  212.5 0.0 copy-done.4
  212.5 1.1 copy.20
Async XLA Ops:
  2.3 0.9 copy-start.3
  27.2 1.5 copy-start
  116.2 59.0 %copy-start.5 = (f32[32,256]{1,0:T(8,128)S(1)}, f32[32,256]{1,0:T(8,128)}, u32[]{:S(2)}) copy-start(f32[32,256]{1,0:T(8,128)} %get-tuple-element.103) | copy-start | bytes 98308
  184.9 1.8 copy-start.1
  186.7 25.8 %copy-start.4 = (bf16[16,192,240]{2,1,0:T(8,128)(2,1)S(1)}, bf16[16,192,240]{2,1,0:T(8,128)(2,1)}, u32[]{:S(2)}) copy-start(bf16[16,192,240]{2,1,0:T(8,128)(2,1)} %get-tuple-element.124) | copy-start | bytes 4423684
  209.6 0.7 copy-start.2

commit v3 on v2

--- a/solution.py
+++ b/solution.py
@@ -51,7 +51,10 @@
     hello(4 * zc + 2 * (1 - yc) + xc, core)
     hello(4 * zc + 2 * yc + 1 - xc, core)
     hello(me, 1 - core)
-    pl.semaphore_wait(barrier, nz + 2)
+
+
+def greeted(nz):
+    pl.semaphore_wait(pltpu.get_barrier_semaphore(), nz + 2)
 
 
 def gather_kernel(nz, src, out, sz, rz, s1, r1, s2, r2, sc, rc):
@@ -60,6 +63,7 @@
     parts = (pl.ds(0, row_a), pl.ds(row_a, rows - row_a))
     me, core, zc, yc, xc = grid_place(nz)
     greet(nz, me, core, zc, yc, xc)
+    greeted(nz)
     out[me, core] = src[...]
     y_peer = 4 * zc + 2 * (1 - yc) + xc
     x_peer = 4 * zc + 2 * yc + 1 - xc
@@ -133,109 +137,128 @@
     )(block)
 
 
-def scatter_kernel(nz, g, out, c1, t1, rx1, t2, rx2, t3, rx3, sc, rc, s1, r1, s2, r2, s3, r3):
-    rows = g.shape[2]
-    row_a = up_to(rows // 2, 16)
-    starts = (0, row_a)
-    sizes = (row_a, rows - row_a)
-    parts = tuple(pl.ds(a, n) for a, n in zip(starts, sizes))
-    me, core, zc, yc, xc = grid_place(nz)
-    greet(nz, me, core, zc, yc, xc)
-    y_peer = 4 * zc + 2 * (1 - yc) + xc
-    x_peer = 4 * zc + 2 * yc + 1 - xc
-    firsts = (x_peer, y_peer)
-    seconds = (y_peer, x_peer)
-    pending = []
-
-    def send(src, dst, send_sem, recv_sem, dp, head):
-        copy = remote(src, dst, send_sem, recv_sem, dp, head)
-        copy.start()
-        pending.append(copy)
-
-    def arrived(block, send_sem, recv_sem):
-        remote(block, block, send_sem, recv_sem, me, 1 - core).wait_recv()
-
-    order = list(range(1, nz)) + [0]
-    zs = [lax.rem(zc + k, nz) for k in range(nz)]
-    give = ((1 - xc, 2 + 1 - xc), (2 * (1 - yc), 2 * (1 - yc) + 1))
-    second_give = (1 - yc, 1 - xc)
-    second_keep = (yc, xc)
-
-    def place(p, b):
-        return 2 * b + xc if p == 0 else 2 * yc + b
-
-    for k in order:
-        z = zs[k]
-        send(g.at[1 - core, pl.ds(4 * z, 4)], c1.at[pl.ds(4 * z, 4)], sc.at[k], rc.at[z], me, 1 - core)
-    for k in order:
-        z = zs[k]
-        arrived(c1.at[pl.ds(4 * z, 4)], sc.at[k], rc.at[z])
-        for p in (0, 1):
-            n = pl.ds(0, sizes[p])
+class Scatter:
+    @staticmethod
+    def scratch(dp, hr, sr):
+        nz, rows = dp // 4, hr + sr
+        dma, vm = pltpu.SemaphoreType.DMA, pltpu.VMEM
+        return [
+            vm((2, dp, rows, LANES), BF), vm((dp, rows, LANES), BF),
+            vm((nz, 2, rows, LANES), BF), vm((nz, 2, rows, LANES), BF),
+            vm((nz, rows, LANES), BF), vm((nz, rows, LANES), BF),
+            vm((nz, rows, LANES), BF), vm((nz, rows, LANES), BF),
+            dma((nz, 2)), dma((nz, 2)), dma((3, nz)), dma((3, nz)), dma((3, nz)), dma((3, nz)), dma((3, nz)), dma((3, nz)),
+        ]
+
+    def __init__(self, nz, hr, sr, mine, refs):
+        self.nz, self.mine = nz, mine
+        (
+            self.g, self.c1, self.t1, self.rx1, self.t2, self.rx2, self.t3, self.rx3,
+            self.sc, self.rc, self.s1, self.r1, self.s2, self.r2, self.s3, self.r3,
+        ) = refs
+        ha = up_to(hr // 2, 16)
+        self.parts = (pl.ds(0, ha), pl.ds(ha, hr - ha), pl.ds(hr, sr))
+        self.kinds = (pl.ds(0, hr), pl.ds(hr, sr))
+        self.me, self.core, self.zc, self.yc, self.xc = grid_place(nz)
+        zc, yc, xc = self.zc, self.yc, self.xc
+        y_peer = 4 * zc + 2 * (1 - yc) + xc
+        x_peer = 4 * zc + 2 * yc + 1 - xc
+        self.firsts = (x_peer, y_peer, x_peer)
+        self.seconds = (y_peer, x_peer, y_peer)
+        self.second_give = (1 - yc, 1 - xc, 1 - yc)
+        self.second_keep = (yc, xc, yc)
+
+    def core_copy(self, z, kind):
+        group, rows = pl.ds(4 * z, 4), self.kinds[kind]
+        return remote(
+            self.g.at[1 - self.core, group, rows], self.c1.at[group, rows],
+            self.sc.at[z, kind], self.rc.at[z, kind], self.me, 1 - self.core,
+        )
+
+    def first_copy(self, z, p):
+        rows = self.parts[p]
+        return remote(
+            self.t1.at[z, :, rows], self.rx1.at[z, :, rows], self.s1.at[p, z], self.r1.at[p, z], self.firsts[p], self.core
+        )
+
+    def second_copy(self, z, p):
+        rows = self.parts[p]
+        return remote(
+            self.t2.at[z, rows], self.rx2.at[z, rows], self.s2.at[p, z], self.r2.at[p, z], self.seconds[p], self.core
+        )
+
+    def third_copy(self, z, p):
+        rows = self.parts[p]
+        return remote(
+            self.t3.at[z, rows], self.rx3.at[self.zc, rows], self.s3.at[p, z], self.r3.at[p, self.zc],
+            4 * z + 2 * self.yc + self.xc, self.core,
+        )
+
+    def place(self, p, z, b):
+        return 4 * z + (2 * self.yc + b if p == 1 else 2 * b + self.xc)
+
+    def held(self, z, p, slot):
+        rows = self.parts[p]
+        return self.g[self.core, slot, rows].astype(F32) + self.c1[slot, rows].astype(F32)
+
+    def partial(self, z, p, b):
+        return self.held(z, p, self.place(p, z, b)) + self.rx1[z, b, self.parts[p]].astype(F32)
+
+    def stage_core(self, z, kind):
+        self.core_copy(z, kind).start()
+
+    def stage_first(self, z, kind):
+        self.core_copy(z, kind).wait_recv()
+        for p in ((0, 1), (2,))[kind]:
             for b in (0, 1):
-                slot = 4 * z + give[p][b]
-                t1[p, z, b, n] = (g[core, slot, parts[p]].astype(F32) + c1[slot, parts[p]].astype(F32)).astype(BF)
-            send(t1.at[p, z, :, n], rx1.at[p, z, :, n], s1.at[p, k], r1.at[p, z], firsts[p], core)
-
-    def partial(p, z, b):
-        slot = 4 * z + place(p, b)
-        n = pl.ds(0, sizes[p])
-        return g[core, slot, parts[p]].astype(F32) + c1[slot, parts[p]].astype(F32) + rx1[p, z, b, n].astype(F32)
-
-    for k in order:
-        z = zs[k]
-        for p in (0, 1):
-            n = pl.ds(0, sizes[p])
-            arrived(rx1.at[p, z, :, n], s1.at[p, k], r1.at[p, z])
-            t2[p, z, n] = partial(p, z, second_give[p]).astype(BF)
-            send(t2.at[p, z, n], rx2.at[p, z, n], s2.at[p, k], r2.at[p, z], seconds[p], core)
-    for k in order:
-        z = zs[k]
-        for p in (0, 1):
-            n = pl.ds(0, sizes[p])
-            arrived(rx2.at[p, z, n], s2.at[p, k], r2.at[p, z])
-            total = partial(p, z, second_keep[p]) + rx2[p, z, n].astype(F32)
-            if k:
-                t3[p, z, n] = total.astype(BF)
-                send(t3.at[p, z, n], rx3.at[p, zc, n], s3.at[p, k], r3.at[p, zc], 4 * z + 2 * yc + xc, core)
-            else:
-                out[parts[p], :] = total
-    for k in order[:-1]:
-        z = zs[k]
-        for p in (0, 1):
-            n = pl.ds(0, sizes[p])
-            arrived(rx3.at[p, z, n], s3.at[p, k], r3.at[p, z])
-            out[parts[p], :] += rx3[p, z, n].astype(F32)
-    for copy in pending:
-        copy.wait_send()
-
-
-def scatter_all(g, collective_id):
-    dp, rows = g.shape[1], g.shape[2]
-    nz = dp // 4
-    half = up_to(rows // 2, 16)
-    dma = pltpu.SemaphoreType.DMA
-    vm = pltpu.VMEM
-    return pl.pallas_call(
-        functools.partial(scatter_kernel, nz),
-        out_shape=jax.ShapeDtypeStruct((rows, LANES), F32),
-        in_specs=[pl.BlockSpec(memory_space=pltpu.VMEM)],
-        out_specs=pl.BlockSpec(memory_space=pltpu.VMEM),
-        scratch_shapes=[
-            vm((dp, rows, LANES), BF),
-            vm((2, nz, 2, half, LANES), BF),
-            vm((2, nz, 2, half, LANES), BF),
-            vm((2, nz, half, LANES), BF),
-            vm((2, nz, half, LANES), BF),
-            vm((2, nz, half, LANES), BF),
-            vm((2, nz, half, LANES), BF),
-            dma((nz,)), dma((nz,)), dma((2, nz)), dma((2, nz)), dma((2, nz)), dma((2, nz)), dma((2, nz)), dma((2, nz)),
-        ],
-        compiler_params=pltpu.CompilerParams(
-            collective_id=collective_id, has_side_effects=True, vmem_limit_bytes=40 << 20
-        ),
-        name="scatter_grads",
-    )(g)
+                slot = 4 * z + (2 * (1 - self.yc) + b if p == 1 else 2 * b + 1 - self.xc)
+                self.t1[z, b, self.parts[p]] = self.held(z, p, slot).astype(BF)
+            self.first_copy(z, p).start()
+
+    def stage_second(self, z, kind):
+        for p in ((0, 1), (2,))[kind]:
+            self.first_copy(z, p).wait_recv()
+            self.t2[z, self.parts[p]] = self.partial(z, p, self.second_give[p]).astype(BF)
+            self.second_copy(z, p).start()
+
+    def stage_third(self, z, kind):
+        for p in ((0, 1), (2,))[kind]:
+            rows = self.parts[p]
+            self.second_copy(z, p).wait_recv()
+            total = self.partial(z, p, self.second_keep[p]) + self.rx2[z, rows].astype(F32)
+
+            @pl.when(self.zc == z)
+            def _():
+                self.mine[rows, :] = total
+
+            @pl.when(self.zc != z)
+            def _():
+                self.t3[z, rows] = total.astype(BF)
+                self.third_copy(z, p).start()
+
+    def finish(self, out):
+        total = self.mine[...]
+        for k in range(1, self.nz):
+            sender = lax.rem(self.zc + k, self.nz)
+            for p in range(3):
+                rows = self.parts[p]
+                remote(
+                    self.t3.at[sender, rows], self.rx3.at[sender, rows], self.s3.at[p, sender], self.r3.at[p, sender],
+                    self.me, 1 - self.core,
+                ).wait_recv()
+            total = total + self.rx3[sender].astype(F32)
+        out[...] = total
+        for z in range(self.nz):
+            for kind in range(2):
+                self.core_copy(z, kind).wait_send()
+            for p in range(3):
+                self.first_copy(z, p).wait_send()
+                self.second_copy(z, p).wait_send()
+
+            @pl.when(self.zc != z)
+            def _():
+                for p in range(3):
+                    self.third_copy(z, p).wait_send()
 
 
 def peer_of(own, total, k):
@@ -394,7 +417,18 @@
     out[pl.ds(hr, sr), :] = push_lanes(x.reshape(sr, LANES), so).astype(BF)
 
 
-def adam_kernel(g_ref, hp, hf, hs, sp, sf, ss, hf_o, hs_o, hp_o, hc_o, sf_o, ss_o, sp_o, sc_o):
+def adam_kernel(
+    early, grad, g_ref, hp, hf, hs, sp, sf, ss, out_o, grad_o, hf_o, hs_o, hp_o, hc_o, sf_o, ss_o, sp_o, sc_o
+):
+    out_o[...] = early[...]
+    grad_o[...] = grad[...]
+
+    @pl.when(pl.program_id(0) == 0)
+    def _():
+        adam_update(g_ref, hp, hf, hs, sp, sf, ss, hf_o, hs_o, hp_o, hc_o, sf_o, ss_o, sp_o, sc_o)
+
+
+def adam_update(g_ref, hp, hf, hs, sp, sf, ss, hf_o, hs_o, hp_o, hc_o, sf_o, ss_o, sp_o, sc_o):
     head_size, shared_size = hp.shape[1], sp.shape[0]
     hr, sr = slot_rows(head_size), slot_rows(shared_size)
     ho, so = own_offsets(head_size, shared_size)
@@ -491,9 +525,10 @@
         dst[:, pl.ds(t * LANES, LANES)] = value.astype(dst.dtype)
 
 
-def load_tiles(src, tiles):
+def load_tiles(src, tiles, factor=None):
     for t in range(src.shape[1] // LANES):
-        tiles[t, pl.ds(0, src.shape[0]), :] = src[:, pl.ds(t * LANES, LANES)]
+        value = src[:, pl.ds(t * LANES, LANES)]
+        tiles[t, pl.ds(0, src.shape[0]), :] = factor * value if factor else value
 
 
 def flat_rows(total, size):
@@ -539,7 +574,7 @@
             take(fh.at[g], hp[place], D, HF, 0, HF, wide, 0, g * HFP)
             take(fh.at[g], hp[bplace], 1, HF, 0, HF, wide, 240, g * HFP)
         patch(wide, 3, 240, lane == HF - 3 * LANES, UNIT)
-        spill(wide, DP, dst_ref)
+        spill(wide, DP, dst_ref, 0.5)
     for dst_ref, place, brow in ((dn1, "dn1", DOWNB_ONE), (dn2, "dn2", DOWNB_TWO)):
         for g in range(2):
             clear(tall, 2, g * HFP + HF, 32)
@@ -553,8 +588,8 @@
             take(fh.at[g], hp[place], D, HC, 0, HC, wide, 0, lane0)
             if bplace:
                 take(fh.at[g], hp[bplace], 1, HC, 0, HC, wide, 240, lane0)
-    patch(wide, 0, 240, lane == MASK_LANE, 1.0)
-    patch(wide, 4, 240, (lane >= MASK_LANE) & (lane < MASK_LANE + 3), 1.0)
+    for tile in (0, 1, 4, 5):
+        patch(wide, tile, 240, lane == MASK_LANE, 1.0)
     spill(wide, DP, qkv)
     clear(tall, 2, 0, DP)
     for g in range(2):
@@ -583,7 +618,7 @@
         row = jnp.concatenate([tmp[t, pl.ds(0, 1), :] for t in range(3)] + [jnp.zeros((1, LANES), F32)], 1)
         rows = jnp.broadcast_to(row, (length, 4 * LANES))
         rows = pltpu.roll(rows, 4 * LANES - (length - 1), 1, stride=1, stride_axis=0)
-        rel[n] = rows[:, :length] * LOG2E
+        rel[pl.ds(n * length, length), :] = rows[:, :length] * LOG2E
 
 
 def make_weights(got, head_size, shared_size, length):
@@ -594,7 +629,7 @@
 
     outs = (
         s(DP, FFP), s(FFP, DP), s(DP, FFP), s(FFP, DP), s(DP, 3 * DP), s(DP, DP), s(DP, 2 * DP), s(DP, DP),
-        s(VEC_ROWS, DP, dtype=F32), s(HEADS, length, length, dtype=F32),
+        s(VEC_ROWS, DP, dtype=F32), s(HEADS * length, length, dtype=F32),
     )
     vm = pltpu.VMEM
     scratch = (
@@ -609,111 +644,142 @@
     )
 
 
-def flatten_kernel(sizes, up1, dn1, up2, dn2, qkv, wo, p1, p2, vec, rel, out, fh, fs, wide, tall, tmp):
-    dp, head_size, shared_size = sizes
-    hr, sr = slot_rows(head_size), slot_rows(shared_size)
-    hp, used_h = head_places()
-    sp, used_s = shared_places()
-    for g in range(2):
-        first = used_h // LANES // 8 * 8
-        fh[g, pl.ds(first, fh.shape[1] - first), :] = jnp.zeros((fh.shape[1] - first, LANES), F32)
-    first = used_s // LANES // 8 * 8
-    fs[pl.ds(first, fs.shape[0] - first), :] = jnp.zeros((fs.shape[0] - first, LANES), F32)
-    for src, place, bplace in ((up1, "up1", "upb1"), (up2, "up2", "upb2")):
-        load_tiles(src, wide)
+class Flat:
+    @staticmethod
+    def scratch(dp, head_size, shared_size):
+        vm = pltpu.VMEM
+        return [
+            vm((2, flat_rows(head_size * dp, head_size), LANES), F32),
+            vm((flat_rows(shared_size * 2 * dp, shared_size), LANES), F32),
+            vm((8, DP, LANES), F32),
+            vm((2, FFP, LANES), F32),
+            vm((4, 8, LANES), F32),
+        ]
+
+    def __init__(self, dp, head_size, shared_size, refs):
+        self.dp, self.head_size, self.shared_size = dp, head_size, shared_size
+        self.hr, self.sr = slot_rows(head_size), slot_rows(shared_size)
+        self.fh, self.fs, self.wide, self.tall, self.tmp = refs
+        self.hp, self.used_h = head_places()
+        self.sp, self.used_s = shared_places()
+
+    def clear_unused(self):
         for g in range(2):
-            give(fh.at[g], hp[place], D, HF, 0, HF, wide, 0, g * HFP)
-            give(fh.at[g], hp[bplace], 1, HF, 0, HF, wide, 240, g * HFP)
-    for src, place, brow in ((dn1, "dn1", DOWNB_ONE), (dn2, "dn2", DOWNB_TWO)):
+            first = self.used_h // LANES // 8 * 8
+            count = self.fh.shape[1] - first
+            self.fh[g, pl.ds(first, count), :] = jnp.zeros((count, LANES), F32)
+        first = self.used_s // LANES // 8 * 8
+        count = self.fs.shape[0] - first
+        self.fs[pl.ds(first, count), :] = jnp.zeros((count, LANES), F32)
+
+    def head(self, g, place, rows, pitch, src, row0, lane0):
+        give(self.fh.at[g], self.hp[place], rows, pitch, 0, pitch, src, row0, lane0)
+
+    def shared(self, place, at, rows, pitch, col, src, row0, lane0):
+        give(self.fs, self.sp[place] + at, rows, pitch, col, D, src, row0, lane0)
+
+    def up(self, up, place, bias_place):
+        load_tiles(up, self.wide, 0.5)
+        for g in range(2):
+            self.head(g, place, D, HF, self.wide, 0, g * HFP)
+            self.head(g, bias_place, 1, HF, self.wide, 240, g * HFP)
+
+    def down(self, dn, place, row):
         for t in range(2):
-            tall[t] = 0.5 * src[pl.ds(t * LANES, LANES), :].T
+            self.tall[t] = (0.5 * dn[pl.ds(t * LANES, LANES), :]).astype(BF).T.astype(F32)
         for g in range(2):
-            give(fh.at[g], hp[place], HF, D, 0, D, tall, g * HFP, 0)
-        give(fs, sp["vec"] + brow * D, 1, D, 0, D, tall, HF, 0)
-    load_tiles(qkv, wide)
-    load_tiles(wo, tall)
-    for g in range(2):
-        for which, (place, bplace) in enumerate((("wq", "bq"), ("wk", None), ("wv", "bv"))):
-            lane0 = which * DP + g * LANES
-            give(fh.at[g], hp[place], D, HC, 0, HC, wide, 0, lane0)
-            if bplace:
-                give(fh.at[g], hp[bplace], 1, HC, 0, HC, wide, 240, lane0)
-        give(fh.at[g], hp["wo"], HC, D, 0, D, tall, g * LANES, 0)
-    give(fs, sp["vec"] + B_OUT * D, 1, D, 0, D, tall, MASK_LANE, 0)
-    load_tiles(p1, wide)
-    load_tiles(p2, tall)
-    for half in range(2):
-        give(fs, sp["p1"], D, 2 * D, half * D, D, wide, 0, half * DP)
-        give(fs, sp["pb1"] + half * D, 1, D, 0, D, wide, 240, half * DP)
-    give(fs, sp["p2"], D, D, 0, D, tall, 0, 0)
-    give(fs, sp["pb2"], 1, D, 0, D, tall, 240, 0)
-    load_tiles(vec, tall)
-    for row in range(10):
-        give(fs, sp["vec"] + row * D, 1, D, 0, D, tall, row, 0)
-    give(fs, sp["taps"], 16, D, 0, D, tall, TAPS, 0)
-    give(fs, sp["bg"], 1, D, 0, D, tall, BATCH_GAIN, 0)
-    give(fs, sp["bb"], 1, D, 0, D, tall, BATCH_BIAS, 0)
-    length = rel.shape[0] // HEADS
-    for n in range(HEADS):
-        total = jnp.zeros((8, 4 * LANES), F32)
-        for block in range(length // 8):
-            rows = rel[pl.ds(n * length + 8 * block, 8), :]
-            rows = jnp.concatenate([rows, jnp.zeros((8, 4 * LANES - length), F32)], 1)
-            total = total + pltpu.roll(rows, length - 8 - 8 * block, 1)
-        row = total[7:8]
-        for i in range(7):
-            row = row + pltpu.roll(total[i : i + 1], 7 - i, 1)
-        for t in range(4):
-            tmp[t, pl.ds(0, 1), :] = row[:, t * LANES : (t + 1) * LANES]
-        give(fh.at[n // 2], hp["rel"] + (n % 2) * KREL, 1, KREL, 0, KREL, tmp, 0, 0)
-
-    @pl.loop(0, dp)
-    def _(i):
+            self.head(g, place, HF, D, self.tall, g * HFP, 0)
+        self.shared("vec", row * D, 1, D, 0, self.tall, HF, 0)
+
+    def attention(self, qkv, wo, rel):
+        load_tiles(qkv, self.wide)
+        load_tiles(wo, self.tall)
+        length = rel.shape[0] // HEADS
         for g in range(2):
-            out[g, i, pl.ds(0, hr), :] = fh[g, pl.ds((i * head_size) // LANES, hr), :].astype(BF)
-            out[g, i, pl.ds(hr, sr), :] = fs[pl.ds(((2 * i + g) * shared_size) // LANES, sr), :].astype(BF)
-
-
-def flatten_grads(grads, dp, head_size, shared_size):
-    rows = slot_rows(head_size) + slot_rows(shared_size)
-    vm = pltpu.VMEM
-    scratch = (
-        vm((2, flat_rows(head_size * dp, head_size), LANES), F32),
-        vm((flat_rows(shared_size * 2 * dp, shared_size), LANES), F32),
-        vm((8, DP, LANES), F32),
-        vm((2, FFP, LANES), F32),
-        vm((4, 8, LANES), F32),
-    )
-    return vmem_call(
-        functools.partial(flatten_kernel, (dp, head_size, shared_size)),
-        jax.ShapeDtypeStruct((2, dp, rows, LANES), BF),
-        grads,
-        scratch,
-        "flatten_grads",
-    )
-
-
-def lane_mask():
-    return jnp.where(lane_iota((1, DP)) < D, 1.0, 0.0)
-
-
-def sigmoid(x):
-    return 0.5 * jnp.tanh(0.5 * x) + 0.5
+            for which, (place, bplace) in enumerate((("wq", "bq"), ("wk", None), ("wv", "bv"))):
+                lane0 = which * DP + g * LANES
+                self.head(g, place, D, HC, self.wide, 0, lane0)
+                if bplace:
+                    self.head(g, bplace, 1, HC, self.wide, 240, lane0)
+            self.head(g, "wo", HC, D, self.tall, g * LANES, 0)
+        for n in range(HEADS):
+            total = jnp.zeros((8, 4 * LANES), F32)
+            for block in range(length // 8):
+                rows = rel[pl.ds(n * length + 8 * block, 8), :]
+                rows = jnp.concatenate([rows, jnp.zeros((8, 4 * LANES - length), F32)], 1)
+                total = total + pltpu.roll(rows, length - 8 - 8 * block, 1)
+            row = total[7:8]
+            for i in range(7):
+                row = row + pltpu.roll(total[i : i + 1], 7 - i, 1)
+            for t in range(4):
+                self.tmp[t, pl.ds(0, 1), :] = row[:, t * LANES : (t + 1) * LANES]
+            give(self.fh.at[n // 2], self.hp["rel"] + (n % 2) * KREL, 1, KREL, 0, KREL, self.tmp, 0, 0)
+        self.shared("vec", B_OUT * D, 1, D, 0, self.tall, MASK_LANE, 0)
+
+    def points(self, p1, p2):
+        load_tiles(p1, self.wide)
+        load_tiles(p2, self.tall)
+        for half in range(2):
+            self.shared("p1", 0, D, 2 * D, half * D, self.wide, 0, half * DP)
+            self.shared("pb1", half * D, 1, D, 0, self.wide, 240, half * DP)
+        self.shared("p2", 0, D, D, 0, self.tall, 0, 0)
+        self.shared("pb2", 0, 1, D, 0, self.tall, 240, 0)
+
+    def vectors(self, vec, vec2):
+        for t in range(2):
+            cols = pl.ds(t * LANES, LANES)
+            self.tall[t, pl.ds(0, VEC_ROWS), :] = vec[:, cols] + vec2[:, cols]
+        for row in range(2, 10):
+            self.shared("vec", row * D, 1, D, 0, self.tall, row, 0)
+        self.shared("taps", 0, 16, D, 0, self.tall, TAPS, 0)
+        self.shared("bg", 0, 1, D, 0, self.tall, BATCH_GAIN, 0)
+        self.shared("bb", 0, 1, D, 0, self.tall, BATCH_BIAS, 0)
+
+    def first_norm(self, vec):
+        for t in range(2):
+            self.tall[t, pl.ds(0, 8), :] = vec[pl.ds(0, 8), pl.ds(t * LANES, LANES)]
+        for row in (FFA, FFA + 1):
+            self.shared("vec", row * D, 1, D, 0, self.tall, row, 0)
+
+    def slots(self, out, z, kind):
+        for i in range(4 * z, 4 * z + 4):
+            for g in range(2):
+                if kind == 0:
+                    out[g, i, pl.ds(0, self.hr), :] = self.fh[g, pl.ds(i * self.head_size // LANES, self.hr), :].astype(BF)
+                else:
+                    at = (2 * i + g) * self.shared_size // LANES
+                    out[g, i, pl.ds(self.hr, self.sr), :] = self.fs[pl.ds(at, self.sr), :].astype(BF)
+
+    def groups(self):
+        size = 4 * self.head_size
+        every = range(self.dp // 4)
+        one = [z for z in every if z * size >= self.hp["up2"] and (z + 1) * size <= self.hp["wq"]]
+        two = [z for z in every if z * size >= self.hp["dn1"] and z not in one]
+        late = [z for z in every if 8 * z * self.shared_size < 2 * D]
+        return one, two, [z for z in every if z not in one and z not in two], [z for z in every if z not in late], late
 
 
 def row_sum(x):
     return jnp.sum(x, -1, keepdims=True)
 
 
+def halves(x):
+    return x[:, :LANES], x[:, LANES:]
+
+
+def both(lo, hi):
+    return jnp.concatenate([lo, hi], 1)
+
+
 def norm(x, gain, bias):
-    centre = (x - row_sum(x) * (1.0 / D)) * lane_mask()
-    inv = lax.rsqrt(row_sum(centre * centre) * (1.0 / D) + NORM_EPS)
-    scaled = centre * inv
-    return scaled * gain + bias, scaled, inv
-
-
-def keep_norm(scaled, inv):
-    return jnp.where(lane_iota(scaled.shape) == DP - 1, inv, scaled)
+    lane = lane_iota((1, LANES))
+    lo, hi = halves(x)
+    mean = row_sum(lo + hi) * (1.0 / D)
+    lo = lo - mean
+    hi = jnp.where(lane < D - LANES, hi - mean, 0.0)
+    inv = lax.rsqrt(row_sum(lo * lo + hi * hi) * (1.0 / D) + NORM_EPS)
+    lo, hi = lo * inv, hi * inv
+    return both(lo, hi) * gain + bias, both(lo, jnp.where(lane == LANES - 1, inv, hi))
 
 
 def norm_grad(grad, kept, gain):
@@ -721,22 +787,28 @@
     inv = kept[:, DP - 1 :]
     first = row_sum(dg) * (1.0 / D)
     second = row_sum(dg * kept) * (1.0 / D)
-    return inv * (dg - first - kept * second) * lane_mask()
-
-
-def add_rows(ref, row, value):
-    ref[pl.ds(row, 1), :] += jnp.sum(value, 0, keepdims=True)
-
-
-def norm_param_grads(ref, row, grad, kept):
-    add_rows(ref, row, grad * kept)
-    add_rows(ref, row + 1, grad)
-
-
-def silu_pair(u):
-    s = sigmoid(u)
-    h = u * s
-    return h, s + h * (1.0 - s)
+    return inv * (dg - first - kept * second)
+
+
+def fold_rows(x):
+    return jnp.sum(x.reshape(x.shape[0] // 8, 8, x.shape[1]), 0)
+
+
+def norm_param_grads(acc, row, grad, kept):
+    acc[row] += fold_rows(grad * kept)
+    acc[row + 1] += fold_rows(grad)
+
+
+def settle(acc, out):
+    for row in range(acc.shape[0]):
+        out[pl.ds(row, 1), :] = jnp.sum(acc[row], 0, keepdims=True)
+
+
+def silu_pair(y):
+    p = jnp.tanh(y) + 1.0
+    h = (y * p).astype(BF)
+    p = p.astype(BF)
+    return h, p + h * (2.0 - p)
 
 
 def widen(x):
@@ -744,13 +816,9 @@
     return jnp.concatenate([x.astype(F32), jnp.zeros((rows, DP - D), F32)], 1)
 
 
-def head_masks():
-    lane = lane_iota((1, DP))
-    out = []
-    for n in range(HEADS):
-        first = (n // 2) * LANES + (n % 2) * HD
-        out.append((lane >= first) & (lane < first + HD))
-    return out
+def head_lanes():
+    lane = lane_iota((1, LANES))
+    return lane < HD, (lane >= HD) & (lane < 2 * HD), lane == MASK_LANE
 
 
 def valid_rows(lengths, at, length):
@@ -778,54 +846,48 @@
         return vec[pl.ds(row, 1), :]
 
     x0 = widen(frames[...].reshape(tokens, D))
-    a, scaled, inv = norm(x0, v(FFA), v(FFA + 1))
+    a, kept1_o[...] = norm(x0, v(FFA), v(FFA + 1))
     a = a.astype(BF)
     a1_o[...] = a
-    kept1_o[...] = keep_norm(scaled, inv)
     h, slope = silu_pair(dot(a, up[...]))
-    h = h.astype(BF)
     h_o[...] = h
-    sp_o[...] = slope.astype(BF)
+    sp_o[...] = slope
     x1 = x0 + dot(h, dn[...])
-    a, scaled, inv = norm(x1, v(ATT), v(ATT + 1))
+    a, kept2_o[...] = norm(x1, v(ATT), v(ATT + 1))
     a = a.astype(BF)
     a2_o[...] = a
-    kept2_o[...] = keep_norm(scaled, inv)
     qkv = dot(a, wqkv[...])
-    lane = lane_iota((1, DP))
-    masks = head_masks()
+    first, second, special = head_lanes()
     for b in range(seqs):
         rows = pl.ds(b * length, length)
-        valid = valid_rows(lengths, first_seq + b, length)
-        part = qkv[b * length : (b + 1) * length]
-        q = (part[:, :DP] * (SCALE * LOG2E)).astype(BF)
-        k = part[:, DP : 2 * DP]
-        k = jnp.where(lane == MASK_LANE, jnp.where(valid, 0.0, NEG), k).astype(BF)
-        vv = part[:, 2 * DP :].astype(BF)
-        qkv_o[rows, pl.ds(0, DP)] = q
-        qkv_o[rows, pl.ds(DP, DP)] = k
-        qkv_o[rows, pl.ds(2 * DP, DP)] = vv
-        zero = jnp.zeros_like(q)
-        mixed = jnp.zeros((length, DP), F32)
-        shares = jnp.zeros((length, DP), F32)
-        for n in range(HEADS):
-            qm = jnp.where(masks[n] | (lane == MASK_LANE), q, zero)
-            s = dot_t(qm, k) + rel[n]
+        fence = jnp.where(valid_rows(lengths, first_seq + b, length), 0.0, NEG)
+        for g in range(2):
+            def piece(which):
+                at = which * DP + g * LANES
+                return qkv[b * length : (b + 1) * length, at : at + LANES]
+
+            q = (piece(0) * (SCALE * LOG2E)).astype(BF)
+            k = jnp.where(special, fence, piece(1)).astype(BF)
+            vv = piece(2).astype(BF)
+            qkv_o[rows, pl.ds(g * LANES, LANES)] = q
+            qkv_o[rows, pl.ds(DP + g * LANES, LANES)] = k
+            qkv_o[rows, pl.ds(2 * DP + g * LANES, LANES)] = vv
+            zero = jnp.zeros_like(q)
+            pair = jnp.concatenate([jnp.where(first | special, q, zero), jnp.where(second | special, q, zero)], 0)
+            at = pl.ds(2 * g * length, 2 * length)
+            s = dot_t(pair, k) + rel[at, :]
             e = jnp.exp2(s - jnp.max(s, -1, keepdims=True)).astype(BF)
-            e_o[b, pl.ds(n * length, length), :] = e
+            e_o[b, at, :] = e
             o = dot(e, vv)
             r = 1.0 / o[:, MASK_LANE : MASK_LANE + 1]
-            here = masks[n] | (lane == MASK_LANE) if n == 0 else masks[n]
-            shares = jnp.where(here, r, shares)
-            mixed = jnp.where(here, o, mixed)
-        rl_o[rows, :] = shares
-        m_o[rows, :] = (mixed * shares).astype(BF)
+            shares = jnp.where(second, r[length:], r[:length])
+            rl_o[rows, pl.ds(g * LANES, LANES)] = shares
+            m_o[rows, pl.ds(g * LANES, LANES)] = (jnp.where(second, o[length:], o[:length]) * shares).astype(BF)
     x2 = x1 + dot(m_o[...], wo[...])
     x2_o[...] = x2
-    a, scaled, inv = norm(x2, v(CNV), v(CNV + 1))
+    a, kept3_o[...] = norm(x2, v(CNV), v(CNV + 1))
     a = a.astype(BF)
     a3_o[...] = a
-    kept3_o[...] = keep_norm(scaled, inv)
     e = dot(a, p1[...])
     half = KW // 2
 
@@ -840,7 +902,7 @@
         rows = pl.ds(b * length, length)
         valid = jnp.where(valid_rows(lengths, first_seq + b, length), 1.0, 0.0)
         linear = e[b * length : (b + 1) * length, :DP]
-        gate = sigmoid(e[b * length : (b + 1) * length, DP:])
+        gate = 0.5 * jnp.tanh(0.5 * e[b * length : (b + 1) * length, DP:]) + 0.5
         f1 = gate * valid
         gl = linear * f1
         f1_o[rows, :] = f1.astype(BF)
@@ -897,63 +959,75 @@
 def phase_b_kernel(
     seqs, keep, w, x2, cotangent, p2, up, dn, vec,
     out_o, dy_o, dx3_o, dup_o, ddn_o, dp2_o, vec_o, keep_o,
-    sums_o, inbox, ss, rs,
+    acc, a_all, du_all, do_all, h_all, hc_all, dc_all, sums_o, inbox, ss, rs,
 ):
     step = pl.program_id(0)
     total = inbox.shape[0]
     length = cotangent.shape[1]
     tokens = seqs * length
+    at = pl.ds(pl.multiple_of(step * tokens, tokens), tokens)
 
     @pl.when(step == 0)
     def _():
         greet_all(total)
-        for ref in (dup_o, ddn_o, dp2_o, vec_o, sums_o):
+        for ref in (dup_o, ddn_o, dp2_o, acc):
             ref[...] = jnp.zeros(ref.shape, F32)
 
     def v(row):
         return vec[pl.ds(row, 1), :]
 
-    z = (w[...] - keep[pl.ds(0, 1), :]) * keep[pl.ds(1, 1), :]
-    hc, slope_c = silu_pair(z * v(BATCH_GAIN) + v(BATCH_BIAS))
-    hc = hc.astype(BF)
+    mean, inv_batch = keep[pl.ds(0, 1), :], keep[pl.ds(1, 1), :]
+    z = (w[...] - mean) * inv_batch
+    hc, slope_c = silu_pair(z * (0.5 * v(BATCH_GAIN)) + 0.5 * v(BATCH_BIAS))
     x3 = x2[...] + dot(hc, p2[...])
-    a, scaled, inv = norm(x3, v(FFB), v(FFB + 1))
+    a, kept = norm(x3, v(FFB), v(FFB + 1))
     a = a.astype(BF)
-    kept = keep_norm(scaled, inv)
     h, slope = silu_pair(dot(a, up[...]))
-    h = h.astype(BF)
-    slope = slope.astype(BF)
     x4 = x3 + dot(h, dn[...])
-    final, scaled, inv = norm(x4, v(OUT), v(OUT + 1))
+    final, kept4 = norm(x4, v(OUT), v(OUT + 1))
     out_o[...] = final[:, :D].astype(BF).reshape(seqs, length, D)
     g = widen(cotangent[...].reshape(tokens, D))
-    kept4 = keep_norm(scaled, inv)
-    norm_param_grads(vec_o, OUT, g, kept4)
+    norm_param_grads(acc, OUT, g, kept4)
     dx4 = norm_grad(g, kept4, v(OUT))
     do = dx4.astype(BF)
-    ddn_o[...] += t_dot(do, h)
-    du = (dot_t(do, dn[...]) * slope.astype(F32)).astype(BF)
-    dup_o[...] += t_dot(a, du)
+    do_all[at, :] = do
+    h_all[at, :] = h
+    du = dot_t(do, dn[...]).astype(BF) * slope
+    a_all[at, :] = a
+    du_all[at, :] = du
     da = dot_t(du, up[...])
-    norm_param_grads(vec_o, FFB, da, kept)
+    norm_param_grads(acc, FFB, da, kept)
     dx3 = dx4 + norm_grad(da, kept, v(FFB))
     dx3_o[...] = dx3
     dc = dx3.astype(BF)
-    dp2_o[...] += t_dot(hc, dc)
-    dy = dot_t(dc, p2[...]) * slope_c
+    hc_all[at, :] = hc
+    dc_all[at, :] = dc
+    dy = dot_t(dc, p2[...]) * slope_c.astype(F32)
     dy_o[...] = dy
-    first = jnp.sum(dy, 0, keepdims=True)
-    second = jnp.sum(dy * z, 0, keepdims=True)
-    vec_o[pl.ds(BATCH_BIAS, 1), :] += first
-    vec_o[pl.ds(BATCH_GAIN, 1), :] += second
-    for t in range(2):
-        cols = slice(t * LANES, (t + 1) * LANES)
-        sums_o[pl.ds(t, 1), :] += first[:, cols]
-        sums_o[pl.ds(2 + t, 1), :] += second[:, cols]
+    acc[BATCH_BIAS] += fold_rows(dy)
+    acc[BATCH_GAIN] += fold_rows(dy * z)
+
+    @pl.when(step == pl.num_programs(0) - 1)
+    def _():
+        acc[BATCH_BIAS] *= 0.5
+        acc[BATCH_GAIN] *= 0.5
+        settle(acc, vec_o)
+        for row, source in ((0, BATCH_BIAS), (2, BATCH_GAIN)):
+            line = vec_o[pl.ds(source, 1), :]
+            for t in range(2):
+                sums_o[pl.ds(row + t, 1), :] = line[:, t * LANES : (t + 1) * LANES]
 
     @pl.when(step == pl.num_programs(0) - 1)
     def _():
         share_start(total, sums_o, inbox, ss, rs)
+
+        @pl.loop(0, pl.num_programs(0))
+        def _(k):
+            at = pl.ds(pl.multiple_of(k * tokens, tokens), tokens)
+            ddn_o[...] += t_dot(do_all[at, :], h_all[at, :])
+            dup_o[...] += t_dot(a_all[at, :], du_all[at, :])
+            dp2_o[...] += t_dot(hc_all[at, :], dc_all[at, :])
+
         share_finish(total, sums_o, inbox, ss, rs)
         sums = jnp.sum(inbox[...], 0)
         keep_o[...] = keep[...]
@@ -962,104 +1036,174 @@
 
 
 def phase_c_kernel(
-    seqs, lengths, keep, w, dy, dx3, gl, f1, f2, a3, kept3, qkv, e_all, rl, m, a2, kept2, h, slope, a1, kept1,
-    p1, wo, wqkv, dn, up, vec,
-    dx0_o, dp1_o, dwo_o, dqkv_o, dup_o, ddn_o, vec_o, rel_o,
-    padw, padg, grads,
+    seqs, steps, sizes, lengths, keep, w, dy, dx3, gl, f1, f2, a3, kept3, qkv, e_all, rl, m, a2, kept2, h, slope, a1, kept1,
+    p1, wo, wqkv, dn, up, vec, dup2, ddn2, dp2, vec2,
+    dx0_o, sum_o,
+    dp1_o, dwo_o, dqkv_o, dup_o, ddn_o, vec_o, rel_o, dx1_buf, mine,
+    acc, padw, padg, grads, *refs,
 ):
     step = pl.program_id(0)
     length = dx0_o.shape[1]
-    tokens = seqs * length
-    first_seq = lax.axis_index("head") * (seqs * pl.num_programs(0)) + step * seqs
+    flat = Flat(*sizes, refs[:5])
+    nz = sizes[0] // 4
+    scatter = Scatter(nz, flat.hr, flat.sr, mine, refs[5:])
+    one, two, rest, shared_two, shared_rest = flat.groups()
+
+    @pl.when(step == 0)
+    def _():
+        greet(nz, scatter.me, scatter.core, scatter.zc, scatter.yc, scatter.xc)
+        for ref in (dp1_o, dwo_o, dqkv_o, dup_o, ddn_o, acc, rel_o, padw, padg):
+            ref[...] = jnp.zeros(ref.shape, F32)
+        flat.clear_unused()
+        flat.up(dup2, "up2", "upb2")
+        flat.down(ddn2, "dn2", DOWNB_TWO)
+        for z in one:
+            flat.slots(scatter.g, z, 0)
+        greeted(nz)
+        for z in one:
+            scatter.stage_core(z, 0)
+
+    @pl.when(step < steps)
+    def _():
+        phase_c_first(
+            seqs, step, steps, length, lengths, keep, w, dy, dx3, gl, f1, f2, a3, kept3, qkv, e_all, rl, m, a2, kept2,
+            h, p1, wo, wqkv, vec, dp1_o, dwo_o, dqkv_o, ddn_o, rel_o, dx1_buf, acc, padw, padg, grads,
+        )
+
+    @pl.when(step == steps)
+    def _():
+        flat.attention(dqkv_o, dwo_o, rel_o)
+        flat.down(ddn_o, "dn1", DOWNB_ONE)
+        for z in two:
+            flat.slots(scatter.g, z, 0)
+            scatter.stage_core(z, 0)
+        settle(acc, vec_o)
+        flat.points(dp1_o, dp2)
+        flat.vectors(vec_o, vec2)
+        for z in shared_two:
+            flat.slots(scatter.g, z, 1)
+            scatter.stage_core(z, 1)
+
+    @pl.when(step >= steps)
+    def _():
+        at = pl.ds(pl.multiple_of((step - steps) * (seqs * length), seqs * length), seqs * length)
+        dx1 = dx1_buf[at, :]
+        du = dot_t(dx1.astype(BF), dn[...]).astype(BF) * slope[...]
+        dup_o[...] += t_dot(a1[...], du)
+        da = dot_t(du, up[...])
+        norm_param_grads(acc, FFA, da, kept1[...])
+        dx0 = dx1 + norm_grad(da, kept1[...], vec[pl.ds(FFA, 1), :])
+        dx0_o[...] = dx0[:, :D].reshape(seqs, length, D)
+
+    stages = (scatter.stage_first, scatter.stage_second, scatter.stage_third)
+    for at, heads, shared in (((1, 3, 5), one, []), ((steps + AT_A, steps + AT_B), two, shared_two)):
+        for when, stage in zip(at, stages):
+            @pl.when(step == when)
+            def _():
+                for z in heads:
+                    stage(z, 0)
+                for z in shared:
+                    stage(z, 1)
+
+    @pl.when(step == 2 * steps - 1)
+    def _():
+        flat.up(dup_o, "up1", "upb1")
+        for z in rest:
+            flat.slots(scatter.g, z, 0)
+            scatter.stage_core(z, 0)
+        settle(acc, vec_o)
+        flat.first_norm(vec_o)
+        for z in shared_rest:
+            flat.slots(scatter.g, z, 1)
+            scatter.stage_core(z, 1)
+        for z in two:
+            scatter.stage_third(z, 0)
+        for z in shared_two:
+            scatter.stage_third(z, 1)
+        for stage in stages:
+            for z in rest:
+                stage(z, 0)
+            for z in shared_rest:
+                stage(z, 1)
+        scatter.finish(sum_o)
+
+
+def phase_c_first(
+    seqs, step, steps, length, lengths, keep, w, dy, dx3, gl, f1, f2, a3, kept3, qkv, e_all, rl, m, a2, kept2,
+    h, p1, wo, wqkv, vec, dp1_o, dwo_o, dqkv_o, ddn_o, rel_o, dx1_buf, acc, padw, padg, grads,
+):
+    first_seq = lax.axis_index("head") * (seqs * steps) + step * seqs
     half = KW // 2
 
     def v(row):
         return vec[pl.ds(row, 1), :]
 
-    @pl.when(step == 0)
-    def _():
-        for ref in (dp1_o, dwo_o, dqkv_o, dup_o, ddn_o, vec_o, rel_o, padw, padg):
-            ref[...] = jnp.zeros(ref.shape, F32)
-
-    gain = v(BATCH_GAIN)
-    inv_batch = keep[pl.ds(1, 1), :]
-    mean = keep[pl.ds(0, 1), :]
-    plain = gain * keep[pl.ds(3, 1), :] / keep[pl.ds(2, 1), :]
-    cross = gain * keep[pl.ds(4, 1), :] / keep[pl.ds(2, 1), :]
+    mean, inv_batch, count = (keep[pl.ds(row, 1), :] for row in range(3))
+    scale = v(BATCH_GAIN) * inv_batch
+    cross = inv_batch * scale * keep[pl.ds(4, 1), :] / count
+    plain = scale * keep[pl.ds(3, 1), :] / count - mean * cross
+    scale = 0.5 * scale
     for b in range(seqs):
         rows = pl.ds(b * length, length)
         valid = jnp.where(valid_rows(lengths, first_seq + b, length), 1.0, 0.0)
-        z = (w[rows, :] - mean) * inv_batch
-        dw = inv_batch * (dy[rows, :] * gain - valid * (plain + z * cross))
-        add_rows(vec_o, DEPTH_BIAS, dw)
+        dw = dy[rows, :] * scale - valid * (plain + w[rows, :] * cross)
+        acc[DEPTH_BIAS] += fold_rows(dw)
         for t in range(2):
             cols = pl.ds(t * LANES, LANES)
             here = dw[:, t * LANES : (t + 1) * LANES]
             padw[b, t, pl.ds(8, length), :] = here
             padg[b, t, pl.ds(8, length), :] = gl[rows, cols].astype(F32)
-            acc = jnp.zeros((length, LANES), F32)
+            total = jnp.zeros((length, LANES), F32)
             for r in range(KW):
-                acc = acc + padw[b, t, pl.ds(8 + half - r, length), :] * vec[pl.ds(TAPS + r, 1), cols]
+                total = total + padw[b, t, pl.ds(8 + half - r, length), :] * vec[pl.ds(TAPS + r, 1), cols]
                 tap = here * padg[b, t, pl.ds(8 - half + r, length), :]
-                vec_o[pl.ds(TAPS + r, 1), cols] += jnp.sum(tap, 0, keepdims=True)
-            grads[rows, cols] = (acc * f1[rows, cols].astype(F32)).astype(BF)
-            grads[rows, pl.ds(DP + t * LANES, LANES)] = (acc * f2[rows, cols].astype(F32)).astype(BF)
+                acc[TAPS + r, :, cols] += fold_rows(tap)
+            grads[rows, cols] = (total * f1[rows, cols].astype(F32)).astype(BF)
+            grads[rows, pl.ds(DP + t * LANES, LANES)] = (total * f2[rows, cols].astype(F32)).astype(BF)
     de = grads[:, pl.ds(0, 2 * DP)]
     dp1_o[...] += t_dot(a3[...], de)
     da = dot_t(de, p1[...])
-    norm_param_grads(vec_o, CNV, da, kept3[...])
+    norm_param_grads(acc, CNV, da, kept3[...])
     dx2 = dx3[...] + norm_grad(da, kept3[...], v(CNV))
     db = dx2.astype(BF)
     dwo_o[...] += t_dot(m[...], db)
     dm = dot_t(db, wo[...])
-    lane = lane_iota((1, DP))
-    masks = head_masks()
-    wide_rows = lax.broadcasted_iota(jnp.int32, (DP, LANES), 0)
-    wide_lane = lane_iota((DP, LANES))
+    first, second, special = head_lanes()
+    source = lax.broadcasted_iota(jnp.int32, (LANES, 2 * LANES), 0)
+    target = lane_iota((LANES, 2 * LANES)) // LANES
+    spread = jnp.where((source >= target * HD) & (source < (target + 1) * HD), 1.0, 0.0).astype(BF)
     for b in range(seqs):
         rows = pl.ds(b * length, length)
-        q = qkv[rows, pl.ds(0, DP)]
-        k = qkv[rows, pl.ds(DP, DP)]
-        vv = qkv[rows, pl.ds(2 * DP, DP)]
-        dmb = (dm[b * length : (b + 1) * length] * rl[rows, :]).astype(BF)
-        product = (dmb.astype(F32) * m[rows, :].astype(F32)).astype(BF)
-        zero = jnp.zeros_like(q)
-        dq = jnp.zeros((length, DP), F32)
-        dk = jnp.zeros((length, DP), F32)
-        dv = jnp.zeros((length, DP), F32)
-        for n in range(HEADS):
-            first = (n // 2) * LANES + (n % 2) * HD
-            pick = (wide_rows >= first) & (wide_rows < first + HD) & (wide_lane > MASK_LANE) & (wide_lane < MASK_LANE + 3)
-            level = dot(product, jnp.where(pick, -1.0, 0.0).astype(BF))
-            high = level.astype(BF)
-            low = (level - high.astype(F32)).astype(BF)
-            side = jnp.where(lane_iota((1, LANES)) == MASK_LANE + 1, high, low)
-            dmm = jnp.where(masks[n], dmb, zero)
-            dmm = jnp.concatenate(
-                [jnp.where(lane_iota((1, LANES)) > MASK_LANE, side, dmm[:, :LANES]), dmm[:, LANES:]], 1
-            )
-            e = e_all[b, pl.ds(n * length, length), :]
-            ds = (e.astype(F32) * dot_t(dmm, vv)).astype(BF)
-            rel_o[pl.ds(n * length, length), :] += ds.astype(F32)
-            dq = jnp.where(masks[n], dot(ds, k), dq)
-            dk = dk + t_dot(ds, jnp.where(masks[n], q, zero))
-            dv = dv + t_dot(e, dmm)
-        grads[rows, pl.ds(0, DP)] = (dq * SCALE).astype(BF)
-        grads[rows, pl.ds(DP, DP)] = (dk * LN2).astype(BF)
-        grads[rows, pl.ds(2 * DP, DP)] = dv.astype(BF)
+        for g in range(2):
+            cols = pl.ds(g * LANES, LANES)
+            q = qkv[rows, cols]
+            k = qkv[rows, pl.ds(DP + g * LANES, LANES)]
+            vv = qkv[rows, pl.ds(2 * DP + g * LANES, LANES)]
+            dmb = (dm[b * length : (b + 1) * length, g * LANES : (g + 1) * LANES] * rl[rows, cols]).astype(BF)
+            level = dot(dmb * m[rows, cols], spread)
+            level = jnp.concatenate([level[:, :LANES], level[:, LANES:]], 0)
+            zero = jnp.zeros_like(q)
+            dm_pair = jnp.concatenate([jnp.where(first, dmb, zero), jnp.where(second, dmb, zero)], 0)
+            q_pair = jnp.concatenate([jnp.where(first, q, zero), jnp.where(second, q, zero)], 0)
+            at = pl.ds(2 * g * length, 2 * length)
+            e = e_all[b, at, :]
+            dp = dot_t(dm_pair, vv)
+            ds = e.astype(F32) * (dp - jnp.concatenate([level, level[:, : length - LANES]], 1))
+            rel_o[at, :] += ds
+            ds = ds.astype(BF)
+            dq = dot(ds, k)
+            dq = jnp.where(second, dq[length:], dq[:length])
+            grads[rows, cols] = (dq * SCALE).astype(BF)
+            grads[rows, pl.ds(DP + g * LANES, LANES)] = (t_dot(ds, q_pair) * LN2).astype(BF)
+            grads[rows, pl.ds(2 * DP + g * LANES, LANES)] = t_dot(e, dm_pair).astype(BF)
     dqkv = grads[...]
     dqkv_o[...] += t_dot(a2[...], dqkv)
     da = dot_t(dqkv, wqkv[...])
-    norm_param_grads(vec_o, ATT, da, kept2[...])
+    norm_param_grads(acc, ATT, da, kept2[...])
     dx1 = dx2 + norm_grad(da, kept2[...], v(ATT))
-    do = dx1.astype(BF)
-    ddn_o[...] += t_dot(do, h[...])
-    du = (dot_t(do, dn[...]) * slope[...].astype(F32)).astype(BF)
-    dup_o[...] += t_dot(a1[...], du)
-    da = dot_t(du, up[...])
-    norm_param_grads(vec_o, FFA, da, kept1[...])
-    dx0 = dx1 + norm_grad(da, kept1[...], v(FFA))
-    dx0_o[...] = dx0[:, :D].reshape(seqs, length, D)
+    at = pl.ds(pl.multiple_of(step * (seqs * length), seqs * length), seqs * length)
+    dx1_buf[at, :] = dx1
+    ddn_o[...] += t_dot(dx1.astype(BF), h[...])
 
 
 def layer_call(body, steps, ins, outs, scratch, name, collective_id=None):
@@ -1069,6 +1213,10 @@
             return pl.BlockSpec(memory_space=pltpu.SMEM)
         if kind == "tile":
             return pl.BlockSpec(shape, lambda i: (i,) + (0,) * (len(shape) - 1))
+        if kind == "early":
+            return pl.BlockSpec(shape, lambda i: (jnp.minimum(i, steps // 2 - 1),) + (0,) * (len(shape) - 1))
+        if kind == "late":
+            return pl.BlockSpec(shape, lambda i: (jnp.maximum(i - steps // 2, 0),) + (0,) * (len(shape) - 1))
         return pl.BlockSpec(shape, lambda i: (0,) * len(shape))
 
     arrays = [a for _, _, a in ins]
@@ -1089,25 +1237,27 @@
     )(*arrays)
 
 
-def tile_in(array, steps):
-    return ("tile", (array.shape[0] // steps,) + array.shape[1:], array)
+def tile_in(array, steps, kind="tile"):
+    return (kind, (array.shape[0] // steps,) + array.shape[1:], array)
 
 
 def whole_in(array):
     return ("whole", array.shape, array)
 
 
-def tile_out(steps, shape, dtype):
-    return ("tile", (shape[0] // steps,) + shape[1:], shape, dtype)
-
-
-def whole_out(shape):
-    return ("whole", shape, shape, F32)
+def tile_out(steps, shape, dtype, kind="tile"):
+    return (kind, (shape[0] // steps,) + shape[1:], shape, dtype)
+
+
+def whole_out(shape, dtype=F32):
+    return ("whole", shape, shape, dtype)
 
 
 SEQS_A = 2
 SEQS_B = 4
 SEQS_C = 2
+AT_A = 4
+AT_B = 7
 
 
 def per_device(
@@ -1148,7 +1298,7 @@
     )
     steps = seq_here // SEQS_B
     t = functools.partial(tile_out, steps)
-    layer_out, dy, dx3, dup2, ddn2, dp2, vec_b, keep = layer_call(
+    early, dy, dx3, dup2, ddn2, dp2, vec_b, keep = layer_call(
         functools.partial(phase_b_kernel, SEQS_B),
         steps,
         [whole_in(keep), tile_in(w, steps), tile_in(x2, steps), tile_in(cotangent, steps)]
@@ -1158,46 +1308,53 @@
             whole_out((DP, FFP)), whole_out((DP, FFP)), whole_out((DP, DP)), whole_out((VEC_ROWS, DP)),
             whole_out((8, DP)),
         ],
-        sharing,
+        [
+            vm((VEC_ROWS, 8, DP), F32), vm((tokens, DP), BF), vm((tokens, FFP), BF), vm((tokens, DP), BF),
+            vm((tokens, FFP), BF), vm((tokens, DP), BF), vm((tokens, DP), BF),
+        ]
+        + sharing,
         "phase_b",
         3,
     )
     steps = seq_here // SEQS_C
-    t = functools.partial(tile_out, steps)
-    input_grad, dp1, dwo, dqkv, dup1, ddn1, vec_c, rel_sum = layer_call(
-        functools.partial(phase_c_kernel, SEQS_C),
-        steps,
+    slot = (slot_rows(head_size), slot_rows(shared_size))
+    block = SEQS_C * length
+    input_grad, summed = layer_call(
+        functools.partial(phase_c_kernel, SEQS_C, steps, (dp, head_size, shared_size)),
+        2 * steps,
         [("smem", None, lengths), whole_in(keep)]
-        + [
-            tile_in(x, steps)
-            for x in (w, dy, dx3, gl, f1, f2, a3, kept3, qkv, e_all, rl, m, a2, kept2, h1, slope1, a1, kept1)
-        ]
-        + [whole_in(x) for x in (p1, wo, wqkv, dn1, up1, vec)],
+        + [tile_in(x, steps, "early") for x in (w, dy, dx3, gl, f1, f2, a3, kept3, qkv, e_all, rl, m, a2, kept2, h1)]
+        + [tile_in(x, steps, "late") for x in (slope1, a1, kept1)]
+        + [whole_in(x) for x in (p1, wo, wqkv, dn1, up1, vec, dup2, ddn2, dp2, vec_b)],
+        [tile_out(steps, (seq_here, length, D), F32, "late"), whole_out((rows, LANES))],
         [
-            t((seq_here, length, D), F32), whole_out((DP, 2 * DP)), whole_out((DP, DP)), whole_out((DP, 3 * DP)),
-            whole_out((DP, FFP)), whole_out((DP, FFP)), whole_out((VEC_ROWS, DP)), whole_out((HEADS * length, length)),
-        ],
-        [
+            vm((DP, 2 * DP), F32), vm((DP, DP), F32), vm((DP, 3 * DP), F32), vm((DP, FFP), F32), vm((DP, FFP), F32),
+            vm((VEC_ROWS, DP), F32), vm((HEADS * length, length), F32), vm((tokens, DP), F32), vm((rows, LANES), F32),
+            vm((VEC_ROWS, 8, DP), F32),
             vm((SEQS_C, 2, length + 16, LANES), F32),
             vm((SEQS_C, 2, length + 16, LANES), F32),
-            vm((SEQS_C * length, 3 * DP), BF),
-        ],
+            vm((block, 3 * DP), BF),
+        ]
+        + Flat.scratch(dp, head_size, shared_size)
+        + Scatter.scratch(dp, *slot),
         "phase_c",
+        4,
     )
-    grads = flatten_grads((dup1, ddn1, dup2, ddn2, dqkv, dwo, dp1, dp2, vec_b + vec_c, rel_sum), dp, head_size, shared_size)
-    summed = scatter_all(grads, 4)
     h_shape, s_shape = head_params.shape, shared_params.shape
-
-    def s(shape, dtype=F32):
-        return jax.ShapeDtypeStruct(shape, dtype)
-
-    updated = vmem_call(
+    steps = 4
+    return layer_call(
         adam_kernel,
-        (s(h_shape), s(h_shape), s(h_shape), s(h_shape, BF), s(s_shape), s(s_shape), s(s_shape), s(s_shape, BF)),
-        (summed, head_params, head_first, head_second, shared_params, shared_first, shared_second),
-        name="adam",
+        steps,
+        [tile_in(x, steps) for x in (early, input_grad)]
+        + [whole_in(x) for x in (summed, head_params, head_first, head_second, shared_params, shared_first, shared_second)],
+        [tile_out(steps, early.shape, BF), tile_out(steps, early.shape, F32)]
+        + [whole_out(h_shape)] * 3
+        + [whole_out(h_shape, BF)]
+        + [whole_out(s_shape)] * 3
+        + [whole_out(s_shape, BF)],
+        [],
+        "adam",
     )
-    return (layer_out, input_grad) + tuple(updated)
 
 
 def solution(mesh):

time: 214 us -> 196 us (0.916)
  Pallas kernels: 206 us -> 192 us
  local copies, waits for them, and re-layouts: 6.01 us -> 2.42 us
    pallas_call x1 -> x0, Pallas kernels: 22.9 us -> none  [scatter_all(): pl.pallas_call(functools.partial(scatter_kernel, nz), out_shape=jax.Shape...]
    pallas_call x3 -> x4, Pallas kernels: 139 us -> 160 us  [layer_call(): pl.pallas_call(body, grid=(steps,), out_shape=tuple((jax.ShapeDtypeStruct...]
    pallas_call x4 -> x2, Pallas kernels: 19.5 us -> 8.83 us  [vmem_call(): pl.pallas_call(body, out_shape=outs, in_specs=[pl.BlockSpec(memory_space=...]
    unnamed x13 -> x4, local copies, waits for them, and re-layouts: 6.01 us -> 2.42 us
where the time goes in v3:
time: 196 us
  Pallas kernels  192 us (98%)
  local copies, waits for them, and re-layouts  2.42 us (1%)
    pallas_call x4, Pallas kernels, layer_call(): pl.pallas_call(body, grid=(steps,), out_shape=tuple((jax.ShapeDtypeStruct...  160 us
    pallas_call x1, Pallas kernels, gather_all(): pl.pallas_call(functools.partial(gather_kernel, nz), out_shape=jax.ShapeD...  23.9 us
    pallas_call x2, Pallas kernels, vmem_call(): pl.pallas_call(body, out_shape=outs, in_specs=[pl.BlockSpec(memory_space=...  8.83 us

profile of v3, /device:TPU:0, one launch (start us, length us, event | category | flops | bytes accessed | tf_op | source)
XLA Modules:
  0.0 195.6 jit_solution(15947883051967889628)
XLA Ops:
  0.6 1.7 align.1.src
  2.3 0.0 copy-start.1
  2.3 0.9 copy-done.1
  3.2 23.9 %gather_weights.1.got = bf16[16,2,336,128]{3,2,1,0:T(8,128)(2,1)S(1)} custom-call(bf16[336,128]{1,0:T(8,128)(2,1)S(1)} %copy-done.1), custom_call_target="tpu_custom_call" | custom-call | tf_op jit(solution)/shard_map/gather_weights/pallas_call | solution.py:127
  27.2 0.0 copy-start
  27.2 1.5 copy-done
  28.7 7.1 %make_weights.1 = (bf16[256,1024]{1,0:T(8,128)(2,1)}, bf16[1024,256]{1,0:T(8,128)(2,1)}, bf16[256,1024]{1,0:T(8,128)(2,1)}, bf16[1024,256]{1,0:T(8,128)(2,1)}, b...) custom-call(bf16[16,2,336,128]{3,2,1,0:T(8,128)(2,1)} %copy-done), custom_call_target="tpu_custom_call" | custom-call | tf_op jit(solution)/shard_map/make_weights/pallas_call | solution.py:380
  35.8 45.7 %phase_a.1 = (f32[3072,256]{1,0:T(8,128)}, bf16[3072,256]{1,0:T(8,128)(2,1)}, bf16[3072,1024]{1,0:T(8,128)(2,1)}, bf16[3072,1024]{1,0:T(8,128)(2,1)}, f32[3072,2...) custom-call(s32[32]{0:T(128)} %lengths.3, ...), custom_call_target="tpu_custom_call" | custom-call | tf_op jit(solution)/shard_map/phase_a/pallas_call | solution.py:1223
  81.5 28.5 %phase_b.1 = (bf16[16,192,240]{2,1,0:T(8,128)(2,1)}, f32[3072,256]{1,0:T(8,128)}, f32[3072,256]{1,0:T(8,128)}, f32[256,1024]{1,0:T(8,128)}, f32[256,1024]{1,0:T(...) custom-call(f32[8,256]{1,0:T(8,128)} %get-tuple-element.55.keep, ...), custom_call_target="tpu_custom_call" | custom-call | tf_op jit(solution)/shard_map/phase_b/pallas_call | solution.py:1223
  110.0 79.8 %phase_c.1 = (f32[16,192,240]{2,1,0:T(8,128)}, f32[336,128]{1,0:T(8,128)}) custom-call(s32[32]{0:T(128)} %lengths.3, f32[8,256]{1,0:T(8,128)} %get-tuple-element.62.keep, f32[3072,256]{1,0:T(8,128)} %get-tuple-element.56.w, f32[3072,256]{1,0:T(8,128)} %get-tuple-element.63.dy, f32[3072,256]{1,0:T(8,128)} %get-tuple-element.64.dx3, ...), custom_call_target="tpu_custom_call" | custom-call | tf_op jit(solution)/shard_map/phase_c/pallas_call | solution.py:1223
  189.7 5.7 %adam.1 = (bf16[16,192,240]{2,1,0:T(8,128)(2,1)}, f32[16,192,240]{2,1,0:T(8,128)}, f32[1,36123]{1,0:T(1,128)}, f32[1,36123]{1,0:T(1,128)}, f32[1,36123]{1,0:T(1,...) custom-call(bf16[16,192,240]{2,1,0:T(8,128)(2,1)} %get-tuple-element, ...), custom_call_target="tpu_custom_call" | custom-call | tf_op jit(solution)/shard_map/adam/pallas_call | solution.py:1223
Async XLA Ops:
  2.3 0.9 copy-start.1
  27.2 1.5 copy-start

commit v4 on v3

--- a/solution.py
+++ b/solution.py
@@ -57,13 +57,12 @@
     pl.semaphore_wait(pltpu.get_barrier_semaphore(), nz + 2)
 
 
-def gather_kernel(nz, src, out, sz, rz, s1, r1, s2, r2, sc, rc):
+def gather(nz, src, out, sems, merge):
+    sz, rz, s1, r1, s2, r2, sc, rc = sems
     rows = src.shape[0]
     row_a = up_to(rows // 2, 16)
     parts = (pl.ds(0, row_a), pl.ds(row_a, rows - row_a))
     me, core, zc, yc, xc = grid_place(nz)
-    greet(nz, me, core, zc, yc, xc)
-    greeted(nz)
     out[me, core] = src[...]
     y_peer = 4 * zc + 2 * (1 - yc) + xc
     x_peer = 4 * zc + 2 * yc + 1 - xc
@@ -98,6 +97,9 @@
             send(slot, p, s2.at[p, k, 0], r2.at[p, z, 0], seconds[p], core)
             send(slot, p, sc.at[p, k, 0], rc.at[p, z, 0], me, 1 - core)
     for k in range(nz):
+        for p in (0, 1):
+            merge(4 * zs[k] + here, core, p)
+    for k in range(nz):
         z = zs[k]
         for p in (0, 1):
             slot = 4 * z + first_here[p]
@@ -105,36 +107,34 @@
             send(slot, p, s2.at[p, k, 1], r2.at[p, z, 1], seconds[p], core)
             send(slot, p, sc.at[p, k, 1], rc.at[p, z, 1], me, 1 - core)
     for k in range(nz):
+        for p in (0, 1):
+            merge(4 * zs[k] + first_here[p], core, p)
+    for k in range(nz):
         z = zs[k]
-        for p in (0, 1):
-            for b in (0, 1):
+        for b in (0, 1):
+            for p in (0, 1):
                 slot = 4 * z + second_here[p][b]
                 arrived(slot, core, p, s2.at[p, k, b], r2.at[p, z, b])
                 send(slot, p, sc.at[p, k, 2 + b], rc.at[p, z, 2 + b], me, 1 - core)
+        for b in (0, 1):
+            for p in (0, 1):
+                merge(4 * z + second_here[p][b], core, p)
     for k in range(nz):
         z = zs[k]
         for p in (0, 1):
             for b, at in enumerate((here, first_here[p]) + second_here[p]):
                 arrived(4 * z + at, 1 - core, p, sc.at[p, k, b], rc.at[p, z, b])
+                merge(4 * z + at, 1 - core, p)
     for copy in pending:
         copy.wait_send()
 
 
-def gather_all(block, dp, collective_id):
-    rows = block.shape[0]
-    nz = dp // 4
+def gather_sems(nz):
     dma = pltpu.SemaphoreType.DMA
-    return pl.pallas_call(
-        functools.partial(gather_kernel, nz),
-        out_shape=jax.ShapeDtypeStruct((dp, 2, rows, LANES), block.dtype),
-        in_specs=[pl.BlockSpec(memory_space=pltpu.VMEM)],
-        out_specs=pl.BlockSpec(memory_space=pltpu.VMEM),
-        scratch_shapes=[dma((2, nz)), dma((2, nz)), dma((2, nz)), dma((2, nz)), dma((2, nz, 2)), dma((2, nz, 2)), dma((2, nz, 4)), dma((2, nz, 4))],
-        compiler_params=pltpu.CompilerParams(
-            collective_id=collective_id, has_side_effects=True, vmem_limit_bytes=40 << 20
-        ),
-        name="gather_weights",
-    )(block)
+    return [
+        dma((2, nz)), dma((2, nz)), dma((2, nz)), dma((2, nz)),
+        dma((2, nz, 2)), dma((2, nz, 2)), dma((2, nz, 4)), dma((2, nz, 4)),
+    ]
 
 
 class Scatter:
@@ -283,8 +283,11 @@
         )
 
 
+def greeted_all(total):
+    pl.semaphore_wait(pltpu.get_barrier_semaphore(), total - 1)
+
+
 def share_start(total, src, inbox, ss, rs):
-    pl.semaphore_wait(pltpu.get_barrier_semaphore(), total - 1)
     own = own_number()
     inbox[own] = src[...]
 
@@ -406,7 +409,7 @@
     return jnp.where(lane_iota(x.shape) < LANES - shift, rolled, after)
 
 
-def align_kernel(head_ref, shared_ref, out):
+def align(head_ref, shared_ref, out):
     head_size, shared_size = head_ref.shape[1], shared_ref.shape[0]
     hr, sr = slot_rows(head_size), slot_rows(shared_size)
     ho, so = own_offsets(head_size, shared_size)
@@ -535,113 +538,96 @@
     return up_to(total // LANES + slot_rows(size) + 16, 16)
 
 
-def weights_kernel(sizes, got, up1, dn1, up2, dn2, qkv, wo, p1, p2, vec, rel, fh, fs, wide, tall, tmp):
-    dp, head_size, shared_size = sizes
-    hr, sr = slot_rows(head_size), slot_rows(shared_size)
-    hp, _ = head_places()
-    sp, _ = shared_places()
-    row8 = lax.broadcasted_iota(jnp.int32, (8, LANES), 0)
-
-    def merge(flat, first_row, block):
-        head = flat[pl.ds(first_row, 8), :]
-        flat[pl.ds(first_row, 8), :] = block[:8] + jnp.where(row8 == 0, head, 0.0)
-        flat[pl.ds(first_row + 8, block.shape[0] - 8), :] = block[8:]
-
-    for g in range(2):
-        fh[g, pl.ds(0, 8), :] = jnp.zeros((8, LANES), F32)
-    fs[pl.ds(0, 8), :] = jnp.zeros((8, LANES), F32)
-
-    @pl.loop(0, dp)
-    def _(i):
-        for g in range(2):
-            merge(fh.at[g], (i * head_size) // LANES, got[i, g, pl.ds(0, hr), :].astype(F32))
-        for g in range(2):
-            merge(fs, ((2 * i + g) * shared_size) // LANES, got[i, g, pl.ds(hr, sr), :].astype(F32))
-
-    lane = lane_iota((1, LANES))
-
-    def clear(tiles, count, row, size):
+class Weights:
+    def __init__(self, dp, head_size, shared_size, got, refs):
+        self.dp, self.head_size, self.shared_size, self.got = dp, head_size, shared_size, got
+        self.hr, self.sr = slot_rows(head_size), slot_rows(shared_size)
+        self.fh, self.fs, self.wide, self.tall, self.tmp = refs
+        self.hp, _ = head_places()
+        self.sp, _ = shared_places()
+
+    def clear_flat(self):
+        self.fh[...] = jnp.zeros(self.fh.shape, F32)
+        self.fs[...] = jnp.zeros(self.fs.shape, F32)
+
+    def merge(self, slot, core, p):
+        rows = self.hr + self.sr
+        cut = up_to(rows // 2, 16)
+        first = (slot * self.head_size) // LANES
+        low, high = ((0, min(cut, self.hr)), (min(cut, self.hr), self.hr))[p]
+        if high > low:
+            at = pl.ds(first + low, high - low)
+            self.fh[core, at, :] += self.got[slot, core, pl.ds(low, high - low), :].astype(F32)
+        low, high = ((self.hr, max(cut, self.hr)), (max(cut, self.hr), rows))[p]
+        if high > low:
+            at = pl.ds(((2 * slot + core) * self.shared_size) // LANES + low - self.hr, high - low)
+            self.fs[at, :] += self.got[slot, core, pl.ds(low, high - low), :].astype(F32)
+
+    def clear(self, tiles, count, row, size):
         for t in range(count):
             tiles[t, pl.ds(row, size), :] = jnp.zeros((size, LANES), F32)
 
-    def patch(tiles, tile, row, where, value):
+    def patch(self, tiles, tile, row, where, value):
         part = tiles[tile, pl.ds(row, 1), :]
         tiles[tile, pl.ds(row, 1), :] = jnp.where(where, value, part)
 
-    for dst_ref, place, bplace in ((up1, "up1", "upb1"), (up2, "up2", "upb2")):
-        clear(wide, 8, 240, 16)
+    def ffn(self, up, dn, up_place, bias_place, dn_place, row):
+        wide, tall, hp = self.wide, self.tall, self.hp
+        self.clear(wide, 8, 240, 16)
         for g in range(2):
-            take(fh.at[g], hp[place], D, HF, 0, HF, wide, 0, g * HFP)
-            take(fh.at[g], hp[bplace], 1, HF, 0, HF, wide, 240, g * HFP)
-        patch(wide, 3, 240, lane == HF - 3 * LANES, UNIT)
-        spill(wide, DP, dst_ref, 0.5)
-    for dst_ref, place, brow in ((dn1, "dn1", DOWNB_ONE), (dn2, "dn2", DOWNB_TWO)):
+            take(self.fh.at[g], hp[up_place], D, HF, 0, HF, wide, 0, g * HFP)
+            take(self.fh.at[g], hp[bias_place], 1, HF, 0, HF, wide, 240, g * HFP)
+        self.patch(wide, 3, 240, lane_iota((1, LANES)) == HF - 3 * LANES, UNIT)
+        spill(wide, DP, up, 0.5)
         for g in range(2):
-            clear(tall, 2, g * HFP + HF, 32)
-            take(fh.at[g], hp[place], HF, D, 0, D, tall, g * HFP, 0)
-        take(fs, sp["vec"] + brow * D, 1, D, 0, D, tall, HF, 0)
-        spill(tall, FFP, dst_ref, 0.5)
-    clear(wide, 6, 240, 16)
-    for g in range(2):
-        for which, (place, bplace) in enumerate((("wq", "bq"), ("wk", None), ("wv", "bv"))):
-            lane0 = which * DP + g * LANES
-            take(fh.at[g], hp[place], D, HC, 0, HC, wide, 0, lane0)
-            if bplace:
-                take(fh.at[g], hp[bplace], 1, HC, 0, HC, wide, 240, lane0)
-    for tile in (0, 1, 4, 5):
-        patch(wide, tile, 240, lane == MASK_LANE, 1.0)
-    spill(wide, DP, qkv)
-    clear(tall, 2, 0, DP)
-    for g in range(2):
-        take(fh.at[g], hp["wo"], HC, D, 0, D, tall, g * LANES, 0)
-    take(fs, sp["vec"] + B_OUT * D, 1, D, 0, D, tall, MASK_LANE, 0)
-    spill(tall, DP, wo)
-    clear(wide, 4, 240, 16)
-    for half in range(2):
-        take(fs, sp["p1"], D, 2 * D, half * D, D, wide, 0, half * DP)
-        take(fs, sp["pb1"] + half * D, 1, D, 0, D, wide, 240, half * DP)
-    spill(wide, DP, p1)
-    clear(tall, 2, 240, 16)
-    take(fs, sp["p2"], D, D, 0, D, tall, 0, 0)
-    take(fs, sp["pb2"], 1, D, 0, D, tall, 240, 0)
-    spill(tall, DP, p2)
-    take(fs, sp["vec"], 16, D, 0, D, tall, 0, 0)
-    take(fs, sp["taps"], 16, D, 0, D, tall, TAPS, 0)
-    take(fs, sp["bg"], 1, D, 0, D, tall, BATCH_GAIN, 0)
-    take(fs, sp["bb"], 1, D, 0, D, tall, BATCH_BIAS, 0)
-    for row, value in ((FFA + 1, 1.0), (ATT + 1, 1.0), (CNV + 1, 1.0), (FFB + 1, 1.0), (BATCH_BIAS, UNIT)):
-        patch(tall, 1, row, lane == D - LANES, value)
-    spill(tall, VEC_ROWS, vec)
-    length = rel.shape[1]
-    for n in range(HEADS):
-        take(fh.at[n // 2], hp["rel"] + (n % 2) * KREL, 1, KREL, 0, KREL, tmp, 0, 0)
-        row = jnp.concatenate([tmp[t, pl.ds(0, 1), :] for t in range(3)] + [jnp.zeros((1, LANES), F32)], 1)
-        rows = jnp.broadcast_to(row, (length, 4 * LANES))
-        rows = pltpu.roll(rows, 4 * LANES - (length - 1), 1, stride=1, stride_axis=0)
-        rel[pl.ds(n * length, length), :] = rows[:, :length] * LOG2E
-
-
-def make_weights(got, head_size, shared_size, length):
-    dp = got.shape[0]
-
-    def s(*shape, dtype=BF):
-        return jax.ShapeDtypeStruct(shape, dtype)
-
-    outs = (
-        s(DP, FFP), s(FFP, DP), s(DP, FFP), s(FFP, DP), s(DP, 3 * DP), s(DP, DP), s(DP, 2 * DP), s(DP, DP),
-        s(VEC_ROWS, DP, dtype=F32), s(HEADS * length, length, dtype=F32),
-    )
-    vm = pltpu.VMEM
-    scratch = (
-        vm((2, flat_rows(head_size * dp, head_size), LANES), F32),
-        vm((flat_rows(shared_size * 2 * dp, shared_size), LANES), F32),
-        vm((8, DP, LANES), F32),
-        vm((2, FFP, LANES), F32),
-        vm((4, 8, LANES), F32),
-    )
-    return vmem_call(
-        functools.partial(weights_kernel, (dp, head_size, shared_size)), outs, (got,), scratch, "make_weights"
-    )
+            self.clear(tall, 2, g * HFP + HF, 32)
+            take(self.fh.at[g], hp[dn_place], HF, D, 0, D, tall, g * HFP, 0)
+        take(self.fs, self.sp["vec"] + row * D, 1, D, 0, D, tall, HF, 0)
+        spill(tall, FFP, dn, 0.5)
+
+    def point_two(self, p2):
+        self.clear(self.tall, 2, 240, 16)
+        take(self.fs, self.sp["p2"], D, D, 0, D, self.tall, 0, 0)
+        take(self.fs, self.sp["pb2"], 1, D, 0, D, self.tall, 240, 0)
+        spill(self.tall, DP, p2)
+
+    def others(self, qkv, wo, p1, vec, rel):
+        wide, tall, tmp, fh, fs, hp, sp = self.wide, self.tall, self.tmp, self.fh, self.fs, self.hp, self.sp
+        lane = lane_iota((1, LANES))
+        self.clear(wide, 6, 240, 16)
+        for g in range(2):
+            for which, (place, bplace) in enumerate((("wq", "bq"), ("wk", None), ("wv", "bv"))):
+                lane0 = which * DP + g * LANES
+                take(fh.at[g], hp[place], D, HC, 0, HC, wide, 0, lane0)
+                if bplace:
+                    take(fh.at[g], hp[bplace], 1, HC, 0, HC, wide, 240, lane0)
+        for tile in (0, 1, 4, 5):
+            self.patch(wide, tile, 240, lane == MASK_LANE, 1.0)
+        spill(wide, DP, qkv)
+        self.clear(tall, 2, 0, DP)
+        for g in range(2):
+            take(fh.at[g], hp["wo"], HC, D, 0, D, tall, g * LANES, 0)
+        take(fs, sp["vec"] + B_OUT * D, 1, D, 0, D, tall, MASK_LANE, 0)
+        spill(tall, DP, wo)
+        self.clear(wide, 4, 240, 16)
+        for half in range(2):
+            take(fs, sp["p1"], D, 2 * D, half * D, D, wide, 0, half * DP)
+            take(fs, sp["pb1"] + half * D, 1, D, 0, D, wide, 240, half * DP)
+        spill(wide, DP, p1)
+        take(fs, sp["vec"], 16, D, 0, D, tall, 0, 0)
+        take(fs, sp["taps"], 16, D, 0, D, tall, TAPS, 0)
+        take(fs, sp["bg"], 1, D, 0, D, tall, BATCH_GAIN, 0)
+        take(fs, sp["bb"], 1, D, 0, D, tall, BATCH_BIAS, 0)
+        for row, value in ((FFA + 1, 1.0), (ATT + 1, 1.0), (CNV + 1, 1.0), (FFB + 1, 1.0), (BATCH_BIAS, UNIT)):
+            self.patch(tall, 1, row, lane == D - LANES, value)
+        spill(tall, VEC_ROWS, vec)
+        length = rel.shape[1]
+        for n in range(HEADS):
+            take(fh.at[n // 2], hp["rel"] + (n % 2) * KREL, 1, KREL, 0, KREL, tmp, 0, 0)
+            row = jnp.concatenate([tmp[t, pl.ds(0, 1), :] for t in range(3)] + [jnp.zeros((1, LANES), F32)], 1)
+            rows = jnp.broadcast_to(row, (length, 4 * LANES))
+            rows = pltpu.roll(rows, 4 * LANES - (length - 1), 1, stride=1, stride_axis=0)
+            rel[pl.ds(n * length, length), :] = rows[:, :length] * LOG2E
 
 
 class Flat:
@@ -826,17 +812,24 @@
 
 
 def phase_a_kernel(
-    seqs, lengths, frames, up, dn, wqkv, wo, p1, vec, rel,
+    seqs, sizes, lengths, frames, head_ref, shared_ref,
     kept1_o, a1_o, h_o, sp_o, kept2_o, a2_o, qkv_o, e_o, rl_o, m_o,
-    x2_o, kept3_o, a3_o, f1_o, f2_o, gl_o, w_o, keep_o,
-    pad, stats_o, inbox, ss, rs,
+    x2_o, kept3_o, a3_o, f1_o, f2_o, gl_o, w_o, keep_o, up, dn, up2, dn2, wqkv, wo, p1, p2, vec, rel,
+    pad, stats_o, inbox, ss, rs, own_slot, got, fh, fs, wide, tall, tmp, *sems,
 ):
     step = pl.program_id(0)
     total = inbox.shape[0]
+    weights = Weights(*sizes, got, (fh, fs, wide, tall, tmp))
 
     @pl.when(step == 0)
     def _():
         greet_all(total)
+        align(head_ref, shared_ref, own_slot)
+        weights.clear_flat()
+        greeted_all(total)
+        gather(sizes[0] // 4, own_slot, got, sems, weights.merge)
+        weights.ffn(up, dn, "up1", "upb1", "dn1", DOWNB_ONE)
+        weights.others(wqkv, wo, p1, vec, rel)
 
     length = frames.shape[1]
     tokens = seqs * length
@@ -936,6 +929,8 @@
     @pl.when(step == pl.num_programs(0) - 1)
     def _():
         share_start(total, stats_o, inbox, ss, rs)
+        weights.ffn(up2, dn2, "up2", "upb2", "dn2", DOWNB_TWO)
+        weights.point_two(p2)
         share_finish(total, stats_o, inbox, ss, rs)
         batch_stats(inbox[...], keep_o)
 
@@ -1019,6 +1014,7 @@
 
     @pl.when(step == pl.num_programs(0) - 1)
     def _():
+        greeted_all(total)
         share_start(total, sums_o, inbox, ss, rs)
 
         @pl.loop(0, pl.num_programs(0))
@@ -1269,32 +1265,34 @@
     head_size, shared_size = head_params.shape[1], shared_params.shape[0]
     rows = slot_rows(head_size) + slot_rows(shared_size)
     vm = pltpu.VMEM
-    mine = vmem_call(
-        align_kernel, jax.ShapeDtypeStruct((rows, LANES), BF), (head_params, shared_params), name="align"
-    )
-    got = gather_all(mine, dp, 1)
-    up1, dn1, up2, dn2, wqkv, wo, p1, p2, vec, rel = make_weights(got, head_size, shared_size, length)
-
     dma = pltpu.SemaphoreType.DMA
     sharing = [vm((8, LANES), F32), vm((2 * dp, 8, LANES), F32), dma((2 * dp,)), dma((2 * dp,))]
     steps = seq_here // SEQS_A
     t = functools.partial(tile_out, steps)
     (
-        kept1, a1, h1, slope1, kept2, a2, qkv, e_all, rl, m, x2, kept3, a3, f1, f2, gl, w, keep
+        kept1, a1, h1, slope1, kept2, a2, qkv, e_all, rl, m, x2, kept3, a3, f1, f2, gl, w, keep,
+        up1, dn1, up2, dn2, wqkv, wo, p1, p2, vec, rel
     ) = layer_call(
-        functools.partial(phase_a_kernel, SEQS_A),
+        functools.partial(phase_a_kernel, SEQS_A, (dp, head_size, shared_size)),
         steps,
-        [("smem", None, lengths), tile_in(frames, steps)] + [whole_in(x) for x in (up1, dn1, wqkv, wo, p1, vec, rel)],
+        [("smem", None, lengths), tile_in(frames, steps), whole_in(head_params), whole_in(shared_params)],
         [
             t((tokens, DP), F32), t((tokens, DP), BF), t((tokens, FFP), BF), t((tokens, FFP), BF),
             t((tokens, DP), F32), t((tokens, DP), BF), t((tokens, 3 * DP), BF),
             t((seq_here, HEADS * length, length), BF), t((tokens, DP), F32), t((tokens, DP), BF),
             t((tokens, DP), F32), t((tokens, DP), F32), t((tokens, DP), BF), t((tokens, DP), BF),
             t((tokens, DP), BF), t((tokens, DP), BF), t((tokens, DP), F32), whole_out((8, DP)),
+            whole_out((DP, FFP), BF), whole_out((FFP, DP), BF), whole_out((DP, FFP), BF), whole_out((FFP, DP), BF),
+            whole_out((DP, 3 * DP), BF), whole_out((DP, DP), BF), whole_out((DP, 2 * DP), BF), whole_out((DP, DP), BF),
+            whole_out((VEC_ROWS, DP)), whole_out((HEADS * length, length)),
         ],
-        [vm((SEQS_A, 2, length + 16, LANES), F32)] + sharing,
+        [vm((SEQS_A, 2, length + 16, LANES), F32)]
+        + sharing
+        + [vm((rows, LANES), BF), vm((dp, 2, rows, LANES), BF)]
+        + Flat.scratch(dp, head_size, shared_size)
+        + gather_sems(dp // 4),
         "phase_a",
-        2,
+        1,
     )
     steps = seq_here // SEQS_B
     t = functools.partial(tile_out, steps)

time: 196 us -> 188 us (0.959)
  Pallas kernels: 192 us -> 187 us
  local copies, waits for them, and re-layouts: 2.42 us -> 0 us
    pallas_call x3 -> x0, Pallas kernels: 32.8 us -> none  [the longest x1 23.9 us: gather_all(): pl.pallas_call(functools.partial(gather_kernel, nz), out_shape=jax.ShapeD...]
    pallas_call x4, Pallas kernels: 160 us -> 187 us  [layer_call(): pl.pallas_call(body, grid=(steps,), out_shape=tuple((jax.ShapeDtypeStruct...]
    unnamed x4 -> x0, local copies, waits for them, and re-layouts: 2.42 us -> none
where the time goes in v4:
time: 188 us
  Pallas kernels  187 us (99%)
    pallas_call x4, Pallas kernels, layer_call(): pl.pallas_call(body, grid=(steps,), out_shape=tuple((jax.ShapeDtypeStruct...  187 us

profile of v4, /device:TPU:0, one launch (start us, length us, event | category | flops | bytes accessed | tf_op | source)
XLA Modules:
  0.0 188.0 jit_solution(10339282352877656047)
XLA Ops:
  0.6 74.0 %phase_a.1 = (f32[3072,256]{1,0:T(8,128)}, bf16[3072,256]{1,0:T(8,128)(2,1)}, bf16[3072,1024]{1,0:T(8,128)(2,1)}, bf16[3072,1024]{1,0:T(8,128)(2,1)}, f32[3072,2...) custom-call(s32[32]{0:T(128)} %lengths.3, ...), custom_call_target="tpu_custom_call" | custom-call | tf_op jit(solution)/shard_map/phase_a/pallas_call | solution.py:1219
  74.6 27.5 %phase_b.1 = (bf16[16,192,240]{2,1,0:T(8,128)(2,1)}, f32[3072,256]{1,0:T(8,128)}, f32[3072,256]{1,0:T(8,128)}, f32[256,1024]{1,0:T(8,128)}, f32[256,1024]{1,0:T(...) custom-call(f32[8,256]{1,0:T(8,128)} %get-tuple-element.47.keep, ...), custom_call_target="tpu_custom_call" | custom-call | tf_op jit(solution)/shard_map/phase_b/pallas_call | solution.py:1219
  102.2 79.9 %phase_c.1 = (f32[16,192,240]{2,1,0:T(8,128)}, f32[336,128]{1,0:T(8,128)}) custom-call(s32[32]{0:T(128)} %lengths.3, f32[8,256]{1,0:T(8,128)} %get-tuple-element.55.keep, f32[3072,256]{1,0:T(8,128)} %get-tuple-element.48.w, f32[3072,256]{1,0:T(8,128)} %get-tuple-element.56.dy, f32[3072,256]{1,0:T(8,128)} %get-tuple-element.57.dx3, ...), custom_call_target="tpu_custom_call" | custom-call | tf_op jit(solution)/shard_map/phase_c/pallas_call | solution.py:1219
  182.1 5.7 %adam.1 = (bf16[16,192,240]{2,1,0:T(8,128)(2,1)}, f32[16,192,240]{2,1,0:T(8,128)}, f32[1,36123]{1,0:T(1,128)}, f32[1,36123]{1,0:T(1,128)}, f32[1,36123]{1,0:T(1,...) custom-call(bf16[16,192,240]{2,1,0:T(8,128)(2,1)} %get-tuple-element, ...), custom_call_target="tpu_custom_call" | custom-call | tf_op jit(solution)/shard_map/adam/pallas_call | solution.py:1219

commit v5 on v4

--- a/solution.py
+++ b/solution.py
@@ -802,6 +802,20 @@
     return jnp.concatenate([x.astype(F32), jnp.zeros((rows, DP - D), F32)], 1)
 
 
+SHORT = (1, 1, 1, 1, 3, 1, 1, 4)
+LATE = (4, 1)
+LONG = (1, 1, 1)
+PAIR = (1, 1)
+
+
+def columns(ref, widths):
+    out, at = [], 0
+    for width in widths:
+        out.append(ref.at[:, pl.ds(at * DP, width * DP)])
+        at += width
+    return out
+
+
 def head_lanes():
     lane = lane_iota((1, LANES))
     return lane < HD, (lane >= HD) & (lane < 2 * HD), lane == MASK_LANE
@@ -813,13 +827,36 @@
 
 def phase_a_kernel(
     seqs, sizes, lengths, frames, head_ref, shared_ref,
-    kept1_o, a1_o, h_o, sp_o, kept2_o, a2_o, qkv_o, e_o, rl_o, m_o,
-    x2_o, kept3_o, a3_o, f1_o, f2_o, gl_o, w_o, keep_o, up, dn, up2, dn2, wqkv, wo, p1, p2, vec, rel,
-    pad, stats_o, inbox, ss, rs, own_slot, got, fh, fs, wide, tall, tmp, *sems,
+    short_far, late_far, long_far, kept1_far, xw_far, e_far, keep_o, up, dn, up2, dn2, wqkv, wo, p1, p2, vec, rel,
+    pad, stats_o, inbox, ss, rs, own_slot, got, fh, fs, wide, tall, tmp,
+    short_b, late_b, long_b, kept1_b, xw_b, e_b, out_sem, *sems,
 ):
     step = pl.program_id(0)
+    slot = lax.rem(step, 2)
+    far = (short_far, late_far, long_far, kept1_far, xw_far, e_far)
+    near = (short_b, late_b, long_b, kept1_b, xw_b, e_b)
+
+    def moves(k):
+        side = lax.rem(k, 2)
+        out = []
+        for j, (here, there) in enumerate(zip(near, far)):
+            size = here.shape[1]
+            rows = pl.ds(pl.multiple_of(k * size, size), size)
+            out.append(pltpu.make_async_copy(here.at[side], there.at[rows], out_sem.at[side, j]))
+        return out
+
+    @pl.when(step >= 2)
+    def _():
+        for move in moves(step - 2):
+            move.wait()
+
+    short_o, late_o, long_o, kept1_o, xw_o, e_o = (ref.at[slot] for ref in near)
     total = inbox.shape[0]
     weights = Weights(*sizes, got, (fh, fs, wide, tall, tmp))
+    gl_o, f1_o, f2_o, a3_o, qkv_o, m_o, a2_o, h_o = columns(short_o, SHORT)
+    sp_o, a1_o = columns(late_o, LATE)
+    kept3_o, kept2_o, rl_o = columns(long_o, LONG)
+    x2_o, w_o = columns(xw_o, PAIR)
 
     @pl.when(step == 0)
     def _():
@@ -846,7 +883,8 @@
     h_o[...] = h
     sp_o[...] = slope
     x1 = x0 + dot(h, dn[...])
-    a, kept2_o[...] = norm(x1, v(ATT), v(ATT + 1))
+    a, kept = norm(x1, v(ATT), v(ATT + 1))
+    kept2_o[...] = kept.astype(BF)
     a = a.astype(BF)
     a2_o[...] = a
     qkv = dot(a, wqkv[...])
@@ -874,11 +912,12 @@
             o = dot(e, vv)
             r = 1.0 / o[:, MASK_LANE : MASK_LANE + 1]
             shares = jnp.where(second, r[length:], r[:length])
-            rl_o[rows, pl.ds(g * LANES, LANES)] = shares
+            rl_o[rows, pl.ds(g * LANES, LANES)] = shares.astype(BF)
             m_o[rows, pl.ds(g * LANES, LANES)] = (jnp.where(second, o[length:], o[:length]) * shares).astype(BF)
     x2 = x1 + dot(m_o[...], wo[...])
     x2_o[...] = x2
-    a, kept3_o[...] = norm(x2, v(CNV), v(CNV + 1))
+    a, kept = norm(x2, v(CNV), v(CNV + 1))
+    kept3_o[...] = kept.astype(BF)
     a = a.astype(BF)
     a3_o[...] = a
     e = dot(a, p1[...])
@@ -925,6 +964,8 @@
         stats_o[pl.ds(t, 1), :] = before + delta * (count / new)
         stats_o[pl.ds(2 + t, 1), :] += square[:, cols] + delta * delta * (old * count / new)
     stats_o[pl.ds(4, 1), :] = new
+    for move in moves(step):
+        move.start()
 
     @pl.when(step == pl.num_programs(0) - 1)
     def _():
@@ -933,6 +974,8 @@
         weights.point_two(p2)
         share_finish(total, stats_o, inbox, ss, rs)
         batch_stats(inbox[...], keep_o)
+        for move in moves(step - 1) + moves(step):
+            move.wait()
 
 
 def batch_stats(shared, keep):
@@ -952,8 +995,8 @@
 
 
 def phase_b_kernel(
-    seqs, keep, w, x2, cotangent, p2, up, dn, vec,
-    out_o, dy_o, dx3_o, dup_o, ddn_o, dp2_o, vec_o, keep_o,
+    seqs, keep, xw, cotangent, p2, up, dn, vec,
+    out_o, back_o, dup_o, ddn_o, dp2_o, vec_o, keep_o,
     acc, a_all, du_all, do_all, h_all, hc_all, dc_all, sums_o, inbox, ss, rs,
 ):
     step = pl.program_id(0)
@@ -961,6 +1004,8 @@
     length = cotangent.shape[1]
     tokens = seqs * length
     at = pl.ds(pl.multiple_of(step * tokens, tokens), tokens)
+    x2, w = columns(xw, PAIR)
+    dy_o, dx3_o = columns(back_o, PAIR)
 
     @pl.when(step == 0)
     def _():
@@ -1032,18 +1077,71 @@
 
 
 def phase_c_kernel(
-    seqs, steps, sizes, lengths, keep, w, dy, dx3, gl, f1, f2, a3, kept3, qkv, e_all, rl, m, a2, kept2, h, slope, a1, kept1,
+    seqs, steps, sizes, lengths, keep, xw_far, back_far, short_far, long_far, e_far, late_far, kept1_far,
     p1, wo, wqkv, dn, up, vec, dup2, ddn2, dp2, vec2,
     dx0_o, sum_o,
     dp1_o, dwo_o, dqkv_o, dup_o, ddn_o, vec_o, rel_o, dx1_buf, mine,
-    acc, padw, padg, grads, *refs,
+    acc, padw, padg, grads, w_b, back_b, short_b, long_b, e_b, late_b, kept1_b, in_sem, *refs,
 ):
     step = pl.program_id(0)
     length = dx0_o.shape[1]
+    side = lax.rem(step, 2)
+    cut = 3 * DP
+
+    def fetch(k, names):
+        to = lax.rem(k, 2)
+        size = seqs * length
+        rows = pl.ds(pl.multiple_of(k * size, size), size)
+        make = pltpu.make_async_copy
+        every = (
+            lambda j: make(xw_far.at[rows, pl.ds(DP, DP)], w_b.at[to], in_sem.at[to, j]),
+            lambda j: make(back_far.at[rows], back_b.at[to], in_sem.at[to, j]),
+            lambda j: make(short_far.at[rows, pl.ds(0, cut)], short_b.at[to, :, pl.ds(0, cut)], in_sem.at[to, j]),
+            lambda j: make(
+                short_far.at[rows, pl.ds(cut, short_b.shape[2] - cut)],
+                short_b.at[to, :, pl.ds(cut, short_b.shape[2] - cut)],
+                in_sem.at[to, j],
+            ),
+            lambda j: make(long_far.at[rows], long_b.at[to], in_sem.at[to, j]),
+            lambda j: make(e_far.at[pl.ds(k * seqs, seqs)], e_b.at[to], in_sem.at[to, j]),
+            lambda j: make(late_far.at[rows], late_b.at[to], in_sem.at[to, j]),
+            lambda j: make(kept1_far.at[rows], kept1_b.at[to], in_sem.at[to, j]),
+        )
+        return [every[j](j) for j in names]
+
+    conv_names, rest_names, late_names = (0, 1, 2), (3, 4, 5), (6, 7)
+
+    @pl.when(step == 0)
+    def _():
+        for move in fetch(step, conv_names + rest_names):
+            move.start()
+
+    @pl.when(step < steps - 1)
+    def _():
+        for move in fetch(step + 1, conv_names + rest_names):
+            move.start()
+
+    @pl.when(step == steps - 1)
+    def _():
+        for move in fetch(step * 0, late_names):
+            move.start()
+
+    @pl.when((step >= steps) & (step < 2 * steps - 1))
+    def _():
+        for move in fetch(step + 1 - steps, late_names):
+            move.start()
+
+    w, back, short, long, e_all = (ref.at[side] for ref in (w_b, back_b, short_b, long_b, e_b))
+    late_side = lax.rem(jnp.maximum(step - steps, 0), 2)
+    late, kept1 = late_b.at[late_side], kept1_b.at[late_side]
     flat = Flat(*sizes, refs[:5])
     nz = sizes[0] // 4
     scatter = Scatter(nz, flat.hr, flat.sr, mine, refs[5:])
     one, two, rest, shared_two, shared_rest = flat.groups()
+    dy, dx3 = columns(back, PAIR)
+    gl, f1, f2, a3, qkv, m, a2, h = columns(short, SHORT)
+    kept3, kept2, rl = columns(long, LONG)
+    slope, a1 = columns(late, LATE)
 
     @pl.when(step == 0)
     def _():
@@ -1061,8 +1159,13 @@
 
     @pl.when(step < steps)
     def _():
+        def ready(names):
+            for move in fetch(step, names):
+                move.wait()
+
+        ready(conv_names)
         phase_c_first(
-            seqs, step, steps, length, lengths, keep, w, dy, dx3, gl, f1, f2, a3, kept3, qkv, e_all, rl, m, a2, kept2,
+            functools.partial(ready, rest_names), seqs, step, steps, length, lengths, keep, w, dy, dx3, gl, f1, f2, a3, kept3, qkv, e_all, rl, m, a2, kept2,
             h, p1, wo, wqkv, vec, dp1_o, dwo_o, dqkv_o, ddn_o, rel_o, dx1_buf, acc, padw, padg, grads,
         )
 
@@ -1082,6 +1185,8 @@
 
     @pl.when(step >= steps)
     def _():
+        for move in fetch(step - steps, late_names):
+            move.wait()
         at = pl.ds(pl.multiple_of((step - steps) * (seqs * length), seqs * length), seqs * length)
         dx1 = dx1_buf[at, :]
         du = dot_t(dx1.astype(BF), dn[...]).astype(BF) * slope[...]
@@ -1092,7 +1197,7 @@
         dx0_o[...] = dx0[:, :D].reshape(seqs, length, D)
 
     stages = (scatter.stage_first, scatter.stage_second, scatter.stage_third)
-    for at, heads, shared in (((1, 3, 5), one, []), ((steps + AT_A, steps + AT_B), two, shared_two)):
+    for at, heads, shared in (((1, 2, 3), one, []), ((steps + AT_A, steps + AT_B), two, shared_two)):
         for when, stage in zip(at, stages):
             @pl.when(step == when)
             def _():
@@ -1125,7 +1230,7 @@
 
 
 def phase_c_first(
-    seqs, step, steps, length, lengths, keep, w, dy, dx3, gl, f1, f2, a3, kept3, qkv, e_all, rl, m, a2, kept2,
+    ready, seqs, step, steps, length, lengths, keep, w, dy, dx3, gl, f1, f2, a3, kept3, qkv, e_all, rl, m, a2, kept2,
     h, p1, wo, wqkv, vec, dp1_o, dwo_o, dqkv_o, ddn_o, rel_o, dx1_buf, acc, padw, padg, grads,
 ):
     first_seq = lax.axis_index("head") * (seqs * steps) + step * seqs
@@ -1156,11 +1261,13 @@
                 acc[TAPS + r, :, cols] += fold_rows(tap)
             grads[rows, cols] = (total * f1[rows, cols].astype(F32)).astype(BF)
             grads[rows, pl.ds(DP + t * LANES, LANES)] = (total * f2[rows, cols].astype(F32)).astype(BF)
+    ready()
     de = grads[:, pl.ds(0, 2 * DP)]
     dp1_o[...] += t_dot(a3[...], de)
     da = dot_t(de, p1[...])
-    norm_param_grads(acc, CNV, da, kept3[...])
-    dx2 = dx3[...] + norm_grad(da, kept3[...], v(CNV))
+    kept = kept3[...].astype(F32)
+    norm_param_grads(acc, CNV, da, kept)
+    dx2 = dx3[...] + norm_grad(da, kept, v(CNV))
     db = dx2.astype(BF)
     dwo_o[...] += t_dot(m[...], db)
     dm = dot_t(db, wo[...])
@@ -1175,7 +1282,7 @@
             q = qkv[rows, cols]
             k = qkv[rows, pl.ds(DP + g * LANES, LANES)]
             vv = qkv[rows, pl.ds(2 * DP + g * LANES, LANES)]
-            dmb = (dm[b * length : (b + 1) * length, g * LANES : (g + 1) * LANES] * rl[rows, cols]).astype(BF)
+            dmb = (dm[b * length : (b + 1) * length, g * LANES : (g + 1) * LANES] * rl[rows, cols].astype(F32)).astype(BF)
             level = dot(dmb * m[rows, cols], spread)
             level = jnp.concatenate([level[:, :LANES], level[:, LANES:]], 0)
             zero = jnp.zeros_like(q)
@@ -1195,8 +1302,9 @@
     dqkv = grads[...]
     dqkv_o[...] += t_dot(a2[...], dqkv)
     da = dot_t(dqkv, wqkv[...])
-    norm_param_grads(acc, ATT, da, kept2[...])
-    dx1 = dx2 + norm_grad(da, kept2[...], v(ATT))
+    kept = kept2[...].astype(F32)
+    norm_param_grads(acc, ATT, da, kept)
+    dx1 = dx2 + norm_grad(da, kept, v(ATT))
     at = pl.ds(pl.multiple_of(step * (seqs * length), seqs * length), seqs * length)
     dx1_buf[at, :] = dx1
     ddn_o[...] += t_dot(dx1.astype(BF), h[...])
@@ -1205,6 +1313,8 @@
 def layer_call(body, steps, ins, outs, scratch, name, collective_id=None):
     def spec(item):
         kind, shape = item
+        if kind == "far":
+            return pl.BlockSpec(memory_space=pl.ANY)
         if kind == "smem":
             return pl.BlockSpec(memory_space=pltpu.SMEM)
         if kind == "tile":
@@ -1245,15 +1355,23 @@
     return (kind, (shape[0] // steps,) + shape[1:], shape, dtype)
 
 
+def far_in(array):
+    return ("far", None, array)
+
+
+def far_out(shape, dtype):
+    return ("far", None, shape, dtype)
+
+
 def whole_out(shape, dtype=F32):
     return ("whole", shape, shape, dtype)
 
 
-SEQS_A = 2
+SEQS_A = 4
 SEQS_B = 4
-SEQS_C = 2
-AT_A = 4
-AT_B = 7
+SEQS_C = 4
+AT_A = 2
+AT_B = 3
 
 
 def per_device(
@@ -1268,20 +1386,20 @@
     dma = pltpu.SemaphoreType.DMA
     sharing = [vm((8, LANES), F32), vm((2 * dp, 8, LANES), F32), dma((2 * dp,)), dma((2 * dp,))]
     steps = seq_here // SEQS_A
+    block = SEQS_A * length
     t = functools.partial(tile_out, steps)
     (
-        kept1, a1, h1, slope1, kept2, a2, qkv, e_all, rl, m, x2, kept3, a3, f1, f2, gl, w, keep,
+        short, late, long, kept1, xw, e_all, keep,
         up1, dn1, up2, dn2, wqkv, wo, p1, p2, vec, rel
     ) = layer_call(
         functools.partial(phase_a_kernel, SEQS_A, (dp, head_size, shared_size)),
         steps,
         [("smem", None, lengths), tile_in(frames, steps), whole_in(head_params), whole_in(shared_params)],
         [
-            t((tokens, DP), F32), t((tokens, DP), BF), t((tokens, FFP), BF), t((tokens, FFP), BF),
-            t((tokens, DP), F32), t((tokens, DP), BF), t((tokens, 3 * DP), BF),
-            t((seq_here, HEADS * length, length), BF), t((tokens, DP), F32), t((tokens, DP), BF),
-            t((tokens, DP), F32), t((tokens, DP), F32), t((tokens, DP), BF), t((tokens, DP), BF),
-            t((tokens, DP), BF), t((tokens, DP), BF), t((tokens, DP), F32), whole_out((8, DP)),
+            far_out((tokens, sum(SHORT) * DP), BF), far_out((tokens, sum(LATE) * DP), BF),
+            far_out((tokens, sum(LONG) * DP), BF), far_out((tokens, DP), F32), far_out((tokens, sum(PAIR) * DP), F32),
+            far_out((seq_here, HEADS * length, length), BF),
+            whole_out((8, DP)),
             whole_out((DP, FFP), BF), whole_out((FFP, DP), BF), whole_out((DP, FFP), BF), whole_out((FFP, DP), BF),
             whole_out((DP, 3 * DP), BF), whole_out((DP, DP), BF), whole_out((DP, 2 * DP), BF), whole_out((DP, DP), BF),
             whole_out((VEC_ROWS, DP)), whole_out((HEADS * length, length)),
@@ -1290,19 +1408,24 @@
         + sharing
         + [vm((rows, LANES), BF), vm((dp, 2, rows, LANES), BF)]
         + Flat.scratch(dp, head_size, shared_size)
+        + [
+            vm((2, block, sum(SHORT) * DP), BF), vm((2, block, sum(LATE) * DP), BF), vm((2, block, sum(LONG) * DP), BF),
+            vm((2, block, DP), F32), vm((2, block, sum(PAIR) * DP), F32), vm((2, SEQS_A, HEADS * length, length), BF),
+            dma((2, 6)),
+        ]
         + gather_sems(dp // 4),
         "phase_a",
         1,
     )
     steps = seq_here // SEQS_B
     t = functools.partial(tile_out, steps)
-    early, dy, dx3, dup2, ddn2, dp2, vec_b, keep = layer_call(
+    early, back, dup2, ddn2, dp2, vec_b, keep = layer_call(
         functools.partial(phase_b_kernel, SEQS_B),
         steps,
-        [whole_in(keep), tile_in(w, steps), tile_in(x2, steps), tile_in(cotangent, steps)]
+        [whole_in(keep), tile_in(xw, steps), tile_in(cotangent, steps)]
         + [whole_in(x) for x in (p2, up2, dn2, vec)],
         [
-            t((seq_here, length, D), BF), t((tokens, DP), F32), t((tokens, DP), F32),
+            t((seq_here, length, D), BF), t((tokens, sum(PAIR) * DP), F32),
             whole_out((DP, FFP)), whole_out((DP, FFP)), whole_out((DP, DP)), whole_out((VEC_ROWS, DP)),
             whole_out((8, DP)),
         ],
@@ -1321,8 +1444,7 @@
         functools.partial(phase_c_kernel, SEQS_C, steps, (dp, head_size, shared_size)),
         2 * steps,
         [("smem", None, lengths), whole_in(keep)]
-        + [tile_in(x, steps, "early") for x in (w, dy, dx3, gl, f1, f2, a3, kept3, qkv, e_all, rl, m, a2, kept2, h1)]
-        + [tile_in(x, steps, "late") for x in (slope1, a1, kept1)]
+        + [far_in(x) for x in (xw, back, short, long, e_all, late, kept1)]
         + [whole_in(x) for x in (p1, wo, wqkv, dn1, up1, vec, dup2, ddn2, dp2, vec_b)],
         [tile_out(steps, (seq_here, length, D), F32, "late"), whole_out((rows, LANES))],
         [
@@ -1332,6 +1454,9 @@
             vm((SEQS_C, 2, length + 16, LANES), F32),
             vm((SEQS_C, 2, length + 16, LANES), F32),
             vm((block, 3 * DP), BF),
+            vm((2, block, DP), F32), vm((2, block, sum(PAIR) * DP), F32), vm((2, block, sum(SHORT) * DP), BF),
+            vm((2, block, sum(LONG) * DP), BF), vm((2, SEQS_C, HEADS * length, length), BF),
+            vm((2, block, sum(LATE) * DP), BF), vm((2, block, DP), F32), dma((2, 8)),
         ]
         + Flat.scratch(dp, head_size, shared_size)
         + Scatter.scratch(dp, *slot),

time: 188 us -> 173 us (0.920)
  Pallas kernels: 187 us -> 172 us
    pallas_call x4, Pallas kernels: 187 us -> 172 us  [layer_call(): pl.pallas_call(body, grid=(steps,), out_shape=tuple((jax.ShapeDtypeStruct...]
where the time goes in v5:
time: 173 us
  Pallas kernels  172 us (99%)
    pallas_call x4, Pallas kernels, layer_call(): pl.pallas_call(body, grid=(steps,), out_shape=tuple((jax.ShapeDtypeStruct...  172 us

profile of v5, /device:TPU:0, one launch (start us, length us, event | category | flops | bytes accessed | tf_op | source)
XLA Modules:
  0.0 173.0 jit_solution(13136259223091956116)
XLA Ops:
  0.6 65.4 %phase_a.1 = (bf16[3072,3328]{1,0:T(8,128)(2,1)}, bf16[3072,1280]{1,0:T(8,128)(2,1)}, bf16[3072,768]{1,0:T(8,128)(2,1)}, f32[3072,256]{1,0:T(8,128)}, f32[3072,5...) custom-call(s32[32]{0:T(128)} %lengths.3, ...), custom_call_target="tpu_custom_call" | custom-call | tf_op jit(solution)/shard_map/phase_a/pallas_call | solution.py:1329
  66.1 27.2 %phase_b.1 = (bf16[16,192,240]{2,1,0:T(8,128)(2,1)}, f32[3072,512]{1,0:T(8,128)}, f32[256,1024]{1,0:T(8,128)}, f32[256,1024]{1,0:T(8,128)}, f32[256,256]{1,0:T(8...) custom-call(f32[8,256]{1,0:T(8,128)} %get-tuple-element.35.keep, f32[3072,512]{1,0:T(8,128)} %get-tuple-element.36.xw.xw_far, ...), custom_call_target="tpu_custom_call" | custom-call | tf_op jit(solution)/shard_map/phase_b/pallas_call | solution.py:1329
  93.3 73.8 %phase_c.1 = (f32[16,192,240]{2,1,0:T(8,128)}, f32[336,128]{1,0:T(8,128)}) custom-call(s32[32]{0:T(128)} %lengths.3, f32[8,256]{1,0:T(8,128)} %get-tuple-element.42.keep, f32[3072,512]{1,0:T(8,128)} %get-tuple-element.36.xw.xw_far, f32[3072,512]{1,0:T(8,128)} %get-tuple-element.43.back_far, bf16[3072,3328]{1,0:T(8,128)(2,1)} %get-tuple-element.44.short_far, ...), custom_call_target="tpu_custom_call" | custom-call | tf_op jit(solution)/shard_map/phase_c/pallas_call | solution.py:1329
  167.1 5.7 %adam.1 = (bf16[16,192,240]{2,1,0:T(8,128)(2,1)}, f32[16,192,240]{2,1,0:T(8,128)}, f32[1,36123]{1,0:T(1,128)}, f32[1,36123]{1,0:T(1,128)}, f32[1,36123]{1,0:T(1,...) custom-call(bf16[16,192,240]{2,1,0:T(8,128)(2,1)} %get-tuple-element, ...), custom_call_target="tpu_custom_call" | custom-call | tf_op jit(solution)/shard_map/adam/pallas_call | solution.py:1329

commit v6 on v5

--- a/solution.py
+++ b/solution.py
@@ -1197,7 +1197,7 @@
         dx0_o[...] = dx0[:, :D].reshape(seqs, length, D)
 
     stages = (scatter.stage_first, scatter.stage_second, scatter.stage_third)
-    for at, heads, shared in (((1, 2, 3), one, []), ((steps + AT_A, steps + AT_B), two, shared_two)):
+    for at, heads, shared in (((1, 2, 3), one, []), (tuple(steps + k for k in TWO_AT), two, shared_two)):
         for when, stage in zip(at, stages):
             @pl.when(step == when)
             def _():
@@ -1217,14 +1217,12 @@
         for z in shared_rest:
             flat.slots(scatter.g, z, 1)
             scatter.stage_core(z, 1)
-        for z in two:
-            scatter.stage_third(z, 0)
-        for z in shared_two:
-            scatter.stage_third(z, 1)
-        for stage in stages:
-            for z in rest:
+        waiting = [(stage, two, shared_two) for stage in stages[len(TWO_AT) :]]
+        last = [(stage, rest, shared_rest) for stage in stages]
+        for stage, heads, shared in [x for pair in zip(waiting, last) for x in pair] + last[len(waiting) :]:
+            for z in heads:
                 stage(z, 0)
-            for z in shared_rest:
+            for z in shared:
                 stage(z, 1)
         scatter.finish(sum_o)
 
@@ -1370,8 +1368,7 @@
 SEQS_A = 4
 SEQS_B = 4
 SEQS_C = 4
-AT_A = 2
-AT_B = 3
+TWO_AT = (1,)
 
 
 def per_device(
@@ -1464,7 +1461,7 @@
         4,
     )
     h_shape, s_shape = head_params.shape, shared_params.shape
-    steps = 4
+    steps = 2
     return layer_call(
         adam_kernel,
         steps,

time: 173 us -> 168 us (0.971)
  Pallas kernels: 172 us -> 167 us
    pallas_call x4, Pallas kernels: 172 us -> 167 us  [layer_call(): pl.pallas_call(body, grid=(steps,), out_shape=tuple((jax.ShapeDtypeStruct...]
where the time goes in v6:
time: 168 us
  Pallas kernels  167 us (99%)
    pallas_call x4, Pallas kernels, layer_call(): pl.pallas_call(body, grid=(steps,), out_shape=tuple((jax.ShapeDtypeStruct...  167 us

profile of v6, /device:TPU:0, one launch (start us, length us, event | category | flops | bytes accessed | tf_op | source)
XLA Modules:
  0.0 167.8 jit_solution(12399194481230165312)
XLA Ops:
  0.6 65.4 %phase_a.1 = (bf16[3072,3328]{1,0:T(8,128)(2,1)}, bf16[3072,1280]{1,0:T(8,128)(2,1)}, bf16[3072,768]{1,0:T(8,128)(2,1)}, f32[3072,256]{1,0:T(8,128)}, f32[3072,5...) custom-call(s32[32]{0:T(128)} %lengths.3, ...), custom_call_target="tpu_custom_call" | custom-call | tf_op jit(solution)/shard_map/phase_a/pallas_call | solution.py:1327
  66.1 27.2 %phase_b.1 = (bf16[16,192,240]{2,1,0:T(8,128)(2,1)}, f32[3072,512]{1,0:T(8,128)}, f32[256,1024]{1,0:T(8,128)}, f32[256,1024]{1,0:T(8,128)}, f32[256,256]{1,0:T(8...) custom-call(f32[8,256]{1,0:T(8,128)} %get-tuple-element.35.keep, f32[3072,512]{1,0:T(8,128)} %get-tuple-element.36.xw.xw_far, ...), custom_call_target="tpu_custom_call" | custom-call | tf_op jit(solution)/shard_map/phase_b/pallas_call | solution.py:1327
  93.3 69.6 %phase_c.1 = (f32[16,192,240]{2,1,0:T(8,128)}, f32[336,128]{1,0:T(8,128)}) custom-call(s32[32]{0:T(128)} %lengths.3, f32[8,256]{1,0:T(8,128)} %get-tuple-element.42.keep, f32[3072,512]{1,0:T(8,128)} %get-tuple-element.36.xw.xw_far, f32[3072,512]{1,0:T(8,128)} %get-tuple-element.43.back_far, bf16[3072,3328]{1,0:T(8,128)(2,1)} %get-tuple-element.44.short_far, ...), custom_call_target="tpu_custom_call" | custom-call | tf_op jit(solution)/shard_map/phase_c/pallas_call | solution.py:1327
  162.9 4.7 %adam.1 = (bf16[16,192,240]{2,1,0:T(8,128)(2,1)}, f32[16,192,240]{2,1,0:T(8,128)}, f32[1,36123]{1,0:T(1,128)}, f32[1,36123]{1,0:T(1,128)}, f32[1,36123]{1,0:T(1,...) custom-call(bf16[16,192,240]{2,1,0:T(8,128)(2,1)} %get-tuple-element, ...), custom_call_target="tpu_custom_call" | custom-call | tf_op jit(solution)/shard_map/adam/pallas_call | solution.py:1327

commit v7 on v6

--- a/solution.py
+++ b/solution.py
@@ -969,17 +969,19 @@
 
     @pl.when(step == pl.num_programs(0) - 1)
     def _():
-        share_start(total, stats_o, inbox, ss, rs)
+        unused = lane_iota((1, LANES)) == LANES - 1
+        stats_o[pl.ds(1, 1), :] = jnp.where(unused, stats_o[pl.ds(4, 1), :], stats_o[pl.ds(1, 1), :])
+        share_start(total, stats_o.at[pl.ds(0, 4)], inbox, ss, rs)
         weights.ffn(up2, dn2, "up2", "upb2", "dn2", DOWNB_TWO)
         weights.point_two(p2)
-        share_finish(total, stats_o, inbox, ss, rs)
+        share_finish(total, stats_o.at[pl.ds(0, 4)], inbox, ss, rs)
         batch_stats(inbox[...], keep_o)
         for move in moves(step - 1) + moves(step):
             move.wait()
 
 
 def batch_stats(shared, keep):
-    counts = shared[:, 4:5, :]
+    counts = jnp.broadcast_to(shared[:, 1:2, LANES - 1 :], (shared.shape[0], 1, LANES))
     total = jnp.sum(counts, 0)
     means, spreads = [], []
     for t in range(2):
@@ -996,8 +998,8 @@
 
 def phase_b_kernel(
     seqs, keep, xw, cotangent, p2, up, dn, vec,
-    out_o, back_o, dup_o, ddn_o, dp2_o, vec_o, keep_o,
-    acc, a_all, du_all, do_all, h_all, hc_all, dc_all, sums_o, inbox, ss, rs,
+    out_o, back_o, dup_far, ddn_far, dp2_far, vec_o, keep_o,
+    dup_o, ddn_o, dp2_o, out_sem, acc, a_all, du_all, do_all, h_all, hc_all, dc_all, sums_o, inbox, ss, rs,
 ):
     step = pl.program_id(0)
     total = inbox.shape[0]
@@ -1060,7 +1062,7 @@
     @pl.when(step == pl.num_programs(0) - 1)
     def _():
         greeted_all(total)
-        share_start(total, sums_o, inbox, ss, rs)
+        share_start(total, sums_o.at[pl.ds(0, 4)], inbox, ss, rs)
 
         @pl.loop(0, pl.num_programs(0))
         def _(k):
@@ -1069,11 +1071,19 @@
             dup_o[...] += t_dot(a_all[at, :], du_all[at, :])
             dp2_o[...] += t_dot(hc_all[at, :], dc_all[at, :])
 
-        share_finish(total, sums_o, inbox, ss, rs)
+        moves = [
+            pltpu.make_async_copy(here, there, out_sem.at[j])
+            for j, (here, there) in enumerate(((dup_o, dup_far), (ddn_o, ddn_far), (dp2_o, dp2_far)))
+        ]
+        for move in moves:
+            move.start()
+        share_finish(total, sums_o.at[pl.ds(0, 4)], inbox, ss, rs)
         sums = jnp.sum(inbox[...], 0)
         keep_o[...] = keep[...]
         keep_o[pl.ds(3, 1), :] = jnp.concatenate([sums[0:1], sums[1:2]], 1)
         keep_o[pl.ds(4, 1), :] = jnp.concatenate([sums[2:3], sums[3:4]], 1)
+        for move in moves:
+            move.wait()
 
 
 def phase_c_kernel(
@@ -1183,17 +1193,29 @@
             flat.slots(scatter.g, z, 1)
             scatter.stage_core(z, 1)
 
+    last_rows = pl.ds(pl.multiple_of(jnp.maximum(step - steps, 0) * (seqs * length), seqs * length), seqs * length)
+
     @pl.when(step >= steps)
     def _():
         for move in fetch(step - steps, late_names):
             move.wait()
-        at = pl.ds(pl.multiple_of((step - steps) * (seqs * length), seqs * length), seqs * length)
-        dx1 = dx1_buf[at, :]
+        dx1 = dx1_buf[last_rows, :]
         du = dot_t(dx1.astype(BF), dn[...]).astype(BF) * slope[...]
+        slope[...] = du
         dup_o[...] += t_dot(a1[...], du)
-        da = dot_t(du, up[...])
+
+    @pl.when(step == 2 * steps - 1)
+    def _():
+        flat.up(dup_o, "up1", "upb1")
+        for z in rest:
+            flat.slots(scatter.g, z, 0)
+            scatter.stage_core(z, 0)
+
+    @pl.when(step >= steps)
+    def _():
+        da = dot_t(slope[...], up[...])
         norm_param_grads(acc, FFA, da, kept1[...])
-        dx0 = dx1 + norm_grad(da, kept1[...], vec[pl.ds(FFA, 1), :])
+        dx0 = dx1_buf[last_rows, :] + norm_grad(da, kept1[...], vec[pl.ds(FFA, 1), :])
         dx0_o[...] = dx0[:, :D].reshape(seqs, length, D)
 
     stages = (scatter.stage_first, scatter.stage_second, scatter.stage_third)
@@ -1208,10 +1230,6 @@
 
     @pl.when(step == 2 * steps - 1)
     def _():
-        flat.up(dup_o, "up1", "upb1")
-        for z in rest:
-            flat.slots(scatter.g, z, 0)
-            scatter.stage_core(z, 0)
         settle(acc, vec_o)
         flat.first_norm(vec_o)
         for z in shared_rest:
@@ -1381,7 +1399,7 @@
     rows = slot_rows(head_size) + slot_rows(shared_size)
     vm = pltpu.VMEM
     dma = pltpu.SemaphoreType.DMA
-    sharing = [vm((8, LANES), F32), vm((2 * dp, 8, LANES), F32), dma((2 * dp,)), dma((2 * dp,))]
+    sharing = [vm((8, LANES), F32), vm((2 * dp, 4, LANES), F32), dma((2 * dp,)), dma((2 * dp,))]
     steps = seq_here // SEQS_A
     block = SEQS_A * length
     t = functools.partial(tile_out, steps)
@@ -1423,10 +1441,11 @@
         + [whole_in(x) for x in (p2, up2, dn2, vec)],
         [
             t((seq_here, length, D), BF), t((tokens, sum(PAIR) * DP), F32),
-            whole_out((DP, FFP)), whole_out((DP, FFP)), whole_out((DP, DP)), whole_out((VEC_ROWS, DP)),
+            far_out((DP, FFP), F32), far_out((DP, FFP), F32), far_out((DP, DP), F32), whole_out((VEC_ROWS, DP)),
             whole_out((8, DP)),
         ],
         [
+            vm((DP, FFP), F32), vm((DP, FFP), F32), vm((DP, DP), F32), dma((3,)),
             vm((VEC_ROWS, 8, DP), F32), vm((tokens, DP), BF), vm((tokens, FFP), BF), vm((tokens, DP), BF),
             vm((tokens, FFP), BF), vm((tokens, DP), BF), vm((tokens, DP), BF),
         ]

time: 168 us -> 167 us (level)
  no operation moved by 1% of the time
where the time goes in v7:
time: 167 us
  Pallas kernels  166 us (99%)
    pallas_call x4, Pallas kernels, layer_call(): pl.pallas_call(body, grid=(steps,), out_shape=tuple((jax.ShapeDtypeStruct...  166 us

profile of v7, /device:TPU:0, one launch (start us, length us, event | category | flops | bytes accessed | tf_op | source)
XLA Modules:
  0.0 167.0 jit_solution(4709712737387940099)
XLA Ops:
  0.6 65.4 %phase_a.1 = (bf16[3072,3328]{1,0:T(8,128)(2,1)}, bf16[3072,1280]{1,0:T(8,128)(2,1)}, bf16[3072,768]{1,0:T(8,128)(2,1)}, f32[3072,256]{1,0:T(8,128)}, f32[3072,5...) custom-call(s32[32]{0:T(128)} %lengths.3, ...), custom_call_target="tpu_custom_call" | custom-call | tf_op jit(solution)/shard_map/phase_a/pallas_call | solution.py:1345
  66.1 27.5 %phase_b.1 = (bf16[16,192,240]{2,1,0:T(8,128)(2,1)}, f32[3072,512]{1,0:T(8,128)}, f32[256,1024]{1,0:T(8,128)}, f32[256,1024]{1,0:T(8,128)}, f32[256,256]{1,0:T(8...) custom-call(f32[8,256]{1,0:T(8,128)} %get-tuple-element.35.keep, f32[3072,512]{1,0:T(8,128)} %get-tuple-element.36.xw.xw_far, ...), custom_call_target="tpu_custom_call" | custom-call | tf_op jit(solution)/shard_map/phase_b/pallas_call | solution.py:1345
  93.5 68.6 %phase_c.1 = (f32[16,192,240]{2,1,0:T(8,128)}, f32[336,128]{1,0:T(8,128)}) custom-call(s32[32]{0:T(128)} %lengths.3, f32[8,256]{1,0:T(8,128)} %get-tuple-element.42.keep, f32[3072,512]{1,0:T(8,128)} %get-tuple-element.36.xw.xw_far, f32[3072,512]{1,0:T(8,128)} %get-tuple-element.43.back_far, bf16[3072,3328]{1,0:T(8,128)(2,1)} %get-tuple-element.44.short_far, ...), custom_call_target="tpu_custom_call" | custom-call | tf_op jit(solution)/shard_map/phase_c/pallas_call | solution.py:1345
  162.1 4.7 %adam.1 = (bf16[16,192,240]{2,1,0:T(8,128)(2,1)}, f32[16,192,240]{2,1,0:T(8,128)}, f32[1,36123]{1,0:T(1,128)}, f32[1,36123]{1,0:T(1,128)}, f32[1,36123]{1,0:T(1,...) custom-call(bf16[16,192,240]{2,1,0:T(8,128)(2,1)} %get-tuple-element, ...), custom_call_target="tpu_custom_call" | custom-call | tf_op jit(solution)/shard_map/adam/pallas_call | solution.py:1345

commit v8 on v7

--- a/solution.py
+++ b/solution.py
@@ -1386,7 +1386,7 @@
 SEQS_A = 4
 SEQS_B = 4
 SEQS_C = 4
-TWO_AT = (1,)
+TWO_AT = (0,)
 
 
 def per_device(

time: 167 us -> 167 us (level)
  no operation moved by 1% of the time
where the time goes in v8:
time: 167 us
  Pallas kernels  166 us (99%)
    pallas_call x4, Pallas kernels, layer_call(): pl.pallas_call(body, grid=(steps,), out_shape=tuple((jax.ShapeDtypeStruct...  166 us

profile of v8, /device:TPU:0, one launch (start us, length us, event | category | flops | bytes accessed | tf_op | source)
XLA Modules:
  0.0 166.5 jit_solution(17814977045248300477)
XLA Ops:
  0.6 65.4 %phase_a.1 = (bf16[3072,3328]{1,0:T(8,128)(2,1)}, bf16[3072,1280]{1,0:T(8,128)(2,1)}, bf16[3072,768]{1,0:T(8,128)(2,1)}, f32[3072,256]{1,0:T(8,128)}, f32[3072,5...) custom-call(s32[32]{0:T(128)} %lengths.3, ...), custom_call_target="tpu_custom_call" | custom-call | tf_op jit(solution)/shard_map/phase_a/pallas_call | solution.py:1345
  66.1 27.5 %phase_b.1 = (bf16[16,192,240]{2,1,0:T(8,128)(2,1)}, f32[3072,512]{1,0:T(8,128)}, f32[256,1024]{1,0:T(8,128)}, f32[256,1024]{1,0:T(8,128)}, f32[256,256]{1,0:T(8...) custom-call(f32[8,256]{1,0:T(8,128)} %get-tuple-element.35.keep, f32[3072,512]{1,0:T(8,128)} %get-tuple-element.36.xw.xw_far, ...), custom_call_target="tpu_custom_call" | custom-call | tf_op jit(solution)/shard_map/phase_b/pallas_call | solution.py:1345
  93.5 68.1 %phase_c.1 = (f32[16,192,240]{2,1,0:T(8,128)}, f32[336,128]{1,0:T(8,128)}) custom-call(s32[32]{0:T(128)} %lengths.3, f32[8,256]{1,0:T(8,128)} %get-tuple-element.42.keep, f32[3072,512]{1,0:T(8,128)} %get-tuple-element.36.xw.xw_far, f32[3072,512]{1,0:T(8,128)} %get-tuple-element.43.back_far, bf16[3072,3328]{1,0:T(8,128)(2,1)} %get-tuple-element.44.short_far, ...), custom_call_target="tpu_custom_call" | custom-call | tf_op jit(solution)/shard_map/phase_c/pallas_call | solution.py:1345
  161.6 4.7 %adam.1 = (bf16[16,192,240]{2,1,0:T(8,128)(2,1)}, f32[16,192,240]{2,1,0:T(8,128)}, f32[1,36123]{1,0:T(1,128)}, f32[1,36123]{1,0:T(1,128)}, f32[1,36123]{1,0:T(1,...) custom-call(bf16[16,192,240]{2,1,0:T(8,128)(2,1)} %get-tuple-element, ...), custom_call_target="tpu_custom_call" | custom-call | tf_op jit(solution)/shard_map/adam/pallas_call | solution.py:1345
